TPU v7x, 32 devices: a whole 2x2x4 slice. The times are simulated.
32 devices in a mesh: gx: 8 (over z, x), gy: 2 (over y), gz: 2 (over core).
Axes of the slice: x: 2, y: 2, z: 4, core: 2. Of those that a mesh axis runs over, the one named last changes fastest.
Arguments:
- forward: float32 [19, 128, 32, 256], P(None, 'gx', 'gy', 'gz'), may hold values from 0.01 to 0.15
- adjoint: float32 [19, 128, 32, 256], P(None, 'gx', 'gy', 'gz'), may hold values from -1.2 to 1.2
- design: float32 [128, 32, 256], P('gx', 'gy', 'gz'), may hold values from 0 to 1
- mask: int32 [128, 32, 256], P('gx', 'gy', 'gz'), may hold values from 0 to 3
Outputs:
- adjoint_next: float32 [19, 128, 32, 256], P(None, 'gx', 'gy', 'gz')
- sensitivity: float32 [128, 32, 256], P('gx', 'gy', 'gz')
All inputs are finite; a program needn't handle non-finite values.
Results may differ from a plain program's by a relative error of at most 0.0003.
Values sent between devices are 32-bit elements; how exact they have to be, the bound alone decides.
No kernel may reach another device: no remote copies, remote signals or barrier semaphores. Data moves between devices by JAX's collectives and lax.ppermute only.
A program may use at most 64 MiB of HBM per device.

v0:
```python
import math

import jax
import jax.numpy as jnp
from jax import lax
from jax.sharding import PartitionSpec as P

Q = 19
RADIUS = 8


velocity = [
    (0, 0, 0),
    (1, 0, 0),
    (-1, 0, 0),
    (0, 1, 0),
    (0, -1, 0),
    (0, 0, 1),
    (0, 0, -1),
    (1, 1, 0),
    (-1, -1, 0),
    (1, -1, 0),
    (-1, 1, 0),
    (1, 0, 1),
    (-1, 0, -1),
    (1, 0, -1),
    (-1, 0, 1),
    (0, 1, 1),
    (0, -1, -1),
    (0, 1, -1),
    (0, -1, 1),
]
lattice_weight = [1.0 / 3.0] + [1.0 / 18.0] * 6 + [1.0 / 36.0] * 12
opposite = [0, 2, 1, 4, 3, 6, 5, 8, 7, 10, 9, 12, 11, 14, 13, 16, 15, 18, 17]
relax_rate = 1.25
sharpness = 64.0
threshold = 0.5
damping_max = 10.0
ramp_shape = 0.1


def extended(cells, sides, width):
    for axis, dim in sides:
        count = lax.axis_size(axis)
        ends = count - 1
        head = lax.slice_in_dim(cells, 0, width, axis=dim)
        tail = lax.slice_in_dim(cells, cells.shape[dim] - width, cells.shape[dim], axis=dim)
        cells = jnp.concatenate(
            [
                lax.ppermute(tail, axis, [(i, (i + 1) % count) for i in range(ends)]),
                cells,
                lax.ppermute(head, axis, [((i + 1) % count, i) for i in range(ends)]),
            ],
            axis=dim,
        )
    return cells


def tap_weights():
    spread_width = RADIUS / 2.0
    unscaled = [
        math.exp(-((k - RADIUS) ** 2) / (2.0 * spread_width * spread_width))
        for k in range(2 * RADIUS + 1)
    ]
    summed = sum(unscaled)
    return [v / summed for v in unscaled]


def filter_along(padded, along, length_out):
    weights = tap_weights()
    result = weights[0] * lax.slice_in_dim(padded, 0, length_out, axis=along)
    for k in range(1, 2 * RADIUS + 1):
        result = result + weights[k] * lax.slice_in_dim(padded, k, k + length_out, axis=along)
    return result


def smooth(field):
    extent = field.shape
    padded = extended(field, (("gx", 0), ("gy", 1), ("gz", 2)), RADIUS)
    padded = filter_along(padded, 0, extent[0])
    padded = filter_along(padded, 1, extent[1])
    field = filter_along(padded, 2, extent[2])
    return field


def project(filtered):
    base = math.tanh(sharpness * threshold)
    denominator = base + math.tanh(sharpness * (1.0 - threshold))
    inner = jnp.tanh(sharpness * (filtered - threshold))
    physical = (base + inner) / denominator
    steep = sharpness * (1.0 - inner * inner) / denominator
    return (physical, steep)


def ramp(physical):
    damping = damping_max * ramp_shape * (1.0 - physical) / (ramp_shape + physical)
    slope = (
        -damping_max
        * ramp_shape
        * (1.0 + ramp_shape)
        / ((ramp_shape + physical) * (ramp_shape + physical))
    )
    return (damping, slope)


def weighted_sum(members, factors):
    result = None
    for member, factor in zip(members, factors):
        if factor == 0:
            continue
        addend = factor * member
        result = addend if result is None else result + addend
    return result


def collide(pulled, forward, mask, damping, slope):
    forward_list = [forward[q] for q in range(Q)]
    density = weighted_sum(forward_list, [1.0] * Q)
    vel = [weighted_sum(forward_list, [float(d[a]) for d in velocity]) / density for a in range(3)]
    speed_sq = vel[0] * vel[0] + vel[1] * vel[1] + vel[2] * vel[2]
    zeroth = weighted_sum(pulled, lattice_weight)
    first = [
        weighted_sum(pulled, [w * d[a] for w, d in zip(lattice_weight, velocity)]) for a in range(3)
    ]
    second = [
        [
            weighted_sum(pulled, [w * d[a] * d[b] for w, d in zip(lattice_weight, velocity)])
            for b in range(3)
        ]
        for a in range(3)
    ]
    quadric = None
    for a in range(3):
        for b in range(3):
            addend = vel[a] * vel[b] * second[a][b]
            quadric = addend if quadric is None else quadric + addend
    eq_scalar = zeroth * (1.0 + 1.5 * speed_sq) - 4.5 * quadric
    eq_vector = [
        3.0 * first[a]
        + 9.0 * (second[a][0] * vel[0] + second[a][1] * vel[1] + second[a][2] * vel[2])
        - 3.0 * zeroth * vel[a]
        for a in range(3)
    ]
    moment = [weighted_sum(pulled, [float(d[a]) for d in velocity]) for a in range(3)]
    source = slope * (speed_sq - (vel[0] * moment[0] + vel[1] * moment[1] + vel[2] * moment[2]))
    outputs = []
    for q in range(Q):
        step_dir = velocity[q]
        along_eq = eq_scalar
        along_vel = 0.0
        for a in range(3):
            if step_dir[a] != 0:
                along_eq = along_eq + step_dir[a] * eq_vector[a]
                along_vel = along_vel + step_dir[a] * vel[a]
        own = pulled[q]
        fluid = (
            (1.0 - relax_rate) * own
            + relax_rate * along_eq
            + 2.0 * damping * (along_vel - speed_sq) / density
        )
        solid = pulled[opposite[q]]
        value = jnp.where(
            mask == 0, fluid, jnp.where(mask == 1, solid, jnp.where(mask == 2, along_eq, eq_scalar))
        )
        outputs.append(value)
    return (jnp.stack(outputs), source)


def local(forward, adjoint, design, mask):
    filtered = smooth(design)
    physical, steep = project(filtered)
    damping, slope = ramp(physical)
    extent = adjoint.shape[1:]
    padded = extended(adjoint, (("gx", 1), ("gy", 2), ("gz", 3)), 1)
    pulled = []
    for q in range(Q):
        step_dir = velocity[q]
        begin = (1 + step_dir[0], 1 + step_dir[1], 1 + step_dir[2])
        pulled.append(
            lax.slice(
                padded[q], begin, (begin[0] + extent[0], begin[1] + extent[1], begin[2] + extent[2])
            )
        )
    adjoint_next, source = collide(pulled, forward, mask, damping, slope)
    sensitivity = smooth(steep * source)
    return (adjoint_next, sensitivity)


def solution(mesh):
    return jax.shard_map(
        local,
        mesh=mesh,
        in_specs=(
            P(None, "gx", "gy", "gz"),
            P(None, "gx", "gy", "gz"),
            P("gx", "gy", "gz"),
            P("gx", "gy", "gz"),
        ),
        out_specs=(P(None, "gx", "gy", "gz"), P("gx", "gy", "gz")),
        check_vma=False,
    )
```

profile of v0, /device:TPU:0, one launch (start us, length us, event | category | flops | bytes accessed | tf_op | source)
XLA Modules:
  0.0 110.8 jit_solution(1459058806867265748)
XLA Ops:
  1.5 4.8 %collective-permute-start.6 = (f32[8,16,128]{2,1,0:T(8,128)S(1)}, f32[8,16,128]{2,1,0:T(8,128)S(1)}, u32[]{:S(2)}, u32[]{:S(2)}) collective-permute-start(f32[8,16,128]{2,1,0:T(8,128)S(1)} %get-tuple-element.57), channel_id=1, source_target_pairs={{0,4},{4,8},{8,12},{12,16},{16,20},{20,24},{24,28},{1,5},{5,9},{9,... | collective-permute-start | bytes 196616 | tf_op jit(solution)/shard_map/ppermute | solution.py:50
  7.4 3.5 %collective-permute-start = (f32[19,1,16,128]{3,2,1,0:T(8,128)S(1)}, f32[19,1,16,128]{3,2,1,0:T(8,128)S(1)}, u32[]{:S(2)}, u32[]{:S(2)}) collective-permute-start(f32[19,1,16,128]{3,2,1,0:T(8,128)S(1)} %get-tuple-element.45), channel_id=1, source_target_pairs={{0,4},{4,8},{8,12},{12,16},{16,20},{20,24},{24,28},{1,5},{5,9},{9,... | collective-permute-start | bytes 466952 | tf_op jit(solution)/shard_map/ppermute | solution.py:50
  10.9 1.3 %collective-permute-start.1 = (f32[19,1,16,128]{3,2,1,0:T(8,128)S(1)}, f32[19,1,16,128]{3,2,1,0:T(8,128)S(1)}, u32[]{:S(2)}, u32[]{:S(2)}) collective-permute-start(f32[19,1,16,128]{3,2,1,0:T(8,128)S(1)} %get-tuple-element.44), channel_id=1, source_target_pairs={{4,0},{8,4},{12,8},{16,12},{20,16},{24,20},{28,24},{5,1},{9,5},{13... | collective-permute-start | bytes 466952 | tf_op jit(solution)/shard_map/ppermute | solution.py:52
  12.2 1.3 %collective-permute-start.7 = (f32[8,16,128]{2,1,0:T(8,128)S(1)}, f32[8,16,128]{2,1,0:T(8,128)S(1)}, u32[]{:S(2)}, u32[]{:S(2)}) collective-permute-start(f32[8,16,128]{2,1,0:T(8,128)S(1)} %get-tuple-element.56), channel_id=1, source_target_pairs={{4,0},{8,4},{12,8},{16,12},{20,16},{24,20},{28,24},{5,1},{9,5},{13... | collective-permute-start | bytes 196616 | tf_op jit(solution)/shard_map/ppermute | solution.py:52
  14.4 5.0 %collective-permute-done.7 = f32[8,16,128]{2,1,0:T(8,128)S(1)} collective-permute-done((f32[8,16,128]{2,1,0:T(8,128)S(1)}, f32[8,16,128]{2,1,0:T(8,128)S(1)}, u32[]{:S(2)}, u32[]{:S(2)}) %collective-permute-start.7) | collective-permute-done | bytes 65568 | tf_op jit(solution)/shard_map/ppermute | solution.py:52
  19.4 3.4 %collective-permute-start.8 = (f32[32,8,128]{2,1,0:T(8,128)S(1)}, f32[32,8,128]{2,1,0:T(8,128)S(1)}, u32[]{:S(2)}, u32[]{:S(2)}) collective-permute-start(f32[32,8,128]{2,1,0:T(8,128)S(1)} %get-tuple-element.52), channel_id=1, source_target_pairs={{0,2},{1,3},{4,6},{5,7},{8,10},{9,11},{12,14},{13,15},{16,18},{17,... | collective-permute-start | bytes 393224 | tf_op jit(solution)/shard_map/ppermute | solution.py:50
  22.9 1.3 %collective-permute-start.9 = (f32[32,8,128]{2,1,0:T(8,128)S(1)}, f32[32,8,128]{2,1,0:T(8,128)S(1)}, u32[]{:S(2)}, u32[]{:S(2)}) collective-permute-start(f32[32,8,128]{2,1,0:T(8,128)S(1)} %get-tuple-element.53), channel_id=1, source_target_pairs={{2,0},{3,1},{6,4},{7,5},{10,8},{11,9},{14,12},{15,13},{18,16},{19,... | collective-permute-start | bytes 393224 | tf_op jit(solution)/shard_map/ppermute | solution.py:52
  24.2 1.9 %constant_dynamic-update-slice_fusion.1 = f32[19,18,16,128]{3,2,1,0:T(8,128)S(1)} fusion(f32[19,18,16,128]{3,2,1,0:T(8,128)S(1)} %constant_dynamic-update-slice_fusion.2, f32[19,16,16,128]{3,2,1,0:T(8,128)} %param.5), kind=kLoop, calls=%fused_computation.328 | loop fusion | bytes 4980736
  26.2 3.5 %collective-permute-done.9 = f32[32,8,128]{2,1,0:T(8,128)S(1)} collective-permute-done((f32[32,8,128]{2,1,0:T(8,128)S(1)}, f32[32,8,128]{2,1,0:T(8,128)S(1)}, u32[]{:S(2)}, u32[]{:S(2)}) %collective-permute-start.9) | collective-permute-done | bytes 131104 | tf_op jit(solution)/shard_map/ppermute | solution.py:52
  30.0 1.3 %collective-permute-start.10 = (f32[32,32,8]{2,1,0:T(8,128)S(1)}, f32[32,32,8]{2,1,0:T(8,128)S(1)}, u32[]{:S(2)}, u32[]{:S(2)}) collective-permute-start(f32[32,32,8]{2,1,0:T(8,128)S(1)} %get-tuple-element.48), channel_id=1, source_target_pairs={{0,1},{2,3},{4,5},{6,7},{8,9},{10,11},{12,13},{14,15},{16,17},{18,... | collective-permute-start | bytes 98312 | tf_op jit(solution)/shard_map/ppermute | solution.py:50
  31.3 1.3 %collective-permute-start.11 = (f32[32,32,8]{2,1,0:T(8,128)S(1)}, f32[32,32,8]{2,1,0:T(8,128)S(1)}, u32[]{:S(2)}, u32[]{:S(2)}) collective-permute-start(f32[32,32,8]{2,1,0:T(8,128)S(1)} %get-tuple-element.49), channel_id=1, source_target_pairs={{1,0},{3,2},{5,4},{7,6},{9,8},{11,10},{13,12},{15,14},{17,16},{19,... | collective-permute-start | bytes 98312 | tf_op jit(solution)/shard_map/ppermute | solution.py:52
  32.9 1.5 %collective-permute-start.2 = (f32[19,18,1,128]{3,2,1,0:T(1,128)S(1)}, f32[19,18,1,128]{3,2,1,0:T(1,128)S(1)}, u32[]{:S(2)}, u32[]{:S(2)}) collective-permute-start(f32[19,18,1,128]{3,2,1,0:T(1,128)S(1)} %get-tuple-element.42), channel_id=1, source_target_pairs={{0,2},{1,3},{4,6},{5,7},{8,10},{9,11},{12,14},{13,15},{16,18},{17,... | collective-permute-start | bytes 525320 | tf_op jit(solution)/shard_map/ppermute | solution.py:50
  34.4 1.3 %collective-permute-start.3 = (f32[19,18,1,128]{3,2,1,0:T(1,128)S(1)}, f32[19,18,1,128]{3,2,1,0:T(1,128)S(1)}, u32[]{:S(2)}, u32[]{:S(2)}) collective-permute-start(f32[19,18,1,128]{3,2,1,0:T(1,128)S(1)} %get-tuple-element.43), channel_id=1, source_target_pairs={{2,0},{3,1},{6,4},{7,5},{10,8},{11,9},{14,12},{15,13},{18,16},{19,... | collective-permute-start | bytes 525320 | tf_op jit(solution)/shard_map/ppermute | solution.py:52
  36.7 2.2 %collective-permute-done.2 = f32[19,18,1,128]{3,2,1,0:T(1,128)S(1)} collective-permute-done((f32[19,18,1,128]{3,2,1,0:T(1,128)S(1)}, f32[19,18,1,128]{3,2,1,0:T(1,128)S(1)}, u32[]{:S(2)}, u32[]{:S(2)}) %collective-permute-start.2) | collective-permute-done | bytes 175136 | tf_op jit(solution)/shard_map/ppermute | solution.py:50
  38.9 4.7 %collective-permute-done.3 = f32[19,18,1,128]{3,2,1,0:T(1,128)S(1)} collective-permute-done((f32[19,18,1,128]{3,2,1,0:T(1,128)S(1)}, f32[19,18,1,128]{3,2,1,0:T(1,128)S(1)}, u32[]{:S(2)}, u32[]{:S(2)}) %collective-permute-start.3) | collective-permute-done | bytes 175136 | tf_op jit(solution)/shard_map/ppermute | solution.py:52
  44.2 4.6 %fusion.134 = (f32[19,18,18,1]{3,2,1,0:T(8,128)}, f32[19,18,18,1]{3,2,1,0:T(8,128)}) fusion(f32[19,18,18,128]{3,2,1,0:T(8,128)S(1)} %pad_maximum_fusion.1), kind=kLoop, calls=%fused_computation.333 | loop fusion | bytes 98496 | tf_op jit(solution)/shard_map/slice | solution.py:47
  48.8 3.7 %copy.27 = f32[19,18,18,1]{0,3,2,1:T(1,128)S(1)} copy(f32[19,18,18,1]{3,2,1,0:T(8,128)} %get-tuple-element.40) | data formatting | bytes 49248 | tf_op jit(solution)/shard_map/slice | solution.py:47
  52.5 2.0 %collective-permute-start.4 = (f32[19,18,18,1]{0,3,2,1:T(1,128)S(1)}, f32[19,18,18,1]{0,3,2,1:T(1,128)S(1)}, u32[]{:S(2)}, u32[]{:S(2)}) collective-permute-start(f32[19,18,18,1]{0,3,2,1:T(1,128)S(1)} %copy.27), channel_id=1, source_target_pairs={{0,1},{2,3},{4,5},{6,7},{8,9},{10,11},{12,13},{14,15},{16,17},{18,... | collective-permute-start | bytes 73880 | tf_op jit(solution)/shard_map/ppermute | solution.py:50
  54.5 4.3 %copy.28 = f32[19,18,18,1]{0,3,2,1:T(1,128)} copy(f32[19,18,18,1]{3,2,1,0:T(8,128)} %get-tuple-element.41) | data formatting | bytes 49248 | tf_op jit(solution)/shard_map/slice | solution.py:46
  58.8 1.5 %collective-permute-start.5 = (f32[19,18,18,1]{0,3,2,1:T(1,128)}, f32[19,18,18,1]{0,3,2,1:T(1,128)}, u32[]{:S(2)}, u32[]{:S(2)}) collective-permute-start(f32[19,18,18,1]{0,3,2,1:T(1,128)} %copy.28), channel_id=1, source_target_pairs={{1,0},{3,2},{5,4},{7,6},{9,8},{11,10},{13,12},{15,14},{17,16},{19,... | collective-permute-start | bytes 73880 | tf_op jit(solution)/shard_map/ppermute | solution.py:52
  60.8 4.1 %copy.29 = f32[19,18,18,1]{3,2,1,0:T(8,128)} copy(f32[19,18,18,1]{0,3,2,1:T(1,128)S(1)} %collective-permute-done.4) | data formatting | bytes 49248 | tf_op jit(solution)/shard_map/ppermute | solution.py:50
  65.0 5.2 %copy.30 = f32[19,18,18,1]{3,2,1,0:T(8,128)} copy(f32[19,18,18,1]{0,3,2,1:T(1,128)} %collective-permute-done.5) | data formatting | bytes 49248 | tf_op jit(solution)/shard_map/ppermute | solution.py:52
  70.2 8.4 %pad_maximum_fusion = f32[19,18,18,130]{3,2,1,0:T(8,128)S(1)} fusion(f32[19,18,18,1]{3,2,1,0:T(8,128)} %copy.30, f32[19,18,1,128]{3,2,1,0:T(1,128)S(1)} %collective-permute-done.3, f32[19,18,16,128]{3,2,1,0:T(8,128)S(1)} %copy-done.1, f32[19,18,1,128]{3,2,1,0:T(1,128)S(1)} %collective-permute-done.2, f32[19,18,18,1]{3,2,1,0:T(8,128)} %copy.29), kind=kLoop, calls=%fused_computation | loop fusion | flops 3201120 | bytes 6402240 | tf_op jit(solution)/shard_map/concatenate | solution.py:48
  81.4 4.4 %collective-permute-start.12 = (f32[8,16,128]{2,1,0:T(8,128)S(1)}, f32[8,16,128]{2,1,0:T(8,128)S(1)}, u32[]{:S(2)}, u32[]{:S(2)}) collective-permute-start(f32[8,16,128]{2,1,0:T(8,128)S(1)} %get-tuple-element.54), channel_id=1, source_target_pairs={{0,4},{4,8},{8,12},{12,16},{16,20},{20,24},{24,28},{1,5},{5,9},{9,... | collective-permute-start | bytes 196616 | tf_op jit(solution)/shard_map/ppermute | solution.py:50
  85.8 1.3 %collective-permute-start.13 = (f32[8,16,128]{2,1,0:T(8,128)S(1)}, f32[8,16,128]{2,1,0:T(8,128)S(1)}, u32[]{:S(2)}, u32[]{:S(2)}) collective-permute-start(f32[8,16,128]{2,1,0:T(8,128)S(1)} %get-tuple-element.55), channel_id=1, source_target_pairs={{4,0},{8,4},{12,8},{16,12},{20,16},{24,20},{28,24},{5,1},{9,5},{13... | collective-permute-start | bytes 196616 | tf_op jit(solution)/shard_map/ppermute | solution.py:52
  92.4 1.5 %collective-permute-start.14 = (f32[32,8,128]{2,1,0:T(8,128)S(1)}, f32[32,8,128]{2,1,0:T(8,128)S(1)}, u32[]{:S(2)}, u32[]{:S(2)}) collective-permute-start(f32[32,8,128]{2,1,0:T(8,128)S(1)} %get-tuple-element.50), channel_id=1, source_target_pairs={{0,2},{1,3},{4,6},{5,7},{8,10},{9,11},{12,14},{13,15},{16,18},{17,... | collective-permute-start | bytes 393224 | tf_op jit(solution)/shard_map/ppermute | solution.py:50
  93.9 1.5 %collective-permute-start.15 = (f32[32,8,128]{2,1,0:T(8,128)S(1)}, f32[32,8,128]{2,1,0:T(8,128)S(1)}, u32[]{:S(2)}, u32[]{:S(2)}) collective-permute-start(f32[32,8,128]{2,1,0:T(8,128)S(1)} %get-tuple-element.51), channel_id=1, source_target_pairs={{2,0},{3,1},{6,4},{7,5},{10,8},{11,9},{14,12},{15,13},{18,16},{19,... | collective-permute-start | bytes 393224 | tf_op jit(solution)/shard_map/ppermute | solution.py:52
  95.6 2.0 %collective-permute-done.14 = f32[32,8,128]{2,1,0:T(8,128)S(1)} collective-permute-done((f32[32,8,128]{2,1,0:T(8,128)S(1)}, f32[32,8,128]{2,1,0:T(8,128)S(1)}, u32[]{:S(2)}, u32[]{:S(2)}) %collective-permute-start.14) | collective-permute-done | bytes 131104 | tf_op jit(solution)/shard_map/ppermute | solution.py:50
  97.7 4.3 %collective-permute-done.15 = f32[32,8,128]{2,1,0:T(8,128)S(1)} collective-permute-done((f32[32,8,128]{2,1,0:T(8,128)S(1)}, f32[32,8,128]{2,1,0:T(8,128)S(1)}, u32[]{:S(2)}, u32[]{:S(2)}) %collective-permute-start.15) | collective-permute-done | bytes 131104 | tf_op jit(solution)/shard_map/ppermute | solution.py:52
  102.3 1.9 %collective-permute-start.16 = (f32[32,32,8]{2,1,0:T(8,128)S(1)}, f32[32,32,8]{2,1,0:T(8,128)S(1)}, u32[]{:S(2)}, u32[]{:S(2)}) collective-permute-start(f32[32,32,8]{2,1,0:T(8,128)S(1)} %get-tuple-element.46), channel_id=1, source_target_pairs={{0,1},{2,3},{4,5},{6,7},{8,9},{10,11},{12,13},{14,15},{16,17},{18,... | collective-permute-start | bytes 98312 | tf_op jit(solution)/shard_map/ppermute | solution.py:50
  104.1 1.3 %collective-permute-start.17 = (f32[32,32,8]{2,1,0:T(8,128)S(1)}, f32[32,32,8]{2,1,0:T(8,128)S(1)}, u32[]{:S(2)}, u32[]{:S(2)}) collective-permute-start(f32[32,32,8]{2,1,0:T(8,128)S(1)} %get-tuple-element.47), channel_id=1, source_target_pairs={{1,0},{3,2},{5,4},{7,6},{9,8},{11,10},{13,12},{15,14},{17,16},{19,... | collective-permute-start | bytes 98312 | tf_op jit(solution)/shard_map/ppermute | solution.py:52
  105.7 2.3 %collective-permute-done.17 = f32[32,32,8]{2,1,0:T(8,128)S(1)} collective-permute-done((f32[32,32,8]{2,1,0:T(8,128)S(1)}, f32[32,32,8]{2,1,0:T(8,128)S(1)}, u32[]{:S(2)}, u32[]{:S(2)}) %collective-permute-start.17) | collective-permute-done | bytes 32800 | tf_op jit(solution)/shard_map/ppermute | solution.py:52
  (66 shorter events, 17.1 us)
Async XLA Ops:
  1.5 11.9 %collective-permute-start.6 = (f32[8,16,128]{2,1,0:T(8,128)S(1)}, f32[8,16,128]{2,1,0:T(8,128)S(1)}, u32[]{:S(2)}, u32[]{:S(2)}) collective-permute-start(f32[8,16,128]{2,1,0:T(8,128)S(1)} %get-tuple-element.57), channel_id=1, source_target_pairs={{0,4},{4,8},{8,12},{12,16},{16,20},{20,24},{24,28},{1,5},{5,9},{9,... | collective-permute-start | bytes 196616 | tf_op jit(solution)/shard_map/ppermute | solution.py:50
  7.4 16.8 %collective-permute-start = (f32[19,1,16,128]{3,2,1,0:T(8,128)S(1)}, f32[19,1,16,128]{3,2,1,0:T(8,128)S(1)}, u32[]{:S(2)}, u32[]{:S(2)}) collective-permute-start(f32[19,1,16,128]{3,2,1,0:T(8,128)S(1)} %get-tuple-element.45), channel_id=1, source_target_pairs={{0,4},{4,8},{8,12},{12,16},{16,20},{20,24},{24,28},{1,5},{5,9},{9,... | collective-permute-start | bytes 466952 | tf_op jit(solution)/shard_map/ppermute | solution.py:50
  10.9 15.3 %collective-permute-start.1 = (f32[19,1,16,128]{3,2,1,0:T(8,128)S(1)}, f32[19,1,16,128]{3,2,1,0:T(8,128)S(1)}, u32[]{:S(2)}, u32[]{:S(2)}) collective-permute-start(f32[19,1,16,128]{3,2,1,0:T(8,128)S(1)} %get-tuple-element.44), channel_id=1, source_target_pairs={{4,0},{8,4},{12,8},{16,12},{20,16},{24,20},{28,24},{5,1},{9,5},{13... | collective-permute-start | bytes 466952 | tf_op jit(solution)/shard_map/ppermute | solution.py:52
  12.2 7.2 %collective-permute-start.7 = (f32[8,16,128]{2,1,0:T(8,128)S(1)}, f32[8,16,128]{2,1,0:T(8,128)S(1)}, u32[]{:S(2)}, u32[]{:S(2)}) collective-permute-start(f32[8,16,128]{2,1,0:T(8,128)S(1)} %get-tuple-element.56), channel_id=1, source_target_pairs={{4,0},{8,4},{12,8},{16,12},{20,16},{24,20},{28,24},{5,1},{9,5},{13... | collective-permute-start | bytes 196616 | tf_op jit(solution)/shard_map/ppermute | solution.py:52
  19.4 6.8 %collective-permute-start.8 = (f32[32,8,128]{2,1,0:T(8,128)S(1)}, f32[32,8,128]{2,1,0:T(8,128)S(1)}, u32[]{:S(2)}, u32[]{:S(2)}) collective-permute-start(f32[32,8,128]{2,1,0:T(8,128)S(1)} %get-tuple-element.52), channel_id=1, source_target_pairs={{0,2},{1,3},{4,6},{5,7},{8,10},{9,11},{12,14},{13,15},{16,18},{17,... | collective-permute-start | bytes 393224 | tf_op jit(solution)/shard_map/ppermute | solution.py:50
  22.9 6.9 %collective-permute-start.9 = (f32[32,8,128]{2,1,0:T(8,128)S(1)}, f32[32,8,128]{2,1,0:T(8,128)S(1)}, u32[]{:S(2)}, u32[]{:S(2)}) collective-permute-start(f32[32,8,128]{2,1,0:T(8,128)S(1)} %get-tuple-element.53), channel_id=1, source_target_pairs={{2,0},{3,1},{6,4},{7,5},{10,8},{11,9},{14,12},{15,13},{18,16},{19,... | collective-permute-start | bytes 393224 | tf_op jit(solution)/shard_map/ppermute | solution.py:52
  26.2 17.4 %copy-start = (f32[19,18,16,128]{3,2,1,0:T(8,128)}, f32[19,18,16,128]{3,2,1,0:T(8,128)S(1)}, u32[]{:S(2)}) copy-start(f32[19,18,16,128]{3,2,1,0:T(8,128)S(1)} %constant_dynamic-update-slice_fusion) | copy-start | bytes 8404996
  30.0 5.7 %collective-permute-start.10 = (f32[32,32,8]{2,1,0:T(8,128)S(1)}, f32[32,32,8]{2,1,0:T(8,128)S(1)}, u32[]{:S(2)}, u32[]{:S(2)}) collective-permute-start(f32[32,32,8]{2,1,0:T(8,128)S(1)} %get-tuple-element.48), channel_id=1, source_target_pairs={{0,1},{2,3},{4,5},{6,7},{8,9},{10,11},{12,13},{14,15},{16,17},{18,... | collective-permute-start | bytes 98312 | tf_op jit(solution)/shard_map/ppermute | solution.py:50
  31.3 4.4 %collective-permute-start.11 = (f32[32,32,8]{2,1,0:T(8,128)S(1)}, f32[32,32,8]{2,1,0:T(8,128)S(1)}, u32[]{:S(2)}, u32[]{:S(2)}) collective-permute-start(f32[32,32,8]{2,1,0:T(8,128)S(1)} %get-tuple-element.49), channel_id=1, source_target_pairs={{1,0},{3,2},{5,4},{7,6},{9,8},{11,10},{13,12},{15,14},{17,16},{19,... | collective-permute-start | bytes 98312 | tf_op jit(solution)/shard_map/ppermute | solution.py:52
  32.9 6.0 %collective-permute-start.2 = (f32[19,18,1,128]{3,2,1,0:T(1,128)S(1)}, f32[19,18,1,128]{3,2,1,0:T(1,128)S(1)}, u32[]{:S(2)}, u32[]{:S(2)}) collective-permute-start(f32[19,18,1,128]{3,2,1,0:T(1,128)S(1)} %get-tuple-element.42), channel_id=1, source_target_pairs={{0,2},{1,3},{4,6},{5,7},{8,10},{9,11},{12,14},{13,15},{16,18},{17,... | collective-permute-start | bytes 525320 | tf_op jit(solution)/shard_map/ppermute | solution.py:50
  34.4 9.2 %collective-permute-start.3 = (f32[19,18,1,128]{3,2,1,0:T(1,128)S(1)}, f32[19,18,1,128]{3,2,1,0:T(1,128)S(1)}, u32[]{:S(2)}, u32[]{:S(2)}) collective-permute-start(f32[19,18,1,128]{3,2,1,0:T(1,128)S(1)} %get-tuple-element.43), channel_id=1, source_target_pairs={{2,0},{3,1},{6,4},{7,5},{10,8},{11,9},{14,12},{15,13},{18,16},{19,... | collective-permute-start | bytes 525320 | tf_op jit(solution)/shard_map/ppermute | solution.py:52
  52.5 8.3 %collective-permute-start.4 = (f32[19,18,18,1]{0,3,2,1:T(1,128)S(1)}, f32[19,18,18,1]{0,3,2,1:T(1,128)S(1)}, u32[]{:S(2)}, u32[]{:S(2)}) collective-permute-start(f32[19,18,18,1]{0,3,2,1:T(1,128)S(1)} %copy.27), channel_id=1, source_target_pairs={{0,1},{2,3},{4,5},{6,7},{8,9},{10,11},{12,13},{14,15},{16,17},{18,... | collective-permute-start | bytes 73880 | tf_op jit(solution)/shard_map/ppermute | solution.py:50
  58.8 6.2 %collective-permute-start.5 = (f32[19,18,18,1]{0,3,2,1:T(1,128)}, f32[19,18,18,1]{0,3,2,1:T(1,128)}, u32[]{:S(2)}, u32[]{:S(2)}) collective-permute-start(f32[19,18,18,1]{0,3,2,1:T(1,128)} %copy.28), channel_id=1, source_target_pairs={{1,0},{3,2},{5,4},{7,6},{9,8},{11,10},{13,12},{15,14},{17,16},{19,... | collective-permute-start | bytes 73880 | tf_op jit(solution)/shard_map/ppermute | solution.py:52
  65.0 5.2 %copy-start.1 = (f32[19,18,16,128]{3,2,1,0:T(8,128)S(1)}, f32[19,18,16,128]{3,2,1,0:T(8,128)}, u32[]{:S(2)}) copy-start(f32[19,18,16,128]{3,2,1,0:T(8,128)} %copy-done) | copy-start | bytes 8404996
  78.6 1.7 %copy-start.2 = (f32[19,16,16,128]{3,2,1,0:T(8,128)S(1)}, f32[19,16,16,128]{3,2,1,0:T(8,128)}, u32[]{:S(2)}) copy-start(f32[19,16,16,128]{3,2,1,0:T(8,128)} %param.4) | copy-start | bytes 7471108
  80.3 6.8 %copy-start.3 = (s32[16,16,128]{2,1,0:T(8,128)S(1)}, s32[16,16,128]{2,1,0:T(8,128)}, u32[]{:S(2)}) copy-start(s32[16,16,128]{2,1,0:T(8,128)} %param.7) | copy-start | bytes 393220
  81.4 10.6 %collective-permute-start.12 = (f32[8,16,128]{2,1,0:T(8,128)S(1)}, f32[8,16,128]{2,1,0:T(8,128)S(1)}, u32[]{:S(2)}, u32[]{:S(2)}) collective-permute-start(f32[8,16,128]{2,1,0:T(8,128)S(1)} %get-tuple-element.54), channel_id=1, source_target_pairs={{0,4},{4,8},{8,12},{12,16},{16,20},{20,24},{24,28},{1,5},{5,9},{9,... | collective-permute-start | bytes 196616 | tf_op jit(solution)/shard_map/ppermute | solution.py:50
  85.8 6.6 %collective-permute-start.13 = (f32[8,16,128]{2,1,0:T(8,128)S(1)}, f32[8,16,128]{2,1,0:T(8,128)S(1)}, u32[]{:S(2)}, u32[]{:S(2)}) collective-permute-start(f32[8,16,128]{2,1,0:T(8,128)S(1)} %get-tuple-element.55), channel_id=1, source_target_pairs={{4,0},{8,4},{12,8},{16,12},{20,16},{24,20},{28,24},{5,1},{9,5},{13... | collective-permute-start | bytes 196616 | tf_op jit(solution)/shard_map/ppermute | solution.py:52
  92.4 5.2 %collective-permute-start.14 = (f32[32,8,128]{2,1,0:T(8,128)S(1)}, f32[32,8,128]{2,1,0:T(8,128)S(1)}, u32[]{:S(2)}, u32[]{:S(2)}) collective-permute-start(f32[32,8,128]{2,1,0:T(8,128)S(1)} %get-tuple-element.50), channel_id=1, source_target_pairs={{0,2},{1,3},{4,6},{5,7},{8,10},{9,11},{12,14},{13,15},{16,18},{17,... | collective-permute-start | bytes 393224 | tf_op jit(solution)/shard_map/ppermute | solution.py:50
  93.9 8.1 %collective-permute-start.15 = (f32[32,8,128]{2,1,0:T(8,128)S(1)}, f32[32,8,128]{2,1,0:T(8,128)S(1)}, u32[]{:S(2)}, u32[]{:S(2)}) collective-permute-start(f32[32,8,128]{2,1,0:T(8,128)S(1)} %get-tuple-element.51), channel_id=1, source_target_pairs={{2,0},{3,1},{6,4},{7,5},{10,8},{11,9},{14,12},{15,13},{18,16},{19,... | collective-permute-start | bytes 393224 | tf_op jit(solution)/shard_map/ppermute | solution.py:52
  102.3 3.4 %collective-permute-start.16 = (f32[32,32,8]{2,1,0:T(8,128)S(1)}, f32[32,32,8]{2,1,0:T(8,128)S(1)}, u32[]{:S(2)}, u32[]{:S(2)}) collective-permute-start(f32[32,32,8]{2,1,0:T(8,128)S(1)} %get-tuple-element.46), channel_id=1, source_target_pairs={{0,1},{2,3},{4,5},{6,7},{8,9},{10,11},{12,13},{14,15},{16,17},{18,... | collective-permute-start | bytes 98312 | tf_op jit(solution)/shard_map/ppermute | solution.py:50
  104.1 3.8 %collective-permute-start.17 = (f32[32,32,8]{2,1,0:T(8,128)S(1)}, f32[32,32,8]{2,1,0:T(8,128)S(1)}, u32[]{:S(2)}, u32[]{:S(2)}) collective-permute-start(f32[32,32,8]{2,1,0:T(8,128)S(1)} %get-tuple-element.47), channel_id=1, source_target_pairs={{1,0},{3,2},{5,4},{7,6},{9,8},{11,10},{13,12},{15,14},{17,16},{19,... | collective-permute-start | bytes 98312 | tf_op jit(solution)/shard_map/ppermute | solution.py:52
  105.6 3.3 %copy-start.4 = (f32[19,16,16,128]{3,2,1,0:T(8,128)}, f32[19,16,16,128]{3,2,1,0:T(8,128)S(1)}, u32[]{:S(2)}) copy-start(f32[19,16,16,128]{3,2,1,0:T(8,128)S(1)} %bitcast_dynamic-update-slice_fusion) | copy-start | bytes 7471108
where the time goes:
time: 112 us; the launch traced here: 111 us
  starting transfers between devices  36.3 us (32%)
  local copies, waits for them, and re-layouts  29.1 us (26%)
  waiting for transfers between devices  24.4 us (22%)
  other arithmetic  19.8 us (18%)
    ppermute x9, starting transfers between devices, extended(): lax.ppermute(tail, axis, [(i, (i + 1) % count) for i in range(ends)])  24.3 us
    ppermute x9, waiting for transfers between devices, extended(): lax.ppermute(head, axis, [((i + 1) % count, i) for i in range(ends)])  20.2 us
    ppermute x9, starting transfers between devices, extended(): lax.ppermute(head, axis, [((i + 1) % count, i) for i in range(ends)])  12 us
    concatenate x7, other arithmetic, extended(): jnp.concatenate([lax.ppermute(tail, axis, [(i, (i + 1) % count) for i in...  10.1 us
    slice x8, local copies, waits for them, and re-layouts, extended(): lax.slice_in_dim(cells, cells.shape[dim] - width, cells.shape[dim], axis=...  8.98 us
    slice x3, local copies, waits for them, and re-layouts, extended(): head = lax.slice_in_dim(cells, 0, width, axis=dim)  6.22 us
    ppermute x1, local copies, waits for them, and re-layouts, extended(): lax.ppermute(head, axis, [((i + 1) % count, i) for i in range(ends)])  5.17 us
    unnamed x18, other arithmetic  5.05 us
  transfers between devices with their start and end apart: 18, of which 8 were waited for; matrix products, arithmetic and copies ran while one was open for 18% of the time, Pallas kernels for 0%

commit v1 on v0

v1 whole, which is shorter than its diff:
```python
import functools
import math

import jax
import jax.numpy as jnp
import numpy as np
from jax import lax
from jax.experimental import pallas as pl
from jax.experimental.pallas import tpu as pltpu
from jax.sharding import PartitionSpec as P

Q = 19
R = 8

velocity = [
    (0, 0, 0),
    (1, 0, 0),
    (-1, 0, 0),
    (0, 1, 0),
    (0, -1, 0),
    (0, 0, 1),
    (0, 0, -1),
    (1, 1, 0),
    (-1, -1, 0),
    (1, -1, 0),
    (-1, 1, 0),
    (1, 0, 1),
    (-1, 0, -1),
    (1, 0, -1),
    (-1, 0, 1),
    (0, 1, 1),
    (0, -1, -1),
    (0, 1, -1),
    (0, -1, 1),
]
relax_rate = 1.25
sharpness = 64.0
threshold = 0.5
damping_max = 10.0
ramp_shape = 0.1


def fields_of(axis, sign):
    plus = [q for q in range(Q) if velocity[q][axis] == 1]
    return plus if sign > 0 else [q + 1 if q % 2 else q - 1 for q in plus]


PLUS = [fields_of(a, 1) for a in range(3)]
MINUS = [fields_of(a, -1) for a in range(3)]


def tap_weights():
    spread_width = R / 2.0
    unscaled = [math.exp(-((k - R) ** 2) / (2.0 * spread_width * spread_width)) for k in range(2 * R + 1)]
    summed = sum(unscaled)
    return [v / summed for v in unscaled]


TAPS = tap_weights()


def band(length):
    out = np.zeros((3, length, length), np.float32)
    for i in range(length):
        for k in range(-R, R + 1):
            j = i + k
            if j < 0:
                out[1, j + length, i] = TAPS[k + R]
            elif j >= length:
                out[2, j - length, i] = TAPS[k + R]
            else:
                out[0, j, i] = TAPS[k + R]
    return out


def sides(parity, even, odd):
    zero = jnp.zeros_like(even)
    if odd is None:
        return jnp.where(parity == 0, zero, even), jnp.where(parity == 0, even, zero)
    return jnp.where(parity == 0, odd, even), jnp.where(parity == 0, even, odd)


def parity_of(axis):
    return lax.rem(lax.axis_index(axis), 2)


def exchange(axis, count, even, odd):
    got_odd = None
    if odd is not None:
        pairs = [(i, i + 1) for i in range(1, count - 1, 2)]
        got_odd = lax.ppermute(odd, axis, pairs + [(b, a) for a, b in pairs])
    pairs = [(i, i + 1) for i in range(0, count - 1, 2)]
    got_even = lax.ppermute(even, axis, pairs + [(b, a) for a, b in pairs])
    return got_even, got_odd


def vmem(count):
    return [pl.BlockSpec(memory_space=pltpu.VMEM)] * count


def f32(*shape):
    return jax.ShapeDtypeStruct(shape, jnp.float32)


def call(body, outs, args, specs=None, scratch=(), limit=16, flops=1e6, moved=1e6, **rest):
    return pl.pallas_call(
        body,
        out_shape=outs,
        in_specs=specs or vmem(len(args)),
        out_specs=rest.pop("out_specs", tuple(vmem(len(outs)))),
        scratch_shapes=list(scratch),
        compiler_params=pltpu.CompilerParams(vmem_limit_bytes=limit * 2**20),
        cost_estimate=pl.CostEstimate(flops=int(flops), bytes_accessed=int(moved), transcendentals=0),
        **rest,
    )(*args)


def filter_rows(load):
    total = TAPS[R] * load(R)
    for k in range(R):
        total = total + TAPS[k] * (load(k) + load(2 * R - k))
    return total


def dot(a, b):
    return jnp.dot(a, b, preferred_element_type=jnp.float32, precision=lax.Precision.HIGHEST)


def row_of(ref, at):
    return ref[pl.ds(at, 1), :]


class Pull:
    def __init__(self, adj, dims, py, y_even, y_odd, pz=None, z_even=None, z_odd=None):
        self.adj, self.dims = adj, dims
        self.py, self.y_even, self.y_odd = py, y_even, y_odd
        self.pz, self.z_even, self.z_odd = pz, z_even, z_odd
        X, Y, Z = dims
        self.row = lax.broadcasted_iota(jnp.int32, (Y, Z), 0)
        self.lane = lax.broadcasted_iota(jnp.int32, (Y, Z), 1)

    def along_y(self, q, x):
        X, Y, Z = self.dims
        here = self.adj[q, x]
        cy = velocity[q][1]
        if cy == 0:
            return here
        at = X * R + X * (PLUS if cy > 0 else MINUS)[1].index(q) + x
        even = row_of(self.y_even, at)
        odd = None if self.y_odd is None else row_of(self.y_odd, at)
        below, above = sides(self.py, even, odd)
        if cy > 0:
            return jnp.where(self.row == Y - 1, above, pltpu.roll(here, Y - 1, 0))
        return jnp.where(self.row == 0, below, pltpu.roll(here, 1, 0))

    def faces(self, x):
        even = self.z_even[x]
        odd = None if self.z_odd is None else self.z_odd[x]
        return sides(self.pz, even, odd)

    def both(self, q, x, faces):
        X, Y, Z = self.dims
        here = self.along_y(q, x)
        cz = velocity[q][2]
        if cz == 0:
            return here
        below, above = faces
        if cz > 0:
            j = PLUS[2].index(q)
            face = pltpu.roll(above, 4 - j, 1) if j != 4 else above
            return jnp.where(self.lane == Z - 1, face, pltpu.roll(here, Z - 1, 1))
        j = MINUS[2].index(q)
        face = pltpu.roll(below, Z - j, 1) if j else below
        return jnp.where(self.lane == 0, face, pltpu.roll(here, 1, 1))


def refs_of(refs, odd):
    even = next(refs)
    return even, (next(refs) if odd else None)


def pack_y(dims, many, adj, design, *rest):
    X, Y, Z = dims
    outs = rest[: 1 + many]
    tiles, sems = rest[1 + many :]
    py = parity_of("gy")

    def fill(n, out, up):
        names = (MINUS if up else PLUS)[1]
        first = Y - R if up else 0
        copies = [
            pltpu.make_async_copy(adj.at[q, :, pl.ds(first, R), :], tiles.at[n, j], sems.at[n, j])
            for j, q in enumerate(names)
        ]
        for c in copies:
            c.start()
        out[: X * R, :] = design[:, first : first + R, :].reshape(X * R, Z)
        for c in copies:
            c.wait()
        for j in range(5):
            out[X * R + X * j : X * R + X * (j + 1), :] = tiles[n, j, :, R - 1 if up else 0, :]

    for n, out in enumerate(outs):

        @pl.when(py == n)
        def _(n=n, out=out):
            fill(n, out, True)

        @pl.when(py != n)
        def _(n=n, out=out):
            fill(n, out, False)


def flow(forward, out):
    members = [forward[q] for q in range(Q)]
    rho = members[0]
    for q in range(1, Q):
        rho = rho + members[q]
    inverse = 1.0 / rho
    for a in range(3):
        total = None
        for q in range(1, Q, 2):
            c = velocity[q][a]
            if c == 0:
                continue
            term = members[q] - members[q + 1]
            term = term if c > 0 else -term
            total = term if total is None else total + term
        out[a] = total * inverse
    out[3] = inverse


def extend_y(dims, pad, own, py, even, odd):
    X, Y, Z = dims
    below, above = sides(py, even, odd)
    pad[:, :R, :] = below
    pad[:, R : R + Y, :] = own
    pad[:, R + Y :, :] = above


def filter_y(dims, pad, store, step=2):
    X, Y, Z = dims
    for x in range(0, X, step):
        store(x, filter_rows(lambda k: pad[x : x + step, k : k + Y, :]))


def design_y(dims, many_y, many_z, adj, design, *rest):
    X, Y, Z = dims
    rest = iter(rest)
    y_even, y_odd = refs_of(rest, many_y)
    filtered = next(rest)
    outs = [next(rest) for _ in range(1 + many_z)]
    pad, held, sems = rest
    pz = parity_of("gz")
    py = parity_of("gy")

    def fetch(up, n):
        names = (MINUS if up else PLUS)[2]
        return [
            pltpu.make_async_copy(adj.at[q], held.at[n, j], sems.at[n, j]) for j, q in enumerate(names)
        ]

    for n, out in enumerate(outs):

        @pl.when(pz == n)
        def _(n=n):
            for c in fetch(True, n):
                c.start()

        @pl.when(pz != n)
        def _(n=n):
            for c in fetch(False, n):
                c.start()

    def halo(ref):
        return ref[: X * R, :].reshape(X, R, Z)

    extend_y(dims, pad, design[...], py, halo(y_even), None if y_odd is None else halo(y_odd))

    def store(x, value):
        filtered[x : x + value.shape[0]] = value

    filter_y(dims, pad, store)

    def fill(out, up, n):
        names = (MINUS if up else PLUS)[2]
        for c in fetch(up, n):
            c.wait()
        by_name = {q: held.at[n, j] for j, q in enumerate(names)}

        class Held:
            def __getitem__(self, at):
                return by_name[at[0]][at[1]]

        pull = Pull(Held(), dims, py, y_even, y_odd)

        def layer(x, _):
            value = filtered[x]
            for j, q in enumerate(names):
                slot = j if up else Z - 5 + j
                shift = (slot - (Z - 1 if up else 0)) % Z
                value = jnp.where(pull.lane == slot, pltpu.roll(pull.along_y(q, x), shift, 1), value)
            out[x] = value
            return 0

        lax.fori_loop(0, X, layer, 0, unroll=2)

    for n, out in enumerate(outs):

        @pl.when(pz == n)
        def _(n=n, out=out):
            fill(out, True, n)

        @pl.when(pz != n)
        def _(n=n, out=out):
            fill(out, False, n)


def signed(terms):
    total = None
    for sign, value in terms:
        value = value if sign > 0 else -value
        total = value if total is None else total + value
    return total


def moment_of(values):
    return [
        signed([(velocity[q][a], v) for q, v in values.items() if velocity[q][a] != 0]) for a in range(3)
    ]


def filter_z(weights, own, pz, even, odd):
    value = dot(own, weights[0]) + dot(even, jnp.where(pz == 0, weights[2], weights[1]))
    if odd is not None:
        value = value + dot(odd, jnp.where(pz == 0, weights[1], weights[2]))
    return value


def pack_x(dims, many_x, many_y, many_z, adj, weights, filtered_y, flow_ref, *rest):
    X, Y, Z = dims
    rest = iter(rest)
    y_even, y_odd = refs_of(rest, many_y)
    z_even, z_odd = refs_of(rest, many_z)
    outs = [next(rest) for _ in range(1 + many_x)]
    factor = next(rest)
    local, rising, falling, sems = rest
    px, py, pz = parity_of("gx"), parity_of("gy"), parity_of("gz")
    part = X // 4
    copies = [
        pltpu.make_async_copy(
            adj.at[:, pl.ds(i * part, part)], local.at[:, pl.ds(i * part, part)], sems.at[i]
        )
        for i in range(4)
    ]
    for c in copies:
        c.start()
    smooth = filter_z(
        weights,
        filtered_y[...].reshape(X * Y, Z),
        pz,
        z_even[...].reshape(X * Y, Z),
        None if z_odd is None else z_odd[...].reshape(X * Y, Z),
    )
    for out in outs:
        out[: X * Y, :] = smooth
    pull = Pull(local, dims, py, y_even, y_odd, pz, z_even, z_odd)

    def layer(x, _):
        faces = pull.faces(x)
        groups = {}
        for q in range(1, Q):
            groups.setdefault(velocity[q][0], {})[q] = pull.both(q, x, faces)
        level = moment_of(groups[0])
        up = moment_of(groups[1])
        down = moment_of(groups[-1])
        for a in range(3):
            rising[a, x] = up[a]
            falling[a, x + 2] = down[a]
        vel = [flow_ref[a, x] for a in range(3)]
        factor[x] = vel[0] * vel[0] + vel[1] * vel[1] + vel[2] * vel[2] - vel[1] * level[1] - vel[2] * level[2]
        return 0

    zero = jnp.zeros((Y, Z), jnp.float32)
    for a in range(3):
        rising[a, X] = zero
        falling[a, 1] = zero
    for i, c in enumerate(copies):
        c.wait()
        lax.fori_loop(i * part, (i + 1) * part, layer, 0)

    def finish(x, _):
        total = factor[x]
        for a in range(3):
            total = total - flow_ref[a, x] * (rising[a, x + 1] + falling[a, x + 1])
        factor[x] = total
        return 0

    lax.fori_loop(0, X, finish, 0, unroll=4)

    def fill(out, up):
        names = (MINUS if up else PLUS)[0]
        edge = X - 1 if up else 0
        at = X * Y
        first = X - R if up else 0
        out[at : at + R * Y, :] = factor[first : first + R].reshape(R * Y, Z)
        at += R * Y
        faces = pull.faces(edge)
        for q in names:
            out[at : at + Y, :] = pull.both(q, edge, faces)
            at += Y
        for a in range(3):
            out[at : at + Y, :] = flow_ref[a, edge]
            at += Y

    for n, out in enumerate(outs):

        @pl.when(px == n)
        def _(out=out):
            fill(out, True)

        @pl.when(px != n)
        def _(out=out):
            fill(out, False)


def project(filtered):
    base = math.tanh(sharpness * threshold)
    denominator = base + math.tanh(sharpness * (1.0 - threshold))
    inner = jnp.tanh(sharpness * (filtered - threshold))
    physical = (base + inner) * (1.0 / denominator)
    steep = (sharpness / denominator) * (1.0 - inner * inner)
    inverse = 1.0 / (ramp_shape + physical)
    return physical, steep, inverse


def source(dims, many_x, many_y, factor, flow_ref, *rest):
    X, Y, Z = dims
    rest = iter(rest)
    own_even, own_odd = refs_of(rest, many_x)
    x_even, x_odd = refs_of(rest, many_x)
    result, damp = next(rest), next(rest)
    outs = [next(rest) for _ in range(1 + many_y)]
    layers, ext = rest
    px, py = parity_of("gx"), parity_of("gy")
    size = X * Y
    g_at, u_at, v_at = size, size + R * Y, size + R * Y + 5 * Y

    def got(at, count):
        return sides(px, x_even[at : at + count, :], None if x_odd is None else x_odd[at : at + count, :])

    def own(at, count):
        return sides(px, own_even[at : at + count, :], None if own_odd is None else own_odd[at : at + count, :])

    below, above = got(0, size)
    layers[:X] = below.reshape(X, Y, Z)
    layers[X : 2 * X] = own_even[:size, :].reshape(X, Y, Z)
    layers[2 * X :] = above.reshape(X, Y, Z)

    below, above = got(g_at, R * Y)
    ext[:R] = below.reshape(R, Y, Z)
    ext[R : R + X] = factor[...]
    ext[R + X :] = above.reshape(R, Y, Z)

    def face_moment(block, names):
        return moment_of({q: block[j * Y : (j + 1) * Y] for j, q in enumerate(names)})

    def less(at, vel, moment):
        ext[at] = ext[at] - (vel[0] * moment[0] + vel[1] * moment[1] + vel[2] * moment[2])

    got_low, got_high = got(u_at, 5 * Y)
    own_low, own_high = own(u_at, 5 * Y)
    vel_low, vel_high = got(v_at, 3 * Y)
    less(R - 1, [vel_low[a * Y : (a + 1) * Y] for a in range(3)], face_moment(own_low, PLUS[0]))
    less(R, [flow_ref[a, 0] for a in range(3)], face_moment(got_low, MINUS[0]))
    less(R + X - 1, [flow_ref[a, X - 1] for a in range(3)], face_moment(got_high, PLUS[0]))
    less(R + X, [vel_high[a * Y : (a + 1) * Y] for a in range(3)], face_moment(own_high, MINUS[0]))

    slope = -damping_max * ramp_shape * (1.0 + ramp_shape)
    base = X - 2 * R

    def layer(e, _):
        smooth = filter_rows(lambda k: layers[base + e + k])
        physical, steep, inverse = project(smooth)
        ext[e] = (slope * steep) * (inverse * inverse) * ext[e]

        @pl.when((e >= R) & (e < R + X))
        def _():
            damp[e - R] = (2.0 * damping_max * ramp_shape) * (1.0 - physical) * inverse

        return 0

    lax.fori_loop(0, X + 2 * R, layer, 0, unroll=2)

    def last(x, _):
        result[x] = filter_rows(lambda k: ext[x + k])
        return 0

    lax.fori_loop(0, X, last, 0, unroll=2)
    for n, out in enumerate(outs):

        @pl.when(py == n)
        def _(out=out):
            out[...] = result[:, Y - R :, :]

        @pl.when(py != n)
        def _(out=out):
            out[...] = result[:, :R, :]


def smooth_y(dims, many_y, own, *rest):
    rest = iter(rest)
    y_even, y_odd = refs_of(rest, many_y)
    result, pad = rest
    extend_y(dims, pad, own[...], parity_of("gy"), y_even[...], None if y_odd is None else y_odd[...])

    def store(x, value):
        result[x : x + value.shape[0]] = value

    filter_y(dims, pad, store)


def smooth_z(dims, many_z, weights, own, *rest):
    X, Y, Z = dims
    rest = iter(rest)
    z_even, z_odd = refs_of(rest, many_z)
    (result,) = rest
    value = filter_z(
        weights,
        own[...].reshape(X * Y, Z),
        parity_of("gz"),
        z_even[...].reshape(X * Y, Z),
        None if z_odd is None else z_odd[...].reshape(X * Y, Z),
    )
    result[...] = value.reshape(X, Y, Z)


def collide(dims, many_x, many_y, many_z, step, adj, flow_ref, damp, mask, *rest):
    X, Y, Z = dims
    rest = iter(rest)
    y_even, y_odd = refs_of(rest, many_y)
    z_even, z_odd = refs_of(rest, many_z)
    x_even, x_odd = refs_of(rest, many_x)
    (out,) = rest
    px, py, pz = parity_of("gx"), parity_of("gy"), parity_of("gz")
    pull = Pull(adj, dims, py, y_even, y_odd, pz, z_even, z_odd)
    begin = pl.program_id(0) * step
    u_at = X * Y + R * Y

    def layer(i, _):
        x = begin + i
        around = {c: pull.faces(jnp.clip(x + c, 0, X - 1)) for c in (-1, 0, 1)}
        pulled = []
        for q in range(Q):
            cx = velocity[q][0]
            value = pull.both(q, jnp.clip(x + cx, 0, X - 1), around[cx])
            if cx != 0:
                at = u_at + Y * (PLUS if cx > 0 else MINUS)[0].index(q)
                below, above = sides(
                    px, x_even[at : at + Y, :], None if x_odd is None else x_odd[at : at + Y, :]
                )
                value = jnp.where(x == (X - 1 if cx > 0 else 0), above if cx > 0 else below, value)
            pulled.append(value)
        vel = [flow_ref[a, x] for a in range(3)]
        inverse = flow_ref[3, x]
        speed_sq = vel[0] * vel[0] + vel[1] * vel[1] + vel[2] * vel[2]
        plus = {q: pulled[q] + pulled[q + 1] for q in range(1, Q, 2)}
        minus = {q: pulled[q] - pulled[q + 1] for q in range(1, Q, 2)}
        axes = (1, 3, 5)
        straight = plus[1] + plus[3] + plus[5]
        slanted = plus[7] + plus[9] + plus[11] + plus[13] + plus[15] + plus[17]
        zeroth = (1.0 / 3.0) * pulled[0] + (1.0 / 18.0) * straight + (1.0 / 36.0) * slanted
        first, diagonal = [], []
        for a in range(3):
            terms = [(velocity[q][a], minus[q]) for q in range(7, Q, 2) if velocity[q][a] != 0]
            first.append((1.0 / 18.0) * minus[axes[a]] + (1.0 / 36.0) * signed(terms))
            both = [(1, plus[q]) for q in range(7, Q, 2) if velocity[q][a] != 0]
            diagonal.append((1.0 / 18.0) * plus[axes[a]] + (1.0 / 36.0) * signed(both))
        xy = (1.0 / 36.0) * (plus[7] - plus[9])
        xz = (1.0 / 36.0) * (plus[11] - plus[13])
        yz = (1.0 / 36.0) * (plus[15] - plus[17])
        turned = [
            diagonal[0] * vel[0] + xy * vel[1] + xz * vel[2],
            xy * vel[0] + diagonal[1] * vel[1] + yz * vel[2],
            xz * vel[0] + yz * vel[1] + diagonal[2] * vel[2],
        ]
        quadric = vel[0] * turned[0] + vel[1] * turned[1] + vel[2] * turned[2]
        eq_scalar = zeroth * (1.0 + 1.5 * speed_sq) - 4.5 * quadric
        eq_vector = [3.0 * first[a] + 9.0 * turned[a] - 3.0 * zeroth * vel[a] for a in range(3)]
        label = mask[x]
        drag = damp[x] * inverse
        fluid, solid, inlet = label == 0, label == 1, label == 2
        zero = jnp.zeros_like(drag)
        keep = jnp.where(fluid, 1.0 - relax_rate, zero)
        bounce = jnp.where(solid, 1.0, zero)
        level = jnp.where(fluid, relax_rate * eq_scalar - drag * speed_sq, jnp.where(solid, zero, eq_scalar))
        tilt = [
            jnp.where(fluid, relax_rate * eq_vector[a] + drag * vel[a], jnp.where(inlet, eq_vector[a], zero))
            for a in range(3)
        ]
        out[0, i] = (keep + bounce) * pulled[0] + level
        for q in range(1, Q, 2):
            lean = signed([(velocity[q][a], tilt[a]) for a in range(3) if velocity[q][a] != 0])
            out[q, i] = keep * pulled[q] + bounce * pulled[q + 1] + (level + lean)
            out[q + 1, i] = keep * pulled[q + 1] + bounce * pulled[q] + (level - lean)
        return 0

    lax.fori_loop(0, step, layer, 0)


def local(counts, forward, adjoint, design, mask):
    many_x, many_y, many_z = (int(n > 2) for n in counts)
    nx, ny, nz = counts
    dims = design.shape
    X, Y, Z = dims
    weights = jnp.asarray(band(Z))
    any_space = pl.BlockSpec(memory_space=pl.ANY)
    cells = X * Y * Z
    some = lambda pair: [v for v in pair if v is not None]
    pair = lambda items: (items[0], items[1] if len(items) > 1 else None)
    dma = pltpu.SemaphoreType.DMA

    y_rows = X * R + 5 * X
    to_y = call(
        functools.partial(pack_y, dims, many_y),
        [f32(y_rows, Z)] * (1 + many_y),
        (adjoint, design),
        [any_space] + vmem(1),
        [pltpu.VMEM((1 + many_y, 5, X, R, Z), jnp.float32), dma((1 + many_y, 5))],
        limit=4,
        name="pack_y",
    )
    got_y = some(exchange("gy", ny, *pair(to_y)))

    step = 4
    flow_values = call(
        flow,
        f32(4, X, Y, Z),
        (forward,),
        [pl.BlockSpec((Q, step, Y, Z), lambda i: (0, i, 0, 0))],
        out_specs=pl.BlockSpec((4, step, Y, Z), lambda i: (0, i, 0, 0)),
        grid=(X // step,),
        flops=40 * cells,
        moved=23 * 4 * cells,
        name="flow",
    )

    to_z = call(
        functools.partial(design_y, dims, many_y, many_z),
        [f32(X, Y, Z)] * (2 + many_z),
        (adjoint, design, *got_y),
        [any_space] + vmem(1 + len(got_y)),
        [
            pltpu.VMEM((X, Y + 2 * R, Z), jnp.float32),
            pltpu.VMEM((1 + many_z, 5, X, Y, Z), jnp.float32),
            dma((1 + many_z, 5)),
        ],
        limit=8,
        name="design_y",
    )
    filtered_y = to_z[0]
    got_z = some(exchange("gz", nz, *pair(to_z[1:])))

    x_rows = X * Y + R * Y + 8 * Y
    *to_x, factor = call(
        functools.partial(pack_x, dims, many_x, many_y, many_z),
        [f32(x_rows, Z)] * (1 + many_x) + [f32(X, Y, Z)],
        (adjoint, weights, filtered_y, flow_values, *got_y, *got_z),
        [any_space] + vmem(3 + len(got_y) + len(got_z)),
        [
            pltpu.VMEM((Q, X, Y, Z), jnp.float32),
            pltpu.VMEM((3, X + 2, Y, Z), jnp.float32),
            pltpu.VMEM((3, X + 2, Y, Z), jnp.float32),
            dma((4,)),
        ],
        limit=16,
        name="pack_x",
    )
    got_x = some(exchange("gx", nx, *pair(to_x)))

    result, damp, *to_y = call(
        functools.partial(source, dims, many_x, many_y),
        [f32(X, Y, Z), f32(X, Y, Z)] + [f32(X, R, Z)] * (1 + many_y),
        (factor, flow_values, *to_x, *got_x),
        None,
        [pltpu.VMEM((3 * X, Y, Z), jnp.float32), pltpu.VMEM((X + 2 * R, Y, Z), jnp.float32)],
        limit=8,
        name="source",
    )
    got_y2 = some(exchange("gy", ny, *pair(to_y)))

    whole = pl.BlockSpec(memory_space=pltpu.VMEM)
    adjoint_next = call(
        functools.partial(collide, dims, many_x, many_y, many_z, step),
        f32(Q, X, Y, Z),
        (adjoint, flow_values, damp, mask, *got_y, *got_z, *got_x),
        [whole] * (4 + len(got_y) + len(got_z) + len(got_x)),
        out_specs=pl.BlockSpec((Q, step, Y, Z), lambda i: (0, i, 0, 0)),
        grid=(X // step,),
        limit=16,
        flops=300 * cells,
        moved=44 * 4 * cells,
        name="collide",
    )

    (filtered_xy,) = call(
        functools.partial(smooth_y, dims, many_y),
        [f32(X, Y, Z)],
        (result, *got_y2),
        None,
        [pltpu.VMEM((X, Y + 2 * R, Z), jnp.float32)],
        limit=4,
        name="smooth_y",
    )
    got_z2 = some(exchange("gz", nz, filtered_xy, filtered_xy if many_z else None))
    (sensitivity,) = call(
        functools.partial(smooth_z, dims, many_z),
        [f32(X, Y, Z)],
        (weights, filtered_xy, *got_z2),
        limit=4,
        name="smooth_z",
    )
    return adjoint_next, sensitivity


def solution(mesh):
    counts = tuple(mesh.shape[a] for a in ("gx", "gy", "gz"))
    populations, field = P(None, "gx", "gy", "gz"), P("gx", "gy", "gz")
    return jax.shard_map(
        functools.partial(local, counts),
        mesh=mesh,
        in_specs=(populations, populations, field, field),
        out_specs=(populations, field),
        check_vma=False,
    )
```

time: 112 us -> 40.1 us (0.36)
  starting transfers between devices: 36.3 us -> 7.2 us
  local copies, waits for them, and re-layouts: 29.1 us -> 3.52 us
  other arithmetic: 19.8 us -> 0 us
  Pallas kernels: 0 us -> 10.9 us
  waiting for transfers between devices: 24.4 us -> 17.4 us
    ppermute x18 -> x6, starting transfers between devices: 36.3 us -> 7.2 us  [the longest x5 6.53 us: exchange(): got_even = lax.ppermute(even, axis, pairs + [(b, a) for a, b in pairs])]
    slice x11 -> x0, local copies, waits for them, and re-layouts: 15.2 us -> none  [the longest x8 8.98 us: extended(): lax.slice_in_dim(cells, cells.shape[dim] - width, cells.shape[dim], axis=...]
    pallas_call x0 -> x8, Pallas kernels: none -> 10.9 us  [call(): pl.pallas_call(body, out_shape=outs, in_specs=specs or vmem(len(args)), o...]
    concatenate x7 -> x0, other arithmetic: 10.1 us -> none  [extended(): jnp.concatenate([lax.ppermute(tail, axis, [(i, (i + 1) % count) for i in...]
    ppermute x2 -> x0, local copies, waits for them, and re-layouts: 9.32 us -> none  [the longest x1 5.17 us: extended(): lax.ppermute(head, axis, [((i + 1) % count, i) for i in range(ends)])]
    ppermute x18 -> x6, waiting for transfers between devices: 24.4 us -> 17.4 us  [the longest x5 17.3 us: exchange(): got_even = lax.ppermute(even, axis, pairs + [(b, a) for a, b in pairs])]
    unnamed x18 -> x0, other arithmetic: 5.05 us -> none
    add x5 -> x0, other arithmetic: 3.39 us -> none  [filter_along(): result + weights[k] * lax.slice_in_dim(padded, k, k + length_out, axis=al...]
  transfers between devices with their start and end apart: 18 -> 6, of which waited for: 8 -> 4; matrix products, arithmetic and copies ran while one was open for 18% -> 0% of each run, Pallas kernels for 0% -> 10%
where the time goes in v1:
time: 40.1 us; the launch traced here: 39.8 us
  waiting for transfers between devices  17.4 us (43%)
  Pallas kernels  10.9 us (27%)
  starting transfers between devices  7.2 us (18%)
  local copies, waits for them, and re-layouts  3.52 us (9%)
  between operations  0.74 us (2%)
    ppermute x5, waiting for transfers between devices, exchange(): got_even = lax.ppermute(even, axis, pairs + [(b, a) for a, b in pairs])  17.3 us
    pallas_call x8, Pallas kernels, call(): pl.pallas_call(body, out_shape=outs, in_specs=specs or vmem(len(args)), o...  10.9 us
    ppermute x5, starting transfers between devices, exchange(): got_even = lax.ppermute(even, axis, pairs + [(b, a) for a, b in pairs])  6.53 us
    unnamed x14, local copies, waits for them, and re-layouts  3.52 us
  transfers between devices with their start and end apart: 6, of which 4 were waited for; matrix products, arithmetic and copies ran while one was open for 0% of the time, Pallas kernels for 10%

profile of v1, /device:TPU:0, one launch (start us, length us, event | category | flops | bytes accessed | tf_op | source)
XLA Modules:
  0.0 39.8 jit_solution(1296975252332513341)
XLA Ops:
  0.6 0.0 copy-start
  0.6 1.7 %copy-done = f32[19,16,16,128]{3,2,1,0:T(8,128)S(1)} copy-done((f32[19,16,16,128]{3,2,1,0:T(8,128)S(1)}, f32[19,16,16,128]{3,2,1,0:T(8,128)}, u32[]{:S(2)}) %copy-start) | copy-done | bytes 2490392
  2.3 0.0 copy-start.4
  2.3 0.9 %copy-done.4 = f32[16,16,128]{2,1,0:T(8,128)S(1)} copy-done((f32[16,16,128]{2,1,0:T(8,128)S(1)}, f32[16,16,128]{2,1,0:T(8,128)}, u32[]{:S(2)}) %copy-start.4) | copy-done | bytes 131096
  3.2 0.0 copy-start.1
  3.2 0.0 copy-start.2
  3.2 0.1 pack_y.1
  3.4 0.0 copy-start.3
  3.4 3.0 %collective-permute-start = (f32[208,128]{1,0:T(8,128)S(1)}, f32[208,128]{1,0:T(8,128)S(1)}, u32[]{:S(2)}, u32[]{:S(2)}) collective-permute-start(f32[208,128]{1,0:T(8,128)S(1)} %pack_y.1), channel_id=1, source_target_pairs={{0,2},{2,0},{1,3},{3,1},{4,6},{6,4},{5,7},{7,5},{8,10},{10,8},{9,1... | collective-permute-start | bytes 319496 | tf_op jit(solution)/shard_map/ppermute | solution.py:93
  6.4 3.0 %collective-permute-done.rest_0_ = f32[208,128]{1,0:T(8,128)S(1)} collective-permute-done((f32[208,128]{1,0:T(8,128)S(1)}, f32[208,128]{1,0:T(8,128)S(1)}, u32[]{:S(2)}, u32[]{:S(2)}) %collective-permute-start) | collective-permute-done | bytes 106528 | tf_op jit(solution)/shard_map/ppermute | solution.py:93
  9.4 0.0 copy-done.1
  9.4 0.9 %copy-done.5 = f32[16,16,128]{2,1,0:T(8,128)S(1)} copy-done((f32[16,16,128]{2,1,0:T(8,128)S(1)}, f32[16,16,128]{2,1,0:T(8,128)}, u32[]{:S(2)}) %copy-start.5) | copy-done | bytes 131096
  10.3 1.7 %design_y.1 = (f32[16,16,128]{2,1,0:T(8,128)S(1)}, f32[16,16,128]{2,1,0:T(8,128)S(1)}) custom-call(f32[19,16,16,128]{3,2,1,0:T(8,128)S(1)} %copy-done.1, f32[16,16,128]{2,1,0:T(8,128)S(1)} %copy-done.5, f32[208,128]{1,0:T(8,128)S(1)} %collective-permute-done.rest_0_), custom_call_target="tpu_custom_call" | custom-call | flops 1000000 | bytes 1000000 | tf_op jit(solution)/shard_map/design_y/pallas_call | solution.py:106
  12.0 0.1 collective-permute-start.1
  12.1 0.0 copy-done.2
  12.1 0.5 %flow.1.flow_ref = f32[4,16,16,128]{3,2,1,0:T(8,128)S(1)} custom-call(f32[19,16,16,128]{3,2,1,0:T(8,128)S(1)} %copy-done.2), custom_call_target="tpu_custom_call" | custom-call | flops 1310720 | bytes 3014656 | tf_op jit(solution)/shard_map/flow/pallas_call | solution.py:106
  12.6 0.8 %collective-permute-done.1.rest_1_ = f32[16,16,128]{2,1,0:T(8,128)S(1)} collective-permute-done((f32[16,16,128]{2,1,0:T(8,128)S(1)}, f32[16,16,128]{2,1,0:T(8,128)S(1)}, u32[]{:S(2)}, u32[]{:S(2)}) %collective-permute-start.1) | collective-permute-done | bytes 131104 | tf_op jit(solution)/shard_map/ppermute | solution.py:93
  13.4 0.0 copy-done.3
  13.4 2.6 %pack_x.1 = (f32[512,128]{1,0:T(8,128)S(1)}, f32[512,128]{1,0:T(8,128)S(1)}, f32[16,16,128]{2,1,0:T(8,128)S(1)}) custom-call(f32[19,16,16,128]{3,2,1,0:T(8,128)S(1)} %copy-done.1, f32[3,128,128]{2,1,0:T(8,128)S(1)} %copy-done.3, f32[16,16,128]{2,1,0:T(8,128)S(1)} %get-tuple-element.10.filtered_y, f32[4,16,16,128]{3,2,1,0:T(8,128)S(1)} %flow.1.flow_ref, ...), custom_call_target="tpu_custom_call" | custom-call | flops 1000000 | bytes 1000000 | tf_op jit(solution)/shard_map/pack_x/pallas_call | solution.py:106
  16.0 1.8 %collective-permute-start.2 = (f32[512,128]{1,0:T(8,128)S(1)}, f32[512,128]{1,0:T(8,128)S(1)}, u32[]{:S(2)}, u32[]{:S(2)}) collective-permute-start(f32[512,128]{1,0:T(8,128)S(1)} %get-tuple-element.13.rest_0_), channel_id=1, source_target_pairs={{0,4},{8,12},{16,20},{24,28},{4,0},{12,8},{20,16},{28,24},{1,5},{9... | collective-permute-start | bytes 786440 | tf_op jit(solution)/shard_map/ppermute | solution.py:93
  17.8 0.7 %collective-permute-start.3 = (f32[512,128]{1,0:T(8,128)S(1)}, f32[512,128]{1,0:T(8,128)S(1)}, u32[]{:S(2)}, u32[]{:S(2)}) collective-permute-start(f32[512,128]{1,0:T(8,128)S(1)} %get-tuple-element.14.rest_1_), channel_id=1, source_target_pairs={{4,8},{12,16},{20,24},{8,4},{16,12},{24,20},{5,9},{13,17},{21,25},... | collective-permute-start | bytes 786440 | tf_op jit(solution)/shard_map/ppermute | solution.py:91
  18.5 10.8 %collective-permute-done.2.rest_2_ = f32[512,128]{1,0:T(8,128)S(1)} collective-permute-done((f32[512,128]{1,0:T(8,128)S(1)}, f32[512,128]{1,0:T(8,128)S(1)}, u32[]{:S(2)}, u32[]{:S(2)}) %collective-permute-start.2) | collective-permute-done | bytes 262176 | tf_op jit(solution)/shard_map/ppermute | solution.py:93
  29.3 0.0 collective-permute-done.3.rest_3_
  29.3 1.3 %source.1 = (f32[16,16,128]{2,1,0:T(8,128)S(1)}, f32[16,16,128]{2,1,0:T(8,128)S(1)}, f32[16,8,128]{2,1,0:T(8,128)S(1)}) custom-call(f32[16,16,128]{2,1,0:T(8,128)S(1)} %get-tuple-element.12.factor, f32[4,16,16,128]{3,2,1,0:T(8,128)S(1)} %flow.1.flow_ref, f32[512,128]{1,0:T(8,128)S(1)} %get-tuple-element.13.rest_0_, ...), custom_call_target="tpu_custom_call" | custom-call | flops 1000000 | bytes 1000000 | tf_op jit(solution)/shard_map/source/pallas_call | solution.py:106
  30.6 1.6 %collective-permute-start.4 = (f32[16,8,128]{2,1,0:T(8,128)S(1)}, f32[16,8,128]{2,1,0:T(8,128)S(1)}, u32[]{:S(2)}, u32[]{:S(2)}) collective-permute-start(f32[16,8,128]{2,1,0:T(8,128)S(1)} %get-tuple-element.17), channel_id=1, source_target_pairs={{0,2},{2,0},{1,3},{3,1},{4,6},{6,4},{5,7},{7,5},{8,10},{10,8},{9,1... | collective-permute-start | bytes 196616 | tf_op jit(solution)/shard_map/ppermute | solution.py:93
  32.2 2.8 %collective-permute-done.4.rest_0_ = f32[16,8,128]{2,1,0:T(8,128)S(1)} collective-permute-done((f32[16,8,128]{2,1,0:T(8,128)S(1)}, f32[16,8,128]{2,1,0:T(8,128)S(1)}, u32[]{:S(2)}, u32[]{:S(2)}) %collective-permute-start.4) | collective-permute-done | bytes 65568 | tf_op jit(solution)/shard_map/ppermute | solution.py:93
  35.0 0.1 smooth_y.1.own
  35.1 0.1 collective-permute-start.5
  35.2 0.0 copy-done.6
  35.2 3.5 %collide.1 = f32[19,16,16,128]{3,2,1,0:T(8,128)} custom-call(f32[19,16,16,128]{3,2,1,0:T(8,128)S(1)} %copy-done.1, f32[4,16,16,128]{3,2,1,0:T(8,128)S(1)} %flow.1.flow_ref, f32[16,16,128]{2,1,0:T(8,128)S(1)} %get-tuple-element.15.damp, s32[16,16,128]{2,1,0:T(8,128)S(1)} %copy-done.6, f32[208,128]{1,0:T(8,128)S(1)} %collective-permute-done.rest_0_, ...), custom_call_target="tpu_custom_call" | custom-call | flops 9830400 | bytes 5767168 | tf_op jit(solution)/shard_map/collide/pallas_call | solution.py:106
  38.7 0.0 collective-permute-done.5.rest_0_
  38.7 1.0 %smooth_z.1 = f32[16,16,128]{2,1,0:T(8,128)} custom-call(f32[3,128,128]{2,1,0:T(8,128)S(1)} %copy-done.3, f32[16,16,128]{2,1,0:T(8,128)S(1)} %smooth_y.1.own, f32[16,16,128]{2,1,0:T(8,128)S(1)} %collective-permute-done.5.rest_0_), custom_call_target="tpu_custom_call" | custom-call | flops 1000000 | bytes 1000000 | tf_op jit(solution)/shard_map/smooth_z/pallas_call | solution.py:106
  (2 shorter events, 0.0 us)
Async XLA Ops:
  0.6 1.7 %copy-start = (f32[19,16,16,128]{3,2,1,0:T(8,128)S(1)}, f32[19,16,16,128]{3,2,1,0:T(8,128)}, u32[]{:S(2)}) copy-start(f32[19,16,16,128]{3,2,1,0:T(8,128)} %adj.7) | copy-start | bytes 7471108
  2.3 0.9 %copy-start.4 = (f32[16,16,128]{2,1,0:T(8,128)S(1)}, f32[16,16,128]{2,1,0:T(8,128)}, u32[]{:S(2)}) copy-start(f32[16,16,128]{2,1,0:T(8,128)} %design.3) | copy-start | bytes 393220
  3.2 6.1 %copy-start.1 = (f32[19,16,16,128]{3,2,1,0:T(8,128)S(1)}, f32[19,16,16,128]{3,2,1,0:T(8,128)}, u32[]{:S(2)}) copy-start(f32[19,16,16,128]{3,2,1,0:T(8,128)} %adj.7) | copy-start | bytes 7471108
  3.2 8.8 %copy-start.2 = (f32[19,16,16,128]{3,2,1,0:T(8,128)S(1)}, f32[19,16,16,128]{3,2,1,0:T(8,128)}, u32[]{:S(2)}) copy-start(f32[19,16,16,128]{3,2,1,0:T(8,128)} %forward.1) | copy-start | bytes 7471108
  3.4 10.1 %copy-start.3 = (f32[3,128,128]{2,1,0:T(8,128)S(1)}, f32[3,128,128]{2,1,0:T(8,128)}, u32[]{:S(2)}) copy-start(f32[3,128,128]{2,1,0:T(8,128)} %constant.2.clone.weights) | copy-start | bytes 589828
  3.4 6.0 %collective-permute-start = (f32[208,128]{1,0:T(8,128)S(1)}, f32[208,128]{1,0:T(8,128)S(1)}, u32[]{:S(2)}, u32[]{:S(2)}) collective-permute-start(f32[208,128]{1,0:T(8,128)S(1)} %pack_y.1), channel_id=1, source_target_pairs={{0,2},{2,0},{1,3},{3,1},{4,6},{6,4},{5,7},{7,5},{8,10},{10,8},{9,1... | collective-permute-start | bytes 319496 | tf_op jit(solution)/shard_map/ppermute | solution.py:93
  9.4 0.9 %copy-start.5 = (f32[16,16,128]{2,1,0:T(8,128)S(1)}, f32[16,16,128]{2,1,0:T(8,128)}, u32[]{:S(2)}) copy-start(f32[16,16,128]{2,1,0:T(8,128)} %design.3) | copy-start | bytes 393220
  12.0 1.4 %collective-permute-start.1 = (f32[16,16,128]{2,1,0:T(8,128)S(1)}, f32[16,16,128]{2,1,0:T(8,128)S(1)}, u32[]{:S(2)}, u32[]{:S(2)}) collective-permute-start(f32[16,16,128]{2,1,0:T(8,128)S(1)} %get-tuple-element.11), channel_id=1, source_target_pairs={{0,1},{1,0},{2,3},{3,2},{4,5},{5,4},{6,7},{7,6},{8,9},{9,8},{10,11... | collective-permute-start | bytes 393224 | tf_op jit(solution)/shard_map/ppermute | solution.py:93
  13.4 21.8 %copy-start.6 = (s32[16,16,128]{2,1,0:T(8,128)S(1)}, s32[16,16,128]{2,1,0:T(8,128)}, u32[]{:S(2)}) copy-start(s32[16,16,128]{2,1,0:T(8,128)} %mask.1) | copy-start | bytes 393220
  16.0 13.3 %collective-permute-start.2 = (f32[512,128]{1,0:T(8,128)S(1)}, f32[512,128]{1,0:T(8,128)S(1)}, u32[]{:S(2)}, u32[]{:S(2)}) collective-permute-start(f32[512,128]{1,0:T(8,128)S(1)} %get-tuple-element.13.rest_0_), channel_id=1, source_target_pairs={{0,4},{8,12},{16,20},{24,28},{4,0},{12,8},{20,16},{28,24},{1,5},{9... | collective-permute-start | bytes 786440 | tf_op jit(solution)/shard_map/ppermute | solution.py:93
  17.8 11.5 %collective-permute-start.3 = (f32[512,128]{1,0:T(8,128)S(1)}, f32[512,128]{1,0:T(8,128)S(1)}, u32[]{:S(2)}, u32[]{:S(2)}) collective-permute-start(f32[512,128]{1,0:T(8,128)S(1)} %get-tuple-element.14.rest_1_), channel_id=1, source_target_pairs={{4,8},{12,16},{20,24},{8,4},{16,12},{24,20},{5,9},{13,17},{21,25},... | collective-permute-start | bytes 786440 | tf_op jit(solution)/shard_map/ppermute | solution.py:91
  30.6 4.3 %collective-permute-start.4 = (f32[16,8,128]{2,1,0:T(8,128)S(1)}, f32[16,8,128]{2,1,0:T(8,128)S(1)}, u32[]{:S(2)}, u32[]{:S(2)}) collective-permute-start(f32[16,8,128]{2,1,0:T(8,128)S(1)} %get-tuple-element.17), channel_id=1, source_target_pairs={{0,2},{2,0},{1,3},{3,1},{4,6},{6,4},{5,7},{7,5},{8,10},{10,8},{9,1... | collective-permute-start | bytes 196616 | tf_op jit(solution)/shard_map/ppermute | solution.py:93
  35.1 3.6 %collective-permute-start.5 = (f32[16,16,128]{2,1,0:T(8,128)S(1)}, f32[16,16,128]{2,1,0:T(8,128)S(1)}, u32[]{:S(2)}, u32[]{:S(2)}) collective-permute-start(f32[16,16,128]{2,1,0:T(8,128)S(1)} %smooth_y.1.own), channel_id=1, source_target_pairs={{0,1},{1,0},{2,3},{3,2},{4,5},{5,4},{6,7},{7,6},{8,9},{9,8},{10,11... | collective-permute-start | bytes 393224 | tf_op jit(solution)/shard_map/ppermute | solution.py:93

commit v2 on v1

--- a/solution.py
+++ b/solution.py
@@ -98,6 +98,10 @@
     return [pl.BlockSpec(memory_space=pltpu.VMEM)] * count
 
 
+def in_hbm(array):
+    return pltpu.with_memory_space_constraint(array, pltpu.HBM)
+
+
 def f32(*shape):
     return jax.ShapeDtypeStruct(shape, jnp.float32)
 
@@ -182,52 +186,134 @@
 def pack_y(dims, many, adj, design, *rest):
     X, Y, Z = dims
     outs = rest[: 1 + many]
-    tiles, sems = rest[1 + many :]
+    kept, tiles, sems, kept_sem = rest[1 + many :]
     py = parity_of("gy")
-
-    def fill(n, out, up):
+    keep = pltpu.make_async_copy(design, kept, kept_sem)
+    keep.start()
+
+    def copies(n, up):
         names = (MINUS if up else PLUS)[1]
         first = Y - R if up else 0
-        copies = [
+        return [
             pltpu.make_async_copy(adj.at[q, :, pl.ds(first, R), :], tiles.at[n, j], sems.at[n, j])
             for j, q in enumerate(names)
         ]
-        for c in copies:
+
+    def start(n, out, up):
+        for c in copies(n, up):
             c.start()
-        out[: X * R, :] = design[:, first : first + R, :].reshape(X * R, Z)
-        for c in copies:
+
+    def fill(n, out, up):
+        first = Y - R if up else 0
+        out[: X * R, :] = kept[:, first : first + R, :].reshape(X * R, Z)
+        for c in copies(n, up):
             c.wait()
         for j in range(5):
             out[X * R + X * j : X * R + X * (j + 1), :] = tiles[n, j, :, R - 1 if up else 0, :]
 
+    def each(act):
+        for n, out in enumerate(outs):
+            pl.when(py == n)(functools.partial(act, n, out, True))
+            pl.when(py != n)(functools.partial(act, n, out, False))
+
+    each(start)
+    keep.wait()
+    each(fill)
+
+
+def prepare(dims, many_z, ahead, forward, adj, *rest):
+    X, Y, Z = dims
+    rest = iter(rest)
+    flow_ref, factor = next(rest), next(rest)
+    outs = [next(rest) for _ in range(1 + many_z)]
+    rising, falling, members_ref, sems = rest
+    pz = parity_of("gz")
+    part = X // 4
+    copies = [
+        pltpu.make_async_copy(
+            forward.at[:, pl.ds(i * part, part)], members_ref.at[:, pl.ds(i * part, part)], sems.at[i]
+        )
+        for i in range(4)
+    ]
+    for c in copies:
+        c.start()
+    row = lax.broadcasted_iota(jnp.int32, (Y, Z), 0)
+    lane = lax.broadcasted_iota(jnp.int32, (Y, Z), 1)
+    zero = jnp.zeros((Y, Z), jnp.float32)
+
+    def along_y(q, x):
+        here, cy = adj[q, x], velocity[q][1]
+        if cy == 0:
+            return here
+        return jnp.where(row == (Y - 1 if cy > 0 else 0), zero, pltpu.roll(here, (-cy) % Y, 0))
+
+    def both(q, x):
+        here, cz = along_y(q, x), velocity[q][2]
+        if cz == 0:
+            return here
+        return jnp.where(lane == (Z - 1 if cz > 0 else 0), zero, pltpu.roll(here, (-cz) % Z, 1))
+
+    def layer(x, _):
+        members = [members_ref[q, x] for q in range(Q)]
+        inverse = 1.0 / sum(members[1:], members[0])
+        vel = [
+            signed([(velocity[q][a], members[q] - members[q + 1]) for q in range(1, Q, 2) if velocity[q][a] != 0])
+            * inverse
+            for a in range(3)
+        ]
+        for a in range(3):
+            flow_ref[a, x] = vel[a]
+        flow_ref[3, x] = inverse
+        groups = {}
+        for q in range(1, Q):
+            groups.setdefault(velocity[q][0], {})[q] = both(q, x)
+        level, up, down = moment_of(groups[0]), moment_of(groups[1]), moment_of(groups[-1])
+        for a in range(3):
+            rising[a, x] = up[a]
+            falling[a, x + 2] = down[a]
+        factor[x] = vel[0] * vel[0] + vel[1] * vel[1] + vel[2] * vel[2] - vel[1] * level[1] - vel[2] * level[2]
+        return 0
+
+    for a in range(3):
+        rising[a, X] = zero
+        falling[a, 1] = zero
+    for i, c in enumerate(copies):
+        c.wait()
+        lax.fori_loop(i * part, (i + 1) * part, layer, 0)
+
+    def finish(x, _):
+        total = factor[x]
+        for a in range(3):
+            total = total - flow_ref[a, x] * (rising[a, x + 1] + falling[a, x + 1])
+        factor[x] = total
+        return 0
+
+    lax.fori_loop(0, X, finish, 0, unroll=4)
+
+    def fill(out, up):
+        names = (MINUS if up else PLUS)[2]
+
+        def face(x, _):
+            value = zero
+            for j, q in enumerate(names):
+                slot = slot_of(Z, up, j)
+                value = jnp.where(lane == slot, pltpu.roll(along_y(q, x), shift_of(Z, up, j), 1), value)
+            out[x] = value
+            return 0
+
+        lax.fori_loop(0, X, face, 0, unroll=2)
+
     for n, out in enumerate(outs):
-
-        @pl.when(py == n)
-        def _(n=n, out=out):
-            fill(n, out, True)
-
-        @pl.when(py != n)
-        def _(n=n, out=out):
-            fill(n, out, False)
-
-
-def flow(forward, out):
-    members = [forward[q] for q in range(Q)]
-    rho = members[0]
-    for q in range(1, Q):
-        rho = rho + members[q]
-    inverse = 1.0 / rho
-    for a in range(3):
-        total = None
-        for q in range(1, Q, 2):
-            c = velocity[q][a]
-            if c == 0:
-                continue
-            term = members[q] - members[q + 1]
-            term = term if c > 0 else -term
-            total = term if total is None else total + term
-        out[a] = total * inverse
-    out[3] = inverse
+        pl.when(pz == n)(functools.partial(fill, out, True))
+        pl.when(pz != n)(functools.partial(fill, out, False))
+
+
+def slot_of(Z, up, j):
+    return j if up else Z - 5 + j
+
+
+def shift_of(Z, up, j):
+    return (slot_of(Z, up, j) - (Z - 1 if up else 0)) % Z
 
 
 def extend_y(dims, pad, own, py, even, odd):
@@ -244,34 +330,17 @@
         store(x, filter_rows(lambda k: pad[x : x + step, k : k + Y, :]))
 
 
-def design_y(dims, many_y, many_z, adj, design, *rest):
+def design_y(dims, many_y, many_z, design, *rest):
     X, Y, Z = dims
     rest = iter(rest)
+    faces = [next(rest) for _ in range(1 + many_z)]
     y_even, y_odd = refs_of(rest, many_y)
     filtered = next(rest)
     outs = [next(rest) for _ in range(1 + many_z)]
-    pad, held, sems = rest
+    pad, edges = rest
     pz = parity_of("gz")
     py = parity_of("gy")
 
-    def fetch(up, n):
-        names = (MINUS if up else PLUS)[2]
-        return [
-            pltpu.make_async_copy(adj.at[q], held.at[n, j], sems.at[n, j]) for j, q in enumerate(names)
-        ]
-
-    for n, out in enumerate(outs):
-
-        @pl.when(pz == n)
-        def _(n=n):
-            for c in fetch(True, n):
-                c.start()
-
-        @pl.when(pz != n)
-        def _(n=n):
-            for c in fetch(False, n):
-                c.start()
-
     def halo(ref):
         return ref[: X * R, :].reshape(X, R, Z)
 
@@ -281,39 +350,36 @@
         filtered[x : x + value.shape[0]] = value
 
     filter_y(dims, pad, store)
-
-    def fill(out, up, n):
+    row = lax.broadcasted_iota(jnp.int32, (Y, Z), 0)
+    lane = lax.broadcasted_iota(jnp.int32, (Y, Z), 1)
+
+    def fill(out, face, up):
         names = (MINUS if up else PLUS)[2]
-        for c in fetch(up, n):
-            c.wait()
-        by_name = {q: held.at[n, j] for j, q in enumerate(names)}
-
-        class Held:
-            def __getitem__(self, at):
-                return by_name[at[0]][at[1]]
-
-        pull = Pull(Held(), dims, py, y_even, y_odd)
+        slanted = [(j, q) for j, q in enumerate(names) if velocity[q][1] != 0]
+        for i, (j, q) in enumerate(slanted):
+            edges[i] = pltpu.roll(rows_of(dims, py, y_even, y_odd, q), shift_of(Z, up, j), 1)
+        first, last = slot_of(Z, up, 0), slot_of(Z, up, 4)
 
         def layer(x, _):
-            value = filtered[x]
-            for j, q in enumerate(names):
-                slot = j if up else Z - 5 + j
-                shift = (slot - (Z - 1 if up else 0)) % Z
-                value = jnp.where(pull.lane == slot, pltpu.roll(pull.along_y(q, x), shift, 1), value)
+            value = jnp.where((lane >= first) & (lane <= last), face[x], filtered[x])
+            for i, (j, q) in enumerate(slanted):
+                at = (row == (Y - 1 if velocity[q][1] > 0 else 0)) & (lane == slot_of(Z, up, j))
+                value = jnp.where(at, edges[i, pl.ds(x, 1), :], value)
             out[x] = value
             return 0
 
-        lax.fori_loop(0, X, layer, 0, unroll=2)
-
-    for n, out in enumerate(outs):
-
-        @pl.when(pz == n)
-        def _(n=n, out=out):
-            fill(out, True, n)
-
-        @pl.when(pz != n)
-        def _(n=n, out=out):
-            fill(out, False, n)
+        lax.fori_loop(0, X, layer, 0, unroll=4)
+
+    for n, (out, face) in enumerate(zip(outs, faces)):
+        pl.when(pz == n)(functools.partial(fill, out, face, True))
+        pl.when(pz != n)(functools.partial(fill, out, face, False))
+
+
+def rows_of(dims, py, even, odd, q):
+    X, Y, Z = dims
+    above = velocity[q][1] > 0
+    at = X * R + X * (PLUS if above else MINUS)[1].index(q)
+    return sides(py, even[at : at + X, :], None if odd is None else odd[at : at + X, :])[int(above)]
 
 
 def signed(terms):
@@ -330,73 +396,90 @@
     ]
 
 
-def filter_z(weights, own, pz, even, odd):
-    value = dot(own, weights[0]) + dot(even, jnp.where(pz == 0, weights[2], weights[1]))
+def halo_z(weights, pz, even, odd):
+    value = dot(even, jnp.where(pz == 0, weights[2], weights[1]))
     if odd is not None:
         value = value + dot(odd, jnp.where(pz == 0, weights[1], weights[2]))
     return value
 
 
-def pack_x(dims, many_x, many_y, many_z, adj, weights, filtered_y, flow_ref, *rest):
+def flat(dims, ref):
+    X, Y, Z = dims
+    return None if ref is None else ref[...].reshape(X * Y, Z)
+
+
+def own_z(dims, weights, field, out):
+    out[...] = dot(flat(dims, field), weights[0])
+
+
+def factor_y(dims, many_y, weights, filtered_y, flow_ref, factor, *rest):
+    X, Y, Z = dims
+    rest = iter(rest)
+    y_even, y_odd = refs_of(rest, many_y)
+    smooth, out = rest
+    smooth[...] = dot(flat(dims, filtered_y), weights[0])
+    out[...] = factor[...]
+    py = parity_of("gy")
+    row = lax.broadcasted_iota(jnp.int32, (X, Z), 0)
+    lane = lax.broadcasted_iota(jnp.int32, (X, Z), 1)
+    for edge, names in ((0, MINUS[1]), (Y - 1, PLUS[1])):
+        values = {}
+        for q in names:
+            value = rows_of(dims, py, y_even, y_odd, q)
+            cx, _, cz = velocity[q]
+            if cx != 0:
+                value = jnp.where(row == (X - 1 if cx > 0 else 0), 0.0, pltpu.roll(value, (-cx) % X, 0))
+            if cz != 0:
+                value = jnp.where(lane == (Z - 1 if cz > 0 else 0), 0.0, pltpu.roll(value, (-cz) % Z, 1))
+            values[q] = value
+        moment = moment_of(values)
+        total = factor[:, edge, :]
+        for a in range(3):
+            total = total - flow_ref[a, :, edge, :] * moment[a]
+        out[:, edge, :] = total
+
+
+def pack_x(dims, many_x, many_y, many_z, adj, weights, smooth, factor_in, flow_ref, *rest):
     X, Y, Z = dims
     rest = iter(rest)
     y_even, y_odd = refs_of(rest, many_y)
     z_even, z_odd = refs_of(rest, many_z)
     outs = [next(rest) for _ in range(1 + many_x)]
-    factor = next(rest)
-    local, rising, falling, sems = rest
+    (factor,) = rest
     px, py, pz = parity_of("gx"), parity_of("gy"), parity_of("gz")
-    part = X // 4
-    copies = [
-        pltpu.make_async_copy(
-            adj.at[:, pl.ds(i * part, part)], local.at[:, pl.ds(i * part, part)], sems.at[i]
-        )
-        for i in range(4)
-    ]
-    for c in copies:
-        c.start()
-    smooth = filter_z(
-        weights,
-        filtered_y[...].reshape(X * Y, Z),
-        pz,
-        z_even[...].reshape(X * Y, Z),
-        None if z_odd is None else z_odd[...].reshape(X * Y, Z),
-    )
+    value = smooth[...] + halo_z(weights, pz, flat(dims, z_even), flat(dims, z_odd))
     for out in outs:
-        out[: X * Y, :] = smooth
-    pull = Pull(local, dims, py, y_even, y_odd, pz, z_even, z_odd)
-
-    def layer(x, _):
-        faces = pull.faces(x)
-        groups = {}
-        for q in range(1, Q):
-            groups.setdefault(velocity[q][0], {})[q] = pull.both(q, x, faces)
-        level = moment_of(groups[0])
-        up = moment_of(groups[1])
-        down = moment_of(groups[-1])
-        for a in range(3):
-            rising[a, x] = up[a]
-            falling[a, x + 2] = down[a]
-        vel = [flow_ref[a, x] for a in range(3)]
-        factor[x] = vel[0] * vel[0] + vel[1] * vel[1] + vel[2] * vel[2] - vel[1] * level[1] - vel[2] * level[2]
-        return 0
-
-    zero = jnp.zeros((Y, Z), jnp.float32)
-    for a in range(3):
-        rising[a, X] = zero
-        falling[a, 1] = zero
-    for i, c in enumerate(copies):
-        c.wait()
-        lax.fori_loop(i * part, (i + 1) * part, layer, 0)
-
-    def finish(x, _):
-        total = factor[x]
-        for a in range(3):
-            total = total - flow_ref[a, x] * (rising[a, x + 1] + falling[a, x + 1])
-        factor[x] = total
-        return 0
-
-    lax.fori_loop(0, X, finish, 0, unroll=4)
+        out[: X * Y, :] = value
+    lane = lax.broadcasted_iota(jnp.int32, (Y, Z), 1)
+    factor[...] = factor_in[...]
+
+    def correct(ref, above):
+        names = (PLUS if above else MINUS)[2]
+        edge = Z - 1 if above else 0
+        zero = jnp.zeros((Y, Z), jnp.float32)
+
+        def layer(x, _):
+            values = {}
+            for j, q in enumerate(names):
+                cx = velocity[q][0]
+                face = ref[jnp.clip(x + cx, 0, X - 1)] if cx else ref[x]
+                shift = (edge - slot_of(Z, not above, j)) % Z
+                face = pltpu.roll(face, shift, 1) if shift else face
+                if cx != 0:
+                    face = jnp.where(x == (X - 1 if cx > 0 else 0), zero, face)
+                values[q] = face
+            moment = moment_of(values)
+            change = flow_ref[0, x] * moment[0] + flow_ref[1, x] * moment[1] + flow_ref[2, x] * moment[2]
+            factor[x] = factor[x] - jnp.where(lane == edge, change, zero)
+            return 0
+
+        lax.fori_loop(0, X, layer, 0, unroll=4)
+
+    for n, ref in enumerate([z_even, z_odd][: 1 + many_z]):
+        pl.when(pz == n)(functools.partial(correct, ref, True))
+        pl.when(pz != n)(functools.partial(correct, ref, False))
+
+    pull = Pull(adj, dims, py, y_even, y_odd, pz, z_even, z_odd)
 
     def fill(out, up):
         names = (MINUS if up else PLUS)[0]
@@ -414,14 +497,8 @@
             at += Y
 
     for n, out in enumerate(outs):
-
-        @pl.when(px == n)
-        def _(out=out):
-            fill(out, True)
-
-        @pl.when(px != n)
-        def _(out=out):
-            fill(out, False)
+        pl.when(px == n)(functools.partial(fill, out, True))
+        pl.when(px != n)(functools.partial(fill, out, False))
 
 
 def project(filtered):
@@ -490,13 +567,13 @@
 
         return 0
 
-    lax.fori_loop(0, X + 2 * R, layer, 0, unroll=2)
+    lax.fori_loop(0, X + 2 * R, layer, 0, unroll=4)
 
     def last(x, _):
         result[x] = filter_rows(lambda k: ext[x + k])
         return 0
 
-    lax.fori_loop(0, X, last, 0, unroll=2)
+    lax.fori_loop(0, X, last, 0, unroll=4)
     for n, out in enumerate(outs):
 
         @pl.when(py == n)
@@ -508,7 +585,7 @@
             out[...] = result[:, :R, :]
 
 
-def smooth_y(dims, many_y, own, *rest):
+def smooth_y(dims, many_y, ahead, own, *rest):
     rest = iter(rest)
     y_even, y_odd = refs_of(rest, many_y)
     result, pad = rest
@@ -521,18 +598,11 @@
 
 
 def smooth_z(dims, many_z, weights, own, *rest):
-    X, Y, Z = dims
     rest = iter(rest)
     z_even, z_odd = refs_of(rest, many_z)
     (result,) = rest
-    value = filter_z(
-        weights,
-        own[...].reshape(X * Y, Z),
-        parity_of("gz"),
-        z_even[...].reshape(X * Y, Z),
-        None if z_odd is None else z_odd[...].reshape(X * Y, Z),
-    )
-    result[...] = value.reshape(X, Y, Z)
+    value = own[...] + halo_z(weights, parity_of("gz"), flat(dims, z_even), flat(dims, z_odd))
+    result[...] = value.reshape(dims)
 
 
 def collide(dims, many_x, many_y, many_z, step, adj, flow_ref, damp, mask, *rest):
@@ -614,65 +684,61 @@
     dims = design.shape
     X, Y, Z = dims
     weights = jnp.asarray(band(Z))
-    any_space = pl.BlockSpec(memory_space=pl.ANY)
+    hbm = pl.BlockSpec(memory_space=pltpu.HBM)
     cells = X * Y * Z
     some = lambda pair: [v for v in pair if v is not None]
     pair = lambda items: (items[0], items[1] if len(items) > 1 else None)
     dma = pltpu.SemaphoreType.DMA
 
     y_rows = X * R + 5 * X
-    to_y = call(
+    *to_y, design = call(
         functools.partial(pack_y, dims, many_y),
-        [f32(y_rows, Z)] * (1 + many_y),
-        (adjoint, design),
-        [any_space] + vmem(1),
-        [pltpu.VMEM((1 + many_y, 5, X, R, Z), jnp.float32), dma((1 + many_y, 5))],
+        [f32(y_rows, Z)] * (1 + many_y) + [f32(X, Y, Z)],
+        (in_hbm(adjoint), in_hbm(design)),
+        [hbm, hbm],
+        [pltpu.VMEM((1 + many_y, 5, X, R, Z), jnp.float32), dma((1 + many_y, 5)), dma],
         limit=4,
         name="pack_y",
     )
     got_y = some(exchange("gy", ny, *pair(to_y)))
 
-    step = 4
-    flow_values = call(
-        flow,
-        f32(4, X, Y, Z),
-        (forward,),
-        [pl.BlockSpec((Q, step, Y, Z), lambda i: (0, i, 0, 0))],
-        out_specs=pl.BlockSpec((4, step, Y, Z), lambda i: (0, i, 0, 0)),
-        grid=(X // step,),
-        flops=40 * cells,
-        moved=23 * 4 * cells,
-        name="flow",
-    )
-
-    to_z = call(
+    flow_values, factor, *faces = call(
+        functools.partial(prepare, dims, many_z),
+        [f32(4, X, Y, Z)] + [f32(X, Y, Z)] * (2 + many_z),
+        (to_y[0], in_hbm(forward), adjoint),
+        vmem(1) + [hbm] + vmem(1),
+        [pltpu.VMEM((3, X + 2, Y, Z), jnp.float32)] * 2 + [pltpu.VMEM((Q, X, Y, Z), jnp.float32), dma((4,))],
+        limit=16,
+        flops=200 * cells,
+        moved=44 * 4 * cells,
+        name="prepare",
+    )
+
+    filtered_y, *to_z = call(
         functools.partial(design_y, dims, many_y, many_z),
         [f32(X, Y, Z)] * (2 + many_z),
-        (adjoint, design, *got_y),
-        [any_space] + vmem(1 + len(got_y)),
-        [
-            pltpu.VMEM((X, Y + 2 * R, Z), jnp.float32),
-            pltpu.VMEM((1 + many_z, 5, X, Y, Z), jnp.float32),
-            dma((1 + many_z, 5)),
-        ],
+        (design, *faces, *got_y),
+        None,
+        [pltpu.VMEM((X, Y + 2 * R, Z), jnp.float32), pltpu.VMEM((2, X, Z), jnp.float32)],
         limit=8,
         name="design_y",
     )
-    filtered_y = to_z[0]
-    got_z = some(exchange("gz", nz, *pair(to_z[1:])))
+    got_z = some(exchange("gz", nz, *pair(to_z)))
+
+    smooth, factor = call(
+        functools.partial(factor_y, dims, many_y),
+        [f32(X * Y, Z), f32(X, Y, Z)],
+        (weights, filtered_y, flow_values, factor, *got_y),
+        limit=8,
+        flops=200 * cells,
+        name="factor_y",
+    )
 
     x_rows = X * Y + R * Y + 8 * Y
     *to_x, factor = call(
         functools.partial(pack_x, dims, many_x, many_y, many_z),
         [f32(x_rows, Z)] * (1 + many_x) + [f32(X, Y, Z)],
-        (adjoint, weights, filtered_y, flow_values, *got_y, *got_z),
-        [any_space] + vmem(3 + len(got_y) + len(got_z)),
-        [
-            pltpu.VMEM((Q, X, Y, Z), jnp.float32),
-            pltpu.VMEM((3, X + 2, Y, Z), jnp.float32),
-            pltpu.VMEM((3, X + 2, Y, Z), jnp.float32),
-            dma((4,)),
-        ],
+        (adjoint, weights, smooth, factor, flow_values, *got_y, *got_z),
         limit=16,
         name="pack_x",
     )
@@ -689,6 +755,7 @@
     )
     got_y2 = some(exchange("gy", ny, *pair(to_y)))
 
+    step = 4
     whole = pl.BlockSpec(memory_space=pltpu.VMEM)
     adjoint_next = call(
         functools.partial(collide, dims, many_x, many_y, many_z, step),
@@ -706,17 +773,25 @@
     (filtered_xy,) = call(
         functools.partial(smooth_y, dims, many_y),
         [f32(X, Y, Z)],
-        (result, *got_y2),
-        None,
+        (in_hbm(adjoint_next), result, *got_y2),
+        [hbm] + vmem(1 + len(got_y2)),
         [pltpu.VMEM((X, Y + 2 * R, Z), jnp.float32)],
         limit=4,
         name="smooth_y",
     )
     got_z2 = some(exchange("gz", nz, filtered_xy, filtered_xy if many_z else None))
+    (own,) = call(
+        functools.partial(own_z, dims),
+        [f32(X * Y, Z)],
+        (weights, filtered_xy),
+        limit=4,
+        flops=200 * cells,
+        name="own_z",
+    )
     (sensitivity,) = call(
         functools.partial(smooth_z, dims, many_z),
         [f32(X, Y, Z)],
-        (weights, filtered_xy, *got_z2),
+        (weights, own, *got_z2),
         limit=4,
         name="smooth_z",
     )

time: 40.1 us -> 32.7 us (0.82)
  waiting for transfers between devices: 17.4 us -> 13 us
  local copies, waits for them, and re-layouts: 3.52 us -> 0.01 us
  Pallas kernels: 10.9 us -> 12.1 us
  starting transfers between devices: 7.2 us -> 6.75 us
    ppermute x5, waiting for transfers between devices: 17.3 us -> 12.9 us  [exchange(): got_even = lax.ppermute(even, axis, pairs + [(b, a) for a, b in pairs])]
    unnamed x14 -> x6, local copies, waits for them, and re-layouts: 3.52 us -> 0.01 us
    pallas_call x8 -> x10, Pallas kernels: 10.9 us -> 12.1 us  [call(): pl.pallas_call(body, out_shape=outs, in_specs=specs or vmem(len(args)), o...]
    ppermute x5, starting transfers between devices: 6.53 us -> 6.08 us  [exchange(): got_even = lax.ppermute(even, axis, pairs + [(b, a) for a, b in pairs])]
  transfers between devices with their start and end apart: 6 -> 6, of which waited for: 4 -> 3; matrix products, arithmetic and copies ran while one was open for 0% -> 0% of each run, Pallas kernels for 10% -> 23%
where the time goes in v2:
time: 32.7 us; the launch traced here: 32.6 us
  waiting for transfers between devices  13 us (40%)
  Pallas kernels  12.1 us (37%)
  starting transfers between devices  6.75 us (21%)
  between operations  0.75 us (2%)
    ppermute x5, waiting for transfers between devices, exchange(): got_even = lax.ppermute(even, axis, pairs + [(b, a) for a, b in pairs])  12.9 us
    pallas_call x10, Pallas kernels, call(): pl.pallas_call(body, out_shape=outs, in_specs=specs or vmem(len(args)), o...  12.1 us
    ppermute x5, starting transfers between devices, exchange(): got_even = lax.ppermute(even, axis, pairs + [(b, a) for a, b in pairs])  6.08 us
    ppermute x1, starting transfers between devices, exchange(): got_odd = lax.ppermute(odd, axis, pairs + [(b, a) for a, b in pairs])  0.67 us
  transfers between devices with their start and end apart: 6, of which 3 were waited for; matrix products, arithmetic and copies ran while one was open for 0% of the time, Pallas kernels for 23%

profile of v2, /device:TPU:0, one launch (start us, length us, event | category | flops | bytes accessed | tf_op | source)
XLA Modules:
  0.0 32.6 jit_solution(582905761114250928)
XLA Ops:
  0.6 0.0 copy-start
  0.6 1.3 %pack_y.1 = (f32[208,128]{1,0:T(8,128)S(1)}, f32[16,16,128]{2,1,0:T(8,128)S(1)}) custom-call(f32[19,16,16,128]{3,2,1,0:T(8,128)} %adj.7, f32[16,16,128]{2,1,0:T(8,128)} %design.1), custom_call_target="tpu_custom_call" | custom-call | flops 1000000 | bytes 1000000 | tf_op jit(solution)/shard_map/pack_y/pallas_call | solution.py:110
  1.9 0.0 copy-start.1
  1.9 3.0 %collective-permute-start = (f32[208,128]{1,0:T(8,128)S(1)}, f32[208,128]{1,0:T(8,128)S(1)}, u32[]{:S(2)}, u32[]{:S(2)}) collective-permute-start(f32[208,128]{1,0:T(8,128)S(1)} %get-tuple-element.17.ahead), channel_id=1, source_target_pairs={{0,2},{2,0},{1,3},{3,1},{4,6},{6,4},{5,7},{7,5},{8,10},{10,8},{9,1... | collective-permute-start | bytes 319496 | tf_op jit(solution)/shard_map/ppermute | solution.py:93
  5.0 0.0 copy-done
  5.0 3.4 %prepare.1 = (f32[4,16,16,128]{3,2,1,0:T(8,128)S(1)}, f32[16,16,128]{2,1,0:T(8,128)S(1)}, f32[16,16,128]{2,1,0:T(8,128)S(1)}) custom-call(f32[208,128]{1,0:T(8,128)S(1)} %get-tuple-element.17.ahead, f32[19,16,16,128]{3,2,1,0:T(8,128)} %forward.1, f32[19,16,16,128]{3,2,1,0:T(8,128)S(1)} %copy-done), custom_call_target="tpu_custom_call" | custom-call | flops 6553600 | bytes 5767168 | tf_op jit(solution)/shard_map/prepare/pallas_call | solution.py:110
  8.3 0.0 collective-permute-done.rest_1_.rest_0_
  8.3 0.2 design_y.1
  8.6 0.1 collective-permute-start.1
  8.7 0.0 copy-done.1
  8.7 0.3 factor_y.1
  8.9 1.1 %collective-permute-done.1.rest_1_ = f32[16,16,128]{2,1,0:T(8,128)S(1)} collective-permute-done((f32[16,16,128]{2,1,0:T(8,128)S(1)}, f32[16,16,128]{2,1,0:T(8,128)S(1)}, u32[]{:S(2)}, u32[]{:S(2)}) %collective-permute-start.1) | collective-permute-done | bytes 131104 | tf_op jit(solution)/shard_map/ppermute | solution.py:93
  10.0 0.0 copy-start.2
  10.0 0.9 %pack_x.1 = (f32[512,128]{1,0:T(8,128)S(1)}, f32[512,128]{1,0:T(8,128)S(1)}, f32[16,16,128]{2,1,0:T(8,128)S(1)}) custom-call(f32[19,16,16,128]{3,2,1,0:T(8,128)S(1)} %copy-done, f32[3,128,128]{2,1,0:T(8,128)S(1)} %copy-done.1, f32[256,128]{1,0:T(8,128)S(1)} %get-tuple-element.23.smooth, f32[16,16,128]{2,1,0:T(8,128)S(1)} %get-tuple-element.24.factor_in, ...), custom_call_target="tpu_custom_call" | custom-call | flops 1000000 | bytes 1000000 | tf_op jit(solution)/shard_map/pack_x/pallas_call | solution.py:110
  10.9 1.5 %collective-permute-start.2 = (f32[512,128]{1,0:T(8,128)S(1)}, f32[512,128]{1,0:T(8,128)S(1)}, u32[]{:S(2)}, u32[]{:S(2)}) collective-permute-start(f32[512,128]{1,0:T(8,128)S(1)} %get-tuple-element.27.rest_0_), channel_id=1, source_target_pairs={{0,4},{8,12},{16,20},{24,28},{4,0},{12,8},{20,16},{28,24},{1,5},{9... | collective-permute-start | bytes 786440 | tf_op jit(solution)/shard_map/ppermute | solution.py:93
  12.4 0.7 %collective-permute-start.3 = (f32[512,128]{1,0:T(8,128)S(1)}, f32[512,128]{1,0:T(8,128)S(1)}, u32[]{:S(2)}, u32[]{:S(2)}) collective-permute-start(f32[512,128]{1,0:T(8,128)S(1)} %get-tuple-element.28.rest_1_), channel_id=1, source_target_pairs={{4,8},{12,16},{20,24},{8,4},{16,12},{24,20},{5,9},{13,17},{21,25},... | collective-permute-start | bytes 786440 | tf_op jit(solution)/shard_map/ppermute | solution.py:91
  13.0 10.8 %collective-permute-done.2.rest_2_ = f32[512,128]{1,0:T(8,128)S(1)} collective-permute-done((f32[512,128]{1,0:T(8,128)S(1)}, f32[512,128]{1,0:T(8,128)S(1)}, u32[]{:S(2)}, u32[]{:S(2)}) %collective-permute-start.2) | collective-permute-done | bytes 262176 | tf_op jit(solution)/shard_map/ppermute | solution.py:93
  23.9 0.0 collective-permute-done.3.rest_3_
  23.9 1.3 %source.1 = (f32[16,16,128]{2,1,0:T(8,128)S(1)}, f32[16,16,128]{2,1,0:T(8,128)S(1)}, f32[16,8,128]{2,1,0:T(8,128)S(1)}) custom-call(f32[16,16,128]{2,1,0:T(8,128)S(1)} %get-tuple-element.26.factor, f32[4,16,16,128]{3,2,1,0:T(8,128)S(1)} %get-tuple-element.18.flow_ref, f32[512,128]{1,0:T(8,128)S(1)} %get-tuple-element.27.rest_0_, ...), custom_call_target="tpu_custom_call" | custom-call | flops 1000000 | bytes 1000000 | tf_op jit(solution)/shard_map/source/pallas_call | solution.py:110
  25.2 1.4 %collective-permute-start.4 = (f32[16,8,128]{2,1,0:T(8,128)S(1)}, f32[16,8,128]{2,1,0:T(8,128)S(1)}, u32[]{:S(2)}, u32[]{:S(2)}) collective-permute-start(f32[16,8,128]{2,1,0:T(8,128)S(1)} %get-tuple-element.31), channel_id=1, source_target_pairs={{0,2},{2,0},{1,3},{3,1},{4,6},{6,4},{5,7},{7,5},{8,10},{10,8},{9,1... | collective-permute-start | bytes 196616 | tf_op jit(solution)/shard_map/ppermute | solution.py:93
  26.6 0.0 copy-done.2
  26.6 3.5 %collide.1.ahead = f32[19,16,16,128]{3,2,1,0:T(8,128)} custom-call(f32[19,16,16,128]{3,2,1,0:T(8,128)S(1)} %copy-done, f32[4,16,16,128]{3,2,1,0:T(8,128)S(1)} %get-tuple-element.18.flow_ref, f32[16,16,128]{2,1,0:T(8,128)S(1)} %get-tuple-element.29.damp, s32[16,16,128]{2,1,0:T(8,128)S(1)} %copy-done.2, f32[208,128]{1,0:T(8,128)S(1)} %collective-permute-done.rest_1_.rest_0_, ...), custom_call_target="tpu_custom_call" | custom-call | flops 9830400 | bytes 5767168 | tf_op jit(solution)/shard_map/collide/pallas_call | solution.py:110
  30.1 0.0 collective-permute-done.4.rest_0_
  30.1 0.1 smooth_y.1.field
  30.2 0.1 collective-permute-start.5
  30.3 0.3 own_z.1.own
  30.6 1.1 %collective-permute-done.5.rest_0_ = f32[16,16,128]{2,1,0:T(8,128)S(1)} collective-permute-done((f32[16,16,128]{2,1,0:T(8,128)S(1)}, f32[16,16,128]{2,1,0:T(8,128)S(1)}, u32[]{:S(2)}, u32[]{:S(2)}) %collective-permute-start.5) | collective-permute-done | bytes 131104 | tf_op jit(solution)/shard_map/ppermute | solution.py:93
  31.6 0.9 %smooth_z.1 = f32[16,16,128]{2,1,0:T(8,128)} custom-call(f32[3,128,128]{2,1,0:T(8,128)S(1)} %copy-done.1, f32[256,128]{1,0:T(8,128)S(1)} %own_z.1.own, f32[16,16,128]{2,1,0:T(8,128)S(1)} %collective-permute-done.5.rest_0_), custom_call_target="tpu_custom_call" | custom-call | flops 1000000 | bytes 1000000 | tf_op jit(solution)/shard_map/smooth_z/pallas_call | solution.py:110
Async XLA Ops:
  0.6 4.3 %copy-start = (f32[19,16,16,128]{3,2,1,0:T(8,128)S(1)}, f32[19,16,16,128]{3,2,1,0:T(8,128)}, u32[]{:S(2)}) copy-start(f32[19,16,16,128]{3,2,1,0:T(8,128)} %adj.7) | copy-start | bytes 7471108
  1.9 6.8 %copy-start.1 = (f32[3,128,128]{2,1,0:T(8,128)S(1)}, f32[3,128,128]{2,1,0:T(8,128)}, u32[]{:S(2)}) copy-start(f32[3,128,128]{2,1,0:T(8,128)} %constant.2.clone.weights) | copy-start | bytes 589828
  1.9 6.4 %collective-permute-start = (f32[208,128]{1,0:T(8,128)S(1)}, f32[208,128]{1,0:T(8,128)S(1)}, u32[]{:S(2)}, u32[]{:S(2)}) collective-permute-start(f32[208,128]{1,0:T(8,128)S(1)} %get-tuple-element.17.ahead), channel_id=1, source_target_pairs={{0,2},{2,0},{1,3},{3,1},{4,6},{6,4},{5,7},{7,5},{8,10},{10,8},{9,1... | collective-permute-start | bytes 319496 | tf_op jit(solution)/shard_map/ppermute | solution.py:93
  8.6 1.4 %collective-permute-start.1 = (f32[16,16,128]{2,1,0:T(8,128)S(1)}, f32[16,16,128]{2,1,0:T(8,128)S(1)}, u32[]{:S(2)}, u32[]{:S(2)}) collective-permute-start(f32[16,16,128]{2,1,0:T(8,128)S(1)} %get-tuple-element.25), channel_id=1, source_target_pairs={{0,1},{1,0},{2,3},{3,2},{4,5},{5,4},{6,7},{7,6},{8,9},{9,8},{10,11... | collective-permute-start | bytes 393224 | tf_op jit(solution)/shard_map/ppermute | solution.py:93
  10.0 16.6 %copy-start.2 = (s32[16,16,128]{2,1,0:T(8,128)S(1)}, s32[16,16,128]{2,1,0:T(8,128)}, u32[]{:S(2)}) copy-start(s32[16,16,128]{2,1,0:T(8,128)} %mask.1) | copy-start | bytes 393220
  10.9 13.0 %collective-permute-start.2 = (f32[512,128]{1,0:T(8,128)S(1)}, f32[512,128]{1,0:T(8,128)S(1)}, u32[]{:S(2)}, u32[]{:S(2)}) collective-permute-start(f32[512,128]{1,0:T(8,128)S(1)} %get-tuple-element.27.rest_0_), channel_id=1, source_target_pairs={{0,4},{8,12},{16,20},{24,28},{4,0},{12,8},{20,16},{28,24},{1,5},{9... | collective-permute-start | bytes 786440 | tf_op jit(solution)/shard_map/ppermute | solution.py:93
  12.4 11.5 %collective-permute-start.3 = (f32[512,128]{1,0:T(8,128)S(1)}, f32[512,128]{1,0:T(8,128)S(1)}, u32[]{:S(2)}, u32[]{:S(2)}) collective-permute-start(f32[512,128]{1,0:T(8,128)S(1)} %get-tuple-element.28.rest_1_), channel_id=1, source_target_pairs={{4,8},{12,16},{20,24},{8,4},{16,12},{24,20},{5,9},{13,17},{21,25},... | collective-permute-start | bytes 786440 | tf_op jit(solution)/shard_map/ppermute | solution.py:91
  25.2 4.9 %collective-permute-start.4 = (f32[16,8,128]{2,1,0:T(8,128)S(1)}, f32[16,8,128]{2,1,0:T(8,128)S(1)}, u32[]{:S(2)}, u32[]{:S(2)}) collective-permute-start(f32[16,8,128]{2,1,0:T(8,128)S(1)} %get-tuple-element.31), channel_id=1, source_target_pairs={{0,2},{2,0},{1,3},{3,1},{4,6},{6,4},{5,7},{7,5},{8,10},{10,8},{9,1... | collective-permute-start | bytes 196616 | tf_op jit(solution)/shard_map/ppermute | solution.py:93
  30.2 1.4 %collective-permute-start.5 = (f32[16,16,128]{2,1,0:T(8,128)S(1)}, f32[16,16,128]{2,1,0:T(8,128)S(1)}, u32[]{:S(2)}, u32[]{:S(2)}) collective-permute-start(f32[16,16,128]{2,1,0:T(8,128)S(1)} %smooth_y.1.field), channel_id=1, source_target_pairs={{0,1},{1,0},{2,3},{3,2},{4,5},{5,4},{6,7},{7,6},{8,9},{9,8},{10,11... | collective-permute-start | bytes 393224 | tf_op jit(solution)/shard_map/ppermute | solution.py:93

commit v3 on v2

--- a/solution.py
+++ b/solution.py
@@ -73,6 +73,22 @@
     return out
 
 
+def packed_band(dims):
+    X, Y, Z = dims
+    out = np.zeros((2, 2, Z, Z), np.float32)
+    for above_x in range(2):
+        for above_z in range(2):
+            for e in range(X):
+                for i in range(X):
+                    for z in range(R):
+                        for j in range(R):
+                            kx = i - e + 2 * R * above_x
+                            kz = j - z + 2 * R * above_z
+                            if 0 <= kx <= 2 * R and 0 <= kz <= 2 * R:
+                                out[above_x, above_z, i * R + j, e * R + z] = TAPS[kx] * TAPS[kz]
+    return out.reshape(4, Z, Z)
+
+
 def sides(parity, even, odd):
     zero = jnp.zeros_like(even)
     if odd is None:
@@ -84,14 +100,18 @@
     return lax.rem(lax.axis_index(axis), 2)
 
 
+def swap(array, axis, count, first):
+    pairs = [(i, i + 1) for i in range(first, count - 1, 2)]
+    return lax.ppermute(array, axis, pairs + [(b, a) for a, b in pairs])
+
+
+def relay(array, axis, count):
+    pairs = [(i + 2, i) for i in range(1, count - 2, 2)] + [(i - 2, i) for i in range(2, count, 2)]
+    return lax.ppermute(array, axis, pairs)
+
+
 def exchange(axis, count, even, odd):
-    got_odd = None
-    if odd is not None:
-        pairs = [(i, i + 1) for i in range(1, count - 1, 2)]
-        got_odd = lax.ppermute(odd, axis, pairs + [(b, a) for a, b in pairs])
-    pairs = [(i, i + 1) for i in range(0, count - 1, 2)]
-    got_even = lax.ppermute(even, axis, pairs + [(b, a) for a, b in pairs])
-    return got_even, got_odd
+    return swap(even, axis, count, 0), (None if odd is None else swap(odd, axis, count, 1))
 
 
 def vmem(count):
@@ -368,7 +388,7 @@
             out[x] = value
             return 0
 
-        lax.fori_loop(0, X, layer, 0, unroll=4)
+        lax.fori_loop(0, X, layer, 0, unroll=True)
 
     for n, (out, face) in enumerate(zip(outs, faces)):
         pl.when(pz == n)(functools.partial(fill, out, face, True))
@@ -416,7 +436,8 @@
     X, Y, Z = dims
     rest = iter(rest)
     y_even, y_odd = refs_of(rest, many_y)
-    smooth, out = rest
+    smooth, out, again = rest
+    again[...] = filtered_y[...]
     smooth[...] = dot(flat(dims, filtered_y), weights[0])
     out[...] = factor[...]
     py = parity_of("gy")
@@ -439,17 +460,57 @@
         out[:, edge, :] = total
 
 
-def pack_x(dims, many_x, many_y, many_z, adj, weights, smooth, factor_in, flow_ref, *rest):
+def faces_x(dims, out, up, factor, flow_ref, pull):
+    X, Y, Z = dims
+    names = (MINUS if up else PLUS)[0]
+    edge = X - 1 if up else 0
+    first = X - R if up else 0
+    at = R * Y
+    out[:at, :] = factor[first : first + R].reshape(R * Y, Z)
+    faces = pull.faces(edge)
+    for q in names:
+        out[at : at + Y, :] = pull.both(q, edge, faces)
+        at += Y
+    for a in range(3):
+        out[at : at + Y, :] = flow_ref[a, edge]
+        at += Y
+
+
+def pack_halo(dims, pz, refs, out):
+    X, Y, Z = dims
+    lane = lax.broadcasted_iota(jnp.int32, (Y, Z), 1)
+    for n, ref in enumerate(refs):
+        value = jnp.zeros((Y, Z), jnp.float32)
+        for x in range(X):
+            there = (lane >= R * x) & (lane < R * (x + 1))
+            value = jnp.where(there, pltpu.roll(ref[x], lanes_x(dims, pz, n, x), 1), value)
+        out[(R + 8 + n) * Y : (R + 9 + n) * Y, :] = value
+
+
+def pack_odd(dims, many_y, many_z, adj, ahead, factor, flow_ref, *rest):
     X, Y, Z = dims
     rest = iter(rest)
     y_even, y_odd = refs_of(rest, many_y)
     z_even, z_odd = refs_of(rest, many_z)
-    outs = [next(rest) for _ in range(1 + many_x)]
-    (factor,) = rest
+    (out,) = rest
+    px = parity_of("gx")
+    pz = parity_of("gz")
+    out[(R + 8) * Y :, :] = ahead[(R + 8) * Y :, :]
+    pull = Pull(adj, dims, parity_of("gy"), y_even, y_odd, pz, z_even, z_odd)
+    pl.when(px == 1)(lambda: faces_x(dims, out, True, factor, flow_ref, pull))
+    pl.when(px != 1)(lambda: faces_x(dims, out, False, factor, flow_ref, pull))
+
+
+def pack_x(dims, many_y, many_z, adj, weights, smooth, factor_in, flow_ref, *rest):
+    X, Y, Z = dims
+    rest = iter(rest)
+    y_even, y_odd = refs_of(rest, many_y)
+    z_even, z_odd = refs_of(rest, many_z)
+    out, whole, factor = rest
     px, py, pz = parity_of("gx"), parity_of("gy"), parity_of("gz")
     value = smooth[...] + halo_z(weights, pz, flat(dims, z_even), flat(dims, z_odd))
-    for out in outs:
-        out[: X * Y, :] = value
+    whole[...] = value
+    pack_halo(dims, pz, [z_even, z_odd][: 1 + many_z], out)
     lane = lax.broadcasted_iota(jnp.int32, (Y, Z), 1)
     factor[...] = factor_in[...]
 
@@ -473,7 +534,7 @@
             factor[x] = factor[x] - jnp.where(lane == edge, change, zero)
             return 0
 
-        lax.fori_loop(0, X, layer, 0, unroll=4)
+        lax.fori_loop(0, X, layer, 0, unroll=True)
 
     for n, ref in enumerate([z_even, z_odd][: 1 + many_z]):
         pl.when(pz == n)(functools.partial(correct, ref, True))
@@ -481,24 +542,8 @@
 
     pull = Pull(adj, dims, py, y_even, y_odd, pz, z_even, z_odd)
 
-    def fill(out, up):
-        names = (MINUS if up else PLUS)[0]
-        edge = X - 1 if up else 0
-        at = X * Y
-        first = X - R if up else 0
-        out[at : at + R * Y, :] = factor[first : first + R].reshape(R * Y, Z)
-        at += R * Y
-        faces = pull.faces(edge)
-        for q in names:
-            out[at : at + Y, :] = pull.both(q, edge, faces)
-            at += Y
-        for a in range(3):
-            out[at : at + Y, :] = flow_ref[a, edge]
-            at += Y
-
-    for n, out in enumerate(outs):
-        pl.when(px == n)(functools.partial(fill, out, True))
-        pl.when(px != n)(functools.partial(fill, out, False))
+    pl.when(px == 0)(lambda: faces_x(dims, out, True, factor, flow_ref, pull))
+    pl.when(px != 0)(lambda: faces_x(dims, out, False, factor, flow_ref, pull))
 
 
 def project(filtered):
@@ -511,17 +556,35 @@
     return physical, steep, inverse
 
 
-def source(dims, many_x, many_y, factor, flow_ref, *rest):
+def taps_of(X, above, e):
+    shift = 2 * R + (X if above else -X) - e
+    return [(TAPS[i + shift], i) for i in range(X) if 0 <= i + shift <= 2 * R]
+
+
+def add_side(dims, base, layers, at, out, above):
+    X, Y, Z = dims
+    for e in range(X + 2 * R):
+        total = base[e]
+        for tap, i in taps_of(X, above, e):
+            total = total + tap * layers[at + i * Y : at + (i + 1) * Y, :]
+        out[e] = total
+
+
+def lanes_x(dims, pz, n, x):
+    Z = dims[2]
+    return jnp.where(pz == n, (R * x) % Z, (R * x + R) % Z)
+
+
+def source(dims, many_x, many_y, many_z, weights, partial, factor, flow_ref, *rest):
     X, Y, Z = dims
     rest = iter(rest)
     own_even, own_odd = refs_of(rest, many_x)
     x_even, x_odd = refs_of(rest, many_x)
     result, damp = next(rest), next(rest)
     outs = [next(rest) for _ in range(1 + many_y)]
-    layers, ext = rest
-    px, py = parity_of("gx"), parity_of("gy")
-    size = X * Y
-    g_at, u_at, v_at = size, size + R * Y, size + R * Y + 5 * Y
+    smooth, ext = rest
+    px, py, pz = parity_of("gx"), parity_of("gy"), parity_of("gz")
+    u_at, v_at, d_at = R * Y, R * Y + 5 * Y, R * Y + 8 * Y
 
     def got(at, count):
         return sides(px, x_even[at : at + count, :], None if x_odd is None else x_odd[at : at + count, :])
@@ -529,15 +592,23 @@
     def own(at, count):
         return sides(px, own_even[at : at + count, :], None if own_odd is None else own_odd[at : at + count, :])
 
-    below, above = got(0, size)
-    layers[:X] = below.reshape(X, Y, Z)
-    layers[X : 2 * X] = own_even[:size, :].reshape(X, Y, Z)
-    layers[2 * X :] = above.reshape(X, Y, Z)
-
-    below, above = got(g_at, R * Y)
-    ext[:R] = below.reshape(R, Y, Z)
+    smooth[...] = partial[...]
+    lane = lax.broadcasted_iota(jnp.int32, (Y, Z), 1)
+    for odd, ref in enumerate([x_even, x_odd][: 1 + many_x]):
+        above_x = jnp.where(px == odd, 1, 0)
+        for n in range(1 + many_z):
+            above_z = jnp.where(pz == n, 1, 0)
+            value = dot(ref[d_at + n * Y : d_at + (n + 1) * Y, :], weights[2 * above_x + above_z])
+            first = (Z - R) * above_z
+            there = (lane >= first) & (lane < first + R)
+            for e in range(X):
+                at = e + X * above_x
+                moved = pltpu.roll(value, lax.rem(first + Z - R * e, Z), 1)
+                smooth[at] = smooth[at] + jnp.where(there, moved, 0.0)
+    low, high = got(0, R * Y)
+    ext[:R] = low.reshape(R, Y, Z)
     ext[R : R + X] = factor[...]
-    ext[R + X :] = above.reshape(R, Y, Z)
+    ext[R + X :] = high.reshape(R, Y, Z)
 
     def face_moment(block, names):
         return moment_of({q: block[j * Y : (j + 1) * Y] for j, q in enumerate(names)})
@@ -554,26 +625,14 @@
     less(R + X, [vel_high[a * Y : (a + 1) * Y] for a in range(3)], face_moment(own_high, MINUS[0]))
 
     slope = -damping_max * ramp_shape * (1.0 + ramp_shape)
-    base = X - 2 * R
-
-    def layer(e, _):
-        smooth = filter_rows(lambda k: layers[base + e + k])
-        physical, steep, inverse = project(smooth)
+    for e in range(X + 2 * R):
+        physical, steep, inverse = project(smooth[e])
         ext[e] = (slope * steep) * (inverse * inverse) * ext[e]
-
-        @pl.when((e >= R) & (e < R + X))
-        def _():
+        if R <= e < R + X:
             damp[e - R] = (2.0 * damping_max * ramp_shape) * (1.0 - physical) * inverse
 
-        return 0
-
-    lax.fori_loop(0, X + 2 * R, layer, 0, unroll=4)
-
-    def last(x, _):
+    for x in range(X):
         result[x] = filter_rows(lambda k: ext[x + k])
-        return 0
-
-    lax.fori_loop(0, X, last, 0, unroll=4)
     for n, out in enumerate(outs):
 
         @pl.when(py == n)
@@ -605,7 +664,90 @@
     result[...] = value.reshape(dims)
 
 
-def collide(dims, many_x, many_y, many_z, step, adj, flow_ref, damp, mask, *rest):
+def relax(pulled, vel, speed_sq, label, drag, store):
+    plus = {q: pulled[q] + pulled[q + 1] for q in range(1, Q, 2)}
+    minus = {q: pulled[q] - pulled[q + 1] for q in range(1, Q, 2)}
+    axes = (1, 3, 5)
+    straight = plus[1] + plus[3] + plus[5]
+    slanted = plus[7] + plus[9] + plus[11] + plus[13] + plus[15] + plus[17]
+    zeroth = (1.0 / 3.0) * pulled[0] + (1.0 / 18.0) * straight + (1.0 / 36.0) * slanted
+    first, diagonal = [], []
+    for a in range(3):
+        terms = [(velocity[q][a], minus[q]) for q in range(7, Q, 2) if velocity[q][a] != 0]
+        first.append((1.0 / 18.0) * minus[axes[a]] + (1.0 / 36.0) * signed(terms))
+        both = [(1, plus[q]) for q in range(7, Q, 2) if velocity[q][a] != 0]
+        diagonal.append((1.0 / 18.0) * plus[axes[a]] + (1.0 / 36.0) * signed(both))
+    xy = (1.0 / 36.0) * (plus[7] - plus[9])
+    xz = (1.0 / 36.0) * (plus[11] - plus[13])
+    yz = (1.0 / 36.0) * (plus[15] - plus[17])
+    turned = [
+        diagonal[0] * vel[0] + xy * vel[1] + xz * vel[2],
+        xy * vel[0] + diagonal[1] * vel[1] + yz * vel[2],
+        xz * vel[0] + yz * vel[1] + diagonal[2] * vel[2],
+    ]
+    quadric = vel[0] * turned[0] + vel[1] * turned[1] + vel[2] * turned[2]
+    eq_scalar = zeroth * (1.0 + 1.5 * speed_sq) - 4.5 * quadric
+    eq_vector = [3.0 * first[a] + 9.0 * turned[a] - 3.0 * zeroth * vel[a] for a in range(3)]
+    fluid, solid, inlet = label == 0, label == 1, label == 2
+    zero = jnp.zeros_like(eq_scalar)
+    keep = jnp.where(fluid, 1.0 - relax_rate, zero)
+    bounce = jnp.where(solid, 1.0, zero)
+    level = relax_rate * eq_scalar
+    tilt = [relax_rate * v for v in eq_vector]
+    if drag is not None:
+        level = level - drag * speed_sq
+        tilt = [t + drag * v for t, v in zip(tilt, vel)]
+    level = jnp.where(fluid, level, jnp.where(solid, zero, eq_scalar))
+    tilt = [jnp.where(fluid, t, jnp.where(inlet, v, zero)) for t, v in zip(tilt, eq_vector)]
+    store(0, (keep + bounce) * pulled[0] + level)
+    for q in range(1, Q, 2):
+        lean = lean_of(q, tilt)
+        store(q, keep * pulled[q] + bounce * pulled[q + 1] + (level + lean))
+        store(q + 1, keep * pulled[q + 1] + bounce * pulled[q] + (level - lean))
+
+
+def lean_of(q, vector):
+    return signed([(velocity[q][a], vector[a]) for a in range(3) if velocity[q][a] != 0])
+
+
+def square(vel):
+    return vel[0] * vel[0] + vel[1] * vel[1] + vel[2] * vel[2]
+
+
+def far_x(dims, odd, weights, partial, beyond, out, smooth):
+    X, Y, Z = dims
+    smooth[...] = dot(flat(dims, beyond), weights[0])
+    px = parity_of("gx")
+    pl.when(px == odd)(lambda: add_side(dims, partial, smooth, 0, out, True))
+    pl.when(px != odd)(lambda: add_side(dims, partial, smooth, 0, out, False))
+
+
+def beside_x(dims, many_y, many_z, adj, flow_ref, mask, own, *rest):
+    X, Y, Z = dims
+    rest = iter(rest)
+    y_even, y_odd = refs_of(rest, many_y)
+    z_even, z_odd = refs_of(rest, many_z)
+    partial, base = rest
+    for e in range(X + 2 * R):
+        terms = [(i - e + 2 * R, i * Y) for i in range(X) if 0 <= i - e + 2 * R <= 2 * R]
+        partial[e] = sum(TAPS[k] * own[at : at + Y, :] for k, at in terms)
+    pull = Pull(adj, dims, parity_of("gy"), y_even, y_odd, parity_of("gz"), z_even, z_odd)
+
+    def layer(x, _):
+        around = {c: pull.faces(x + c) for c in (-1, 0, 1)}
+        pulled = [pull.both(q, x + velocity[q][0], around[velocity[q][0]]) for q in range(Q)]
+        vel = [flow_ref[a, x] for a in range(3)]
+
+        def store(q, value):
+            base[q, x] = value
+
+        relax(pulled, vel, square(vel), mask[x], None, store)
+        return 0
+
+    lax.fori_loop(1, X - 1, layer, 0)
+
+
+def collide(dims, many_x, many_y, many_z, step, adj, base, flow_ref, damp, mask, *rest):
     X, Y, Z = dims
     rest = iter(rest)
     y_even, y_odd = refs_of(rest, many_y)
@@ -615,67 +757,42 @@
     px, py, pz = parity_of("gx"), parity_of("gy"), parity_of("gz")
     pull = Pull(adj, dims, py, y_even, y_odd, pz, z_even, z_odd)
     begin = pl.program_id(0) * step
-    u_at = X * Y + R * Y
+    u_at = R * Y
 
     def layer(i, _):
         x = begin + i
-        around = {c: pull.faces(jnp.clip(x + c, 0, X - 1)) for c in (-1, 0, 1)}
+        vel = [flow_ref[a, x] for a in range(3)]
+        drag = jnp.where(mask[x] == 0, damp[x] * flow_ref[3, x], 0.0)
+        level = drag * square(vel)
+        tilt = [drag * v for v in vel]
+        out[0, i] = base[0, x] - level
+        for q in range(1, Q, 2):
+            lean = lean_of(q, tilt)
+            out[q, i] = base[q, x] + (lean - level)
+            out[q + 1, i] = base[q + 1, x] - (lean + level)
+        return 0
+
+    def edge(x, i, toward):
+        around = {c: pull.faces(x + c) for c in (0, -toward)}
         pulled = []
         for q in range(Q):
             cx = velocity[q][0]
-            value = pull.both(q, jnp.clip(x + cx, 0, X - 1), around[cx])
-            if cx != 0:
+            if cx == toward:
                 at = u_at + Y * (PLUS if cx > 0 else MINUS)[0].index(q)
-                below, above = sides(
-                    px, x_even[at : at + Y, :], None if x_odd is None else x_odd[at : at + Y, :]
-                )
-                value = jnp.where(x == (X - 1 if cx > 0 else 0), above if cx > 0 else below, value)
-            pulled.append(value)
+                both = sides(px, x_even[at : at + Y, :], None if x_odd is None else x_odd[at : at + Y, :])
+                pulled.append(both[int(cx > 0)])
+            else:
+                pulled.append(pull.both(q, x + cx, around[cx]))
         vel = [flow_ref[a, x] for a in range(3)]
-        inverse = flow_ref[3, x]
-        speed_sq = vel[0] * vel[0] + vel[1] * vel[1] + vel[2] * vel[2]
-        plus = {q: pulled[q] + pulled[q + 1] for q in range(1, Q, 2)}
-        minus = {q: pulled[q] - pulled[q + 1] for q in range(1, Q, 2)}
-        axes = (1, 3, 5)
-        straight = plus[1] + plus[3] + plus[5]
-        slanted = plus[7] + plus[9] + plus[11] + plus[13] + plus[15] + plus[17]
-        zeroth = (1.0 / 3.0) * pulled[0] + (1.0 / 18.0) * straight + (1.0 / 36.0) * slanted
-        first, diagonal = [], []
-        for a in range(3):
-            terms = [(velocity[q][a], minus[q]) for q in range(7, Q, 2) if velocity[q][a] != 0]
-            first.append((1.0 / 18.0) * minus[axes[a]] + (1.0 / 36.0) * signed(terms))
-            both = [(1, plus[q]) for q in range(7, Q, 2) if velocity[q][a] != 0]
-            diagonal.append((1.0 / 18.0) * plus[axes[a]] + (1.0 / 36.0) * signed(both))
-        xy = (1.0 / 36.0) * (plus[7] - plus[9])
-        xz = (1.0 / 36.0) * (plus[11] - plus[13])
-        yz = (1.0 / 36.0) * (plus[15] - plus[17])
-        turned = [
-            diagonal[0] * vel[0] + xy * vel[1] + xz * vel[2],
-            xy * vel[0] + diagonal[1] * vel[1] + yz * vel[2],
-            xz * vel[0] + yz * vel[1] + diagonal[2] * vel[2],
-        ]
-        quadric = vel[0] * turned[0] + vel[1] * turned[1] + vel[2] * turned[2]
-        eq_scalar = zeroth * (1.0 + 1.5 * speed_sq) - 4.5 * quadric
-        eq_vector = [3.0 * first[a] + 9.0 * turned[a] - 3.0 * zeroth * vel[a] for a in range(3)]
-        label = mask[x]
-        drag = damp[x] * inverse
-        fluid, solid, inlet = label == 0, label == 1, label == 2
-        zero = jnp.zeros_like(drag)
-        keep = jnp.where(fluid, 1.0 - relax_rate, zero)
-        bounce = jnp.where(solid, 1.0, zero)
-        level = jnp.where(fluid, relax_rate * eq_scalar - drag * speed_sq, jnp.where(solid, zero, eq_scalar))
-        tilt = [
-            jnp.where(fluid, relax_rate * eq_vector[a] + drag * vel[a], jnp.where(inlet, eq_vector[a], zero))
-            for a in range(3)
-        ]
-        out[0, i] = (keep + bounce) * pulled[0] + level
-        for q in range(1, Q, 2):
-            lean = signed([(velocity[q][a], tilt[a]) for a in range(3) if velocity[q][a] != 0])
-            out[q, i] = keep * pulled[q] + bounce * pulled[q + 1] + (level + lean)
-            out[q + 1, i] = keep * pulled[q + 1] + bounce * pulled[q] + (level - lean)
-        return 0
-
-    lax.fori_loop(0, step, layer, 0)
+
+        def store(q, value):
+            out[q, i] = value
+
+        relax(pulled, vel, square(vel), mask[x], damp[x] * flow_ref[3, x], store)
+
+    lax.fori_loop(0, step, layer, 0, unroll=2)
+    pl.when(pl.program_id(0) == 0)(lambda: edge(0, 0, -1))
+    pl.when(pl.program_id(0) == X // step - 1)(lambda: edge(X - 1, step - 1, 1))
 
 
 def local(counts, forward, adjoint, design, mask):
@@ -725,31 +842,63 @@
     )
     got_z = some(exchange("gz", nz, *pair(to_z)))
 
-    smooth, factor = call(
+    smooth, factor, beyond = call(
         functools.partial(factor_y, dims, many_y),
-        [f32(X * Y, Z), f32(X, Y, Z)],
+        [f32(X * Y, Z), f32(X, Y, Z), f32(X, Y, Z)],
         (weights, filtered_y, flow_values, factor, *got_y),
         limit=8,
         flops=200 * cells,
         name="factor_y",
     )
-
-    x_rows = X * Y + R * Y + 8 * Y
-    *to_x, factor = call(
-        functools.partial(pack_x, dims, many_x, many_y, many_z),
-        [f32(x_rows, Z)] * (1 + many_x) + [f32(X, Y, Z)],
+    beyond = swap(beyond, "gx", nx, 0)
+
+    x_rows = R * Y + 8 * Y
+    even, smooth, factor = call(
+        functools.partial(pack_x, dims, many_y, many_z),
+        [f32(x_rows + (1 + many_z) * Y, Z), f32(X * Y, Z), f32(X, Y, Z)],
         (adjoint, weights, smooth, factor, flow_values, *got_y, *got_z),
         limit=16,
         name="pack_x",
     )
+    to_x = [even]
+    if many_x:
+        to_x += call(
+            functools.partial(pack_odd, dims, many_y, many_z),
+            [f32(x_rows + (1 + many_z) * Y, Z)],
+            (adjoint, even, factor, flow_values, *got_y, *got_z),
+            limit=16,
+            name="pack_odd",
+        )
     got_x = some(exchange("gx", nx, *pair(to_x)))
 
+    partial, base = call(
+        functools.partial(beside_x, dims, many_y, many_z),
+        [f32(X + 2 * R, Y, Z), f32(Q, X, Y, Z)],
+        (adjoint, flow_values, mask, smooth, *got_y, *got_z),
+        limit=16,
+        flops=100000 * cells,
+        moved=1000,
+        name="beside_x",
+    )
+    for odd, layers in enumerate([beyond] + ([relay(beyond, "gx", nx)] if many_x else [])):
+        (partial,) = call(
+            functools.partial(far_x, dims, odd),
+            [f32(X + 2 * R, Y, Z)],
+            (weights, partial, layers),
+            None,
+            [pltpu.VMEM((X * Y, Z), jnp.float32)],
+            limit=8,
+            flops=1000,
+            moved=1000,
+            name="far_odd" if odd else "far_even",
+        )
+
     result, damp, *to_y = call(
-        functools.partial(source, dims, many_x, many_y),
+        functools.partial(source, dims, many_x, many_y, many_z),
         [f32(X, Y, Z), f32(X, Y, Z)] + [f32(X, R, Z)] * (1 + many_y),
-        (factor, flow_values, *to_x, *got_x),
+        (jnp.asarray(packed_band(dims)), partial, factor, flow_values, *to_x, *got_x),
         None,
-        [pltpu.VMEM((3 * X, Y, Z), jnp.float32), pltpu.VMEM((X + 2 * R, Y, Z), jnp.float32)],
+        [pltpu.VMEM((X + 2 * R, Y, Z), jnp.float32)] * 2,
         limit=8,
         name="source",
     )
@@ -760,8 +909,8 @@
     adjoint_next = call(
         functools.partial(collide, dims, many_x, many_y, many_z, step),
         f32(Q, X, Y, Z),
-        (adjoint, flow_values, damp, mask, *got_y, *got_z, *got_x),
-        [whole] * (4 + len(got_y) + len(got_z) + len(got_x)),
+        (adjoint, base, flow_values, damp, mask, *got_y, *got_z, *got_x),
+        [whole] * (5 + len(got_y) + len(got_z) + len(got_x)),
         out_specs=pl.BlockSpec((Q, step, Y, Z), lambda i: (0, i, 0, 0)),
         grid=(X // step,),
         limit=16,

time: 32.7 us -> 29.4 us (0.90)
  waiting for transfers between devices: 13 us -> 4.19 us
  starting transfers between devices: 6.75 us -> 11.3 us
  Pallas kernels: 12.1 us -> 12.9 us
    ppermute x6 -> x8, waiting for transfers between devices: 13 us -> 4.19 us  [the longest x7 4.18 us: swap(): return lax.ppermute(array, axis, pairs + [(b, a) for a, b in pairs])]
    ppermute x6 -> x8, starting transfers between devices: 6.75 us -> 11.3 us  [the longest x7 7.82 us: swap(): return lax.ppermute(array, axis, pairs + [(b, a) for a, b in pairs])]
    pallas_call x10 -> x14, Pallas kernels: 12.1 us -> 12.9 us  [call(): pl.pallas_call(body, out_shape=outs, in_specs=specs or vmem(len(args)), o...]
  transfers between devices with their start and end apart: 6 -> 8, of which waited for: 3 -> 3; matrix products, arithmetic and copies ran while one was open for 0% -> 0% of each run, Pallas kernels for 23% -> 33%
where the time goes in v3:
time: 29.4 us; the launch traced here: 29.2 us
  Pallas kernels  12.9 us (44%)
  starting transfers between devices  11.3 us (38%)
  waiting for transfers between devices  4.19 us (14%)
  between operations  0.82 us (3%)
    pallas_call x14, Pallas kernels, call(): pl.pallas_call(body, out_shape=outs, in_specs=specs or vmem(len(args)), o...  12.9 us
    ppermute x7, starting transfers between devices, swap(): return lax.ppermute(array, axis, pairs + [(b, a) for a, b in pairs])  7.82 us
    ppermute x7, waiting for transfers between devices, swap(): return lax.ppermute(array, axis, pairs + [(b, a) for a, b in pairs])  4.18 us
    ppermute x1, starting transfers between devices, relay(): return lax.ppermute(array, axis, pairs)  3.48 us
  transfers between devices with their start and end apart: 8, of which 3 were waited for; matrix products, arithmetic and copies ran while one was open for 0% of the time, Pallas kernels for 33%

profile of v3, /device:TPU:0, one launch (start us, length us, event | category | flops | bytes accessed | tf_op | source)
XLA Modules:
  0.0 29.2 jit_solution(3172113223849508863)
XLA Ops:
  0.6 1.3 %pack_y.1 = (f32[208,128]{1,0:T(8,128)S(1)}, f32[16,16,128]{2,1,0:T(8,128)S(1)}) custom-call(f32[19,16,16,128]{3,2,1,0:T(8,128)} %adj.11, f32[16,16,128]{2,1,0:T(8,128)} %design.1), custom_call_target="tpu_custom_call" | custom-call | flops 1000000 | bytes 1000000 | tf_op jit(solution)/shard_map/pack_y/pallas_call | solution.py:130
  1.9 0.0 copy-start.1
  1.9 3.0 %collective-permute-start = (f32[208,128]{1,0:T(8,128)S(1)}, f32[208,128]{1,0:T(8,128)S(1)}, u32[]{:S(2)}, u32[]{:S(2)}) collective-permute-start(f32[208,128]{1,0:T(8,128)S(1)} %get-tuple-element.20.ahead), channel_id=1, source_target_pairs={{0,2},{2,0},{1,3},{3,1},{4,6},{6,4},{5,7},{7,5},{8,10},{10,8},{9,1... | collective-permute-start | bytes 319496 | tf_op jit(solution)/shard_map/ppermute | solution.py:105
  5.0 3.4 %prepare.1 = (f32[4,16,16,128]{3,2,1,0:T(8,128)S(1)}, f32[16,16,128]{2,1,0:T(8,128)S(1)}, f32[16,16,128]{2,1,0:T(8,128)S(1)}) custom-call(f32[208,128]{1,0:T(8,128)S(1)} %get-tuple-element.20.ahead, f32[19,16,16,128]{3,2,1,0:T(8,128)} %forward.1, f32[19,16,16,128]{3,2,1,0:T(8,128)S(1)} %copy-done), custom_call_target="tpu_custom_call" | custom-call | flops 6553600 | bytes 5767168 | tf_op jit(solution)/shard_map/prepare/pallas_call | solution.py:130
  8.3 0.0 collective-permute-done.rest_1_.rest_0_
  8.3 0.2 design_y.1
  8.6 0.1 collective-permute-start.1
  8.7 0.3 factor_y.1
  8.9 1.6 %collective-permute-start.2 = (f32[16,16,128]{2,1,0:T(8,128)S(1)}, f32[16,16,128]{2,1,0:T(8,128)S(1)}, u32[]{:S(2)}, u32[]{:S(2)}) collective-permute-start(f32[16,16,128]{2,1,0:T(8,128)S(1)} %get-tuple-element.32), channel_id=1, source_target_pairs={{0,4},{8,12},{16,20},{24,28},{4,0},{12,8},{20,16},{28,24},{1,5},{9... | collective-permute-start | bytes 393224 | tf_op jit(solution)/shard_map/ppermute | solution.py:105
  10.5 0.0 collective-permute-done.1.rest_1_
  10.5 0.5 %pack_x.1 = (f32[272,128]{1,0:T(8,128)S(1)}, f32[256,128]{1,0:T(8,128)S(1)}, f32[16,16,128]{2,1,0:T(8,128)S(1)}) custom-call(f32[19,16,16,128]{3,2,1,0:T(8,128)S(1)} %copy-done, f32[3,128,128]{2,1,0:T(8,128)S(1)} %copy-done.1, f32[256,128]{1,0:T(8,128)S(1)} %get-tuple-element.26.smooth, f32[16,16,128]{2,1,0:T(8,128)S(1)} %get-tuple-element.27.factor_in, ...), custom_call_target="tpu_custom_call" | custom-call | flops 1000000 | bytes 1000000 | tf_op jit(solution)/shard_map/pack_x/pallas_call | solution.py:130
  11.0 1.0 %collective-permute-start.4 = (f32[272,128]{1,0:T(8,128)S(1)}, f32[272,128]{1,0:T(8,128)S(1)}, u32[]{:S(2)}, u32[]{:S(2)}) collective-permute-start(f32[272,128]{1,0:T(8,128)S(1)} %get-tuple-element.34.ahead.rest_0_), channel_id=1, source_target_pairs={{0,4},{8,12},{16,20},{24,28},{4,0},{12,8},{20,16},{28,24},{1,5},{9... | collective-permute-start | bytes 417800 | tf_op jit(solution)/shard_map/ppermute | solution.py:105
  12.1 0.1 pack_odd.1.rest_1_
  12.2 0.7 %collective-permute-start.5 = (f32[272,128]{1,0:T(8,128)S(1)}, f32[272,128]{1,0:T(8,128)S(1)}, u32[]{:S(2)}, u32[]{:S(2)}) collective-permute-start(f32[272,128]{1,0:T(8,128)S(1)} %pack_odd.1.rest_1_), channel_id=1, source_target_pairs={{4,8},{12,16},{20,24},{8,4},{16,12},{24,20},{5,9},{13,17},{21,25},... | collective-permute-start | bytes 417800 | tf_op jit(solution)/shard_map/ppermute | solution.py:105
  12.8 2.5 %collective-permute-done.2.beyond = f32[16,16,128]{2,1,0:T(8,128)S(1)} collective-permute-done((f32[16,16,128]{2,1,0:T(8,128)S(1)}, f32[16,16,128]{2,1,0:T(8,128)S(1)}, u32[]{:S(2)}, u32[]{:S(2)}) %collective-permute-start.2) | collective-permute-done | bytes 131104 | tf_op jit(solution)/shard_map/ppermute | solution.py:105
  15.3 3.5 %collective-permute-start.3 = (f32[16,16,128]{2,1,0:T(8,128)S(1)}, f32[16,16,128]{2,1,0:T(8,128)S(1)}, u32[]{:S(2)}, u32[]{:S(2)}) collective-permute-start(f32[16,16,128]{2,1,0:T(8,128)S(1)} %collective-permute-done.2.beyond), channel_id=1, source_target_pairs={{12,4},{20,12},{28,20},{0,8},{8,16},{16,24},{13,5},{21,13},{29,21}... | collective-permute-start | bytes 393224 | tf_op jit(solution)/shard_map/ppermute | solution.py:110
  18.8 0.0 copy-start.2
  18.8 2.2 %beside_x.1 = (f32[32,16,128]{2,1,0:T(8,128)S(1)}, f32[19,16,16,128]{3,2,1,0:T(8,128)S(1)}) custom-call(f32[19,16,16,128]{3,2,1,0:T(8,128)S(1)} %copy-done, f32[4,16,16,128]{3,2,1,0:T(8,128)S(1)} %get-tuple-element.21.flow_ref, s32[16,16,128]{2,1,0:T(8,128)S(1)} %copy-done.3, f32[256,128]{1,0:T(8,128)S(1)} %get-tuple-element.29.own, ...), custom_call_target="tpu_custom_call" | custom-call | flops 3276800000 | bytes 1000 | tf_op jit(solution)/shard_map/beside_x/pallas_call | solution.py:130
  21.0 0.3 %far_even.1.partial = f32[32,16,128]{2,1,0:T(8,128)S(1)} custom-call(f32[3,128,128]{2,1,0:T(8,128)S(1)} %copy-done.1, f32[32,16,128]{2,1,0:T(8,128)S(1)} %get-tuple-element.31.partial, f32[16,16,128]{2,1,0:T(8,128)S(1)} %collective-permute-done.2.beyond), custom_call_target="tpu_custom_call" | custom-call | flops 1000 | bytes 1000 | tf_op jit(solution)/shard_map/far_even/pallas_call | solution.py:130
  21.3 0.0 collective-permute-done.3.beyond
  21.3 0.3 %far_odd.1.partial = f32[32,16,128]{2,1,0:T(8,128)S(1)} custom-call(f32[3,128,128]{2,1,0:T(8,128)S(1)} %copy-done.1, f32[32,16,128]{2,1,0:T(8,128)S(1)} %far_even.1.partial, f32[16,16,128]{2,1,0:T(8,128)S(1)} %collective-permute-done.3.beyond), custom_call_target="tpu_custom_call" | custom-call | flops 1000 | bytes 1000 | tf_op jit(solution)/shard_map/far_odd/pallas_call | solution.py:130
  21.7 0.0 collective-permute-done.5.rest_3_
  21.7 0.0 collective-permute-done.4.rest_2_
  21.7 0.7 %source.1 = (f32[16,16,128]{2,1,0:T(8,128)S(1)}, f32[16,16,128]{2,1,0:T(8,128)S(1)}, f32[16,8,128]{2,1,0:T(8,128)S(1)}) custom-call(f32[4,128,128]{2,1,0:T(8,128)S(1)} %copy-done.2, f32[32,16,128]{2,1,0:T(8,128)S(1)} %far_odd.1.partial, f32[16,16,128]{2,1,0:T(8,128)S(1)} %get-tuple-element.33.factor, f32[4,16,16,128]{3,2,1,0:T(8,128)S(1)} %get-tuple-element.21.flow_ref, ...), custom_call_target="tpu_custom_call" | custom-call | flops 1000000 | bytes 1000000 | tf_op jit(solution)/shard_map/source/pallas_call | solution.py:130
  22.4 1.4 %collective-permute-start.6 = (f32[16,8,128]{2,1,0:T(8,128)S(1)}, f32[16,8,128]{2,1,0:T(8,128)S(1)}, u32[]{:S(2)}, u32[]{:S(2)}) collective-permute-start(f32[16,8,128]{2,1,0:T(8,128)S(1)} %get-tuple-element.37), channel_id=1, source_target_pairs={{0,2},{2,0},{1,3},{3,1},{4,6},{6,4},{5,7},{7,5},{8,10},{10,8},{9,1... | collective-permute-start | bytes 196616 | tf_op jit(solution)/shard_map/ppermute | solution.py:105
  23.8 2.3 %collide.1.ahead = f32[19,16,16,128]{3,2,1,0:T(8,128)} custom-call(f32[19,16,16,128]{3,2,1,0:T(8,128)S(1)} %copy-done, f32[19,16,16,128]{3,2,1,0:T(8,128)S(1)} %get-tuple-element.30.base, f32[4,16,16,128]{3,2,1,0:T(8,128)S(1)} %get-tuple-element.21.flow_ref, f32[16,16,128]{2,1,0:T(8,128)S(1)} %get-tuple-element.35.damp, s32[16,16,128]{2,1,0:T(8,128)S(1)} %copy-done.3, ...), custom_call_target="tpu_custom_call" | custom-call | flops 9830400 | bytes 5767168 | tf_op jit(solution)/shard_map/collide/pallas_call | solution.py:130
  26.1 0.6 %collective-permute-done.6.rest_0_ = f32[16,8,128]{2,1,0:T(8,128)S(1)} collective-permute-done((f32[16,8,128]{2,1,0:T(8,128)S(1)}, f32[16,8,128]{2,1,0:T(8,128)S(1)}, u32[]{:S(2)}, u32[]{:S(2)}) %collective-permute-start.6) | collective-permute-done | bytes 65568 | tf_op jit(solution)/shard_map/ppermute | solution.py:105
  26.7 0.1 smooth_y.1.field
  26.9 0.1 collective-permute-start.7
  27.0 0.3 own_z.1.own
  27.2 1.1 %collective-permute-done.7.rest_0_ = f32[16,16,128]{2,1,0:T(8,128)S(1)} collective-permute-done((f32[16,16,128]{2,1,0:T(8,128)S(1)}, f32[16,16,128]{2,1,0:T(8,128)S(1)}, u32[]{:S(2)}, u32[]{:S(2)}) %collective-permute-start.7) | collective-permute-done | bytes 131104 | tf_op jit(solution)/shard_map/ppermute | solution.py:105
  28.3 0.9 %smooth_z.1 = f32[16,16,128]{2,1,0:T(8,128)} custom-call(f32[3,128,128]{2,1,0:T(8,128)S(1)} %copy-done.1, f32[256,128]{1,0:T(8,128)S(1)} %own_z.1.own, f32[16,16,128]{2,1,0:T(8,128)S(1)} %collective-permute-done.7.rest_0_), custom_call_target="tpu_custom_call" | custom-call | flops 1000000 | bytes 1000000 | tf_op jit(solution)/shard_map/smooth_z/pallas_call | solution.py:130
  (6 shorter events, 0.0 us)
Async XLA Ops:
  0.6 4.3 %copy-start = (f32[19,16,16,128]{3,2,1,0:T(8,128)S(1)}, f32[19,16,16,128]{3,2,1,0:T(8,128)}, u32[]{:S(2)}) copy-start(f32[19,16,16,128]{3,2,1,0:T(8,128)} %adj.11) | copy-start | bytes 7471108
  1.9 6.7 %copy-start.1 = (f32[3,128,128]{2,1,0:T(8,128)S(1)}, f32[3,128,128]{2,1,0:T(8,128)}, u32[]{:S(2)}) copy-start(f32[3,128,128]{2,1,0:T(8,128)} %constant.4.clone.weights) | copy-start | bytes 589828
  1.9 6.4 %collective-permute-start = (f32[208,128]{1,0:T(8,128)S(1)}, f32[208,128]{1,0:T(8,128)S(1)}, u32[]{:S(2)}, u32[]{:S(2)}) collective-permute-start(f32[208,128]{1,0:T(8,128)S(1)} %get-tuple-element.20.ahead), channel_id=1, source_target_pairs={{0,2},{2,0},{1,3},{3,1},{4,6},{6,4},{5,7},{7,5},{8,10},{10,8},{9,1... | collective-permute-start | bytes 319496 | tf_op jit(solution)/shard_map/ppermute | solution.py:105
  8.6 1.9 %collective-permute-start.1 = (f32[16,16,128]{2,1,0:T(8,128)S(1)}, f32[16,16,128]{2,1,0:T(8,128)S(1)}, u32[]{:S(2)}, u32[]{:S(2)}) collective-permute-start(f32[16,16,128]{2,1,0:T(8,128)S(1)} %get-tuple-element.28), channel_id=1, source_target_pairs={{0,1},{1,0},{2,3},{3,2},{4,5},{5,4},{6,7},{7,6},{8,9},{9,8},{10,11... | collective-permute-start | bytes 393224 | tf_op jit(solution)/shard_map/ppermute | solution.py:105
  8.9 6.4 %collective-permute-start.2 = (f32[16,16,128]{2,1,0:T(8,128)S(1)}, f32[16,16,128]{2,1,0:T(8,128)S(1)}, u32[]{:S(2)}, u32[]{:S(2)}) collective-permute-start(f32[16,16,128]{2,1,0:T(8,128)S(1)} %get-tuple-element.32), channel_id=1, source_target_pairs={{0,4},{8,12},{16,20},{24,28},{4,0},{12,8},{20,16},{28,24},{1,5},{9... | collective-permute-start | bytes 393224 | tf_op jit(solution)/shard_map/ppermute | solution.py:105
  11.0 7.7 %copy-start.3 = (s32[16,16,128]{2,1,0:T(8,128)S(1)}, s32[16,16,128]{2,1,0:T(8,128)}, u32[]{:S(2)}) copy-start(s32[16,16,128]{2,1,0:T(8,128)} %mask.3) | copy-start | bytes 393220
  11.0 10.7 %collective-permute-start.4 = (f32[272,128]{1,0:T(8,128)S(1)}, f32[272,128]{1,0:T(8,128)S(1)}, u32[]{:S(2)}, u32[]{:S(2)}) collective-permute-start(f32[272,128]{1,0:T(8,128)S(1)} %get-tuple-element.34.ahead.rest_0_), channel_id=1, source_target_pairs={{0,4},{8,12},{16,20},{24,28},{4,0},{12,8},{20,16},{28,24},{1,5},{9... | collective-permute-start | bytes 417800 | tf_op jit(solution)/shard_map/ppermute | solution.py:105
  12.2 9.5 %collective-permute-start.5 = (f32[272,128]{1,0:T(8,128)S(1)}, f32[272,128]{1,0:T(8,128)S(1)}, u32[]{:S(2)}, u32[]{:S(2)}) collective-permute-start(f32[272,128]{1,0:T(8,128)S(1)} %pack_odd.1.rest_1_), channel_id=1, source_target_pairs={{4,8},{12,16},{20,24},{8,4},{16,12},{24,20},{5,9},{13,17},{21,25},... | collective-permute-start | bytes 417800 | tf_op jit(solution)/shard_map/ppermute | solution.py:105
  15.3 6.0 %collective-permute-start.3 = (f32[16,16,128]{2,1,0:T(8,128)S(1)}, f32[16,16,128]{2,1,0:T(8,128)S(1)}, u32[]{:S(2)}, u32[]{:S(2)}) collective-permute-start(f32[16,16,128]{2,1,0:T(8,128)S(1)} %collective-permute-done.2.beyond), channel_id=1, source_target_pairs={{12,4},{20,12},{28,20},{0,8},{8,16},{16,24},{13,5},{21,13},{29,21}... | collective-permute-start | bytes 393224 | tf_op jit(solution)/shard_map/ppermute | solution.py:110
  18.8 2.9 %copy-start.2 = (f32[4,128,128]{2,1,0:T(8,128)S(1)}, f32[4,128,128]{2,1,0:T(8,128)}, u32[]{:S(2)}) copy-start(f32[4,128,128]{2,1,0:T(8,128)} %constant.5.clone.weights) | copy-start | bytes 786436
  22.4 4.3 %collective-permute-start.6 = (f32[16,8,128]{2,1,0:T(8,128)S(1)}, f32[16,8,128]{2,1,0:T(8,128)S(1)}, u32[]{:S(2)}, u32[]{:S(2)}) collective-permute-start(f32[16,8,128]{2,1,0:T(8,128)S(1)} %get-tuple-element.37), channel_id=1, source_target_pairs={{0,2},{2,0},{1,3},{3,1},{4,6},{6,4},{5,7},{7,5},{8,10},{10,8},{9,1... | collective-permute-start | bytes 196616 | tf_op jit(solution)/shard_map/ppermute | solution.py:105
  26.9 1.4 %collective-permute-start.7 = (f32[16,16,128]{2,1,0:T(8,128)S(1)}, f32[16,16,128]{2,1,0:T(8,128)S(1)}, u32[]{:S(2)}, u32[]{:S(2)}) collective-permute-start(f32[16,16,128]{2,1,0:T(8,128)S(1)} %smooth_y.1.field), channel_id=1, source_target_pairs={{0,1},{1,0},{2,3},{3,2},{4,5},{5,4},{6,7},{7,6},{8,9},{9,8},{10,11... | collective-permute-start | bytes 393224 | tf_op jit(solution)/shard_map/ppermute | solution.py:105

commit v4 on v3

--- a/solution.py
+++ b/solution.py
@@ -246,7 +246,7 @@
     rest = iter(rest)
     flow_ref, factor = next(rest), next(rest)
     outs = [next(rest) for _ in range(1 + many_z)]
-    rising, falling, members_ref, sems = rest
+    rising, falling, straight, members_ref, sems = rest
     pz = parity_of("gz")
     part = X // 4
     copies = [
@@ -273,17 +273,11 @@
             return here
         return jnp.where(lane == (Z - 1 if cz > 0 else 0), zero, pltpu.roll(here, (-cz) % Z, 1))
 
-    def layer(x, _):
-        members = [members_ref[q, x] for q in range(Q)]
-        inverse = 1.0 / sum(members[1:], members[0])
-        vel = [
-            signed([(velocity[q][a], members[q] - members[q + 1]) for q in range(1, Q, 2) if velocity[q][a] != 0])
-            * inverse
-            for a in range(3)
-        ]
-        for a in range(3):
-            flow_ref[a, x] = vel[a]
-        flow_ref[3, x] = inverse
+    for a in range(3):
+        rising[a, X] = zero
+        falling[a, 1] = zero
+
+    def moments(x, _):
         groups = {}
         for q in range(1, Q):
             groups.setdefault(velocity[q][0], {})[q] = both(q, x)
@@ -291,24 +285,26 @@
         for a in range(3):
             rising[a, x] = up[a]
             falling[a, x + 2] = down[a]
-        factor[x] = vel[0] * vel[0] + vel[1] * vel[1] + vel[2] * vel[2] - vel[1] * level[1] - vel[2] * level[2]
+        for a in range(1, 3):
+            straight[a - 1, x] = level[a]
         return 0
 
-    for a in range(3):
-        rising[a, X] = zero
-        falling[a, 1] = zero
-    for i, c in enumerate(copies):
-        c.wait()
-        lax.fori_loop(i * part, (i + 1) * part, layer, 0)
-
-    def finish(x, _):
-        total = factor[x]
+    def layer(x, _):
+        members = [members_ref[q, x] for q in range(Q)]
+        inverse = 1.0 / sum(members[1:], members[0])
+        total = None
         for a in range(3):
-            total = total - flow_ref[a, x] * (rising[a, x + 1] + falling[a, x + 1])
+            terms = [(velocity[q][a], members[q] - members[q + 1]) for q in range(1, Q, 2) if velocity[q][a] != 0]
+            vel = signed(terms) * inverse
+            flow_ref[a, x] = vel
+            moment = rising[a, x + 1] + falling[a, x + 1]
+            if a > 0:
+                moment = moment + straight[a - 1, x]
+            term = vel * (vel - moment)
+            total = term if total is None else total + term
+        flow_ref[3, x] = inverse
         factor[x] = total
         return 0
-
-    lax.fori_loop(0, X, finish, 0, unroll=4)
 
     def fill(out, up):
         names = (MINUS if up else PLUS)[2]
@@ -323,9 +319,13 @@
 
         lax.fori_loop(0, X, face, 0, unroll=2)
 
+    lax.fori_loop(0, X, moments, 0, unroll=2)
     for n, out in enumerate(outs):
         pl.when(pz == n)(functools.partial(fill, out, True))
         pl.when(pz != n)(functools.partial(fill, out, False))
+    for i, c in enumerate(copies):
+        c.wait()
+        lax.fori_loop(i * part, (i + 1) * part, layer, 0, unroll=2)
 
 
 def slot_of(Z, up, j):
@@ -436,8 +436,7 @@
     X, Y, Z = dims
     rest = iter(rest)
     y_even, y_odd = refs_of(rest, many_y)
-    smooth, out, again = rest
-    again[...] = filtered_y[...]
+    smooth, out = rest
     smooth[...] = dot(flat(dims, filtered_y), weights[0])
     out[...] = factor[...]
     py = parity_of("gy")
@@ -575,64 +574,88 @@
     return jnp.where(pz == n, (R * x) % Z, (R * x + R) % Z)
 
 
-def source(dims, many_x, many_y, many_z, weights, partial, factor, flow_ref, *rest):
+def half_source(dims, above, near, many_z, pz, weights, partial, relayed, factor, flow_ref, own, got, smooth, ext, damp, base, result):
+    X, Y, Z = dims
+    if near:
+        layers = range(2 * R, X + 2 * R) if above else range(X)
+    else:
+        layers = range(X, X + 2 * R) if above else range(2 * R)
+    u_at, v_at, d_at = R * Y, R * Y + 5 * Y, R * Y + 8 * Y
+    for e in layers:
+        total = partial[e]
+        if relayed is not None:
+            for tap, i in taps_of(X, above, e):
+                total = total + tap * relayed[i * Y : (i + 1) * Y, :]
+        smooth[e] = total
+        if R <= e < R + X:
+            ext[e] = factor[e - R]
+        elif got is None:
+            ext[e] = jnp.zeros((Y, Z), jnp.float32)
+        else:
+            at = (e - R - X if above else e) * Y
+            ext[e] = got[at : at + Y, :]
+    if got is not None:
+        lane = lax.broadcasted_iota(jnp.int32, (Y, Z), 1)
+        for n in range(1 + many_z):
+            above_z = jnp.where(pz == n, 1, 0)
+            value = dot(got[d_at + n * Y : d_at + (n + 1) * Y, :], weights[2 * int(above) + above_z])
+            first = (Z - R) * above_z
+            there = (lane >= first) & (lane < first + R)
+            for i in range(X):
+                e = i + X * int(above)
+                moved = pltpu.roll(value, lax.rem(first + Z - R * i, Z), 1)
+                smooth[e] = smooth[e] + jnp.where(there, moved, 0.0)
+
+        def moment(ref, names):
+            return moment_of({q: ref[u_at + j * Y : u_at + (j + 1) * Y, :] for j, q in enumerate(names)})
+
+        def less(e, vel, m):
+            ext[e] = ext[e] - (vel[0] * m[0] + vel[1] * m[1] + vel[2] * m[2])
+
+        inner, outer = (R + X - 1, R + X) if above else (R, R - 1)
+        there, here = (PLUS[0], MINUS[0]) if above else (MINUS[0], PLUS[0])
+        less(inner, [flow_ref[a, inner - R] for a in range(3)], moment(got, there))
+        less(outer, [got[v_at + a * Y : v_at + (a + 1) * Y, :] for a in range(3)], moment(own, here))
+    slope = -damping_max * ramp_shape * (1.0 + ramp_shape)
+    for e in layers:
+        physical, steep, inverse = project(smooth[e])
+        ext[e] = (slope * steep) * (inverse * inverse) * ext[e]
+        if R <= e < R + X:
+            damp[e - R] = (2.0 * damping_max * ramp_shape) * (1.0 - physical) * inverse
+    for x in range(X):
+        terms = [TAPS[e - x] * ext[e] for e in layers if 0 <= e - x <= 2 * R]
+        if base is not None:
+            terms = [base[x]] + terms
+        result[x] = sum(terms[1:], terms[0]) if terms else jnp.zeros((Y, Z), jnp.float32)
+
+
+def near_x(dims, many_z, weights, partial, factor, flow_ref, own, got, result, damp, smooth, ext):
+    px, pz = parity_of("gx"), parity_of("gz")
+    for parity in range(2):
+        pl.when(px == parity)(
+            functools.partial(
+                half_source, dims, parity == 0, True, many_z, pz, weights, partial, None, factor, flow_ref,
+                own, got, smooth, ext, damp, None, result,
+            )
+        )
+
+
+def source(dims, many_x, many_y, many_z, weights, partial, factor, flow_ref, near, near_damp, *rest):
     X, Y, Z = dims
     rest = iter(rest)
-    own_even, own_odd = refs_of(rest, many_x)
-    x_even, x_odd = refs_of(rest, many_x)
+    own, got, relayed = (next(rest), next(rest), next(rest)) if many_x else (None, None, None)
     result, damp = next(rest), next(rest)
     outs = [next(rest) for _ in range(1 + many_y)]
     smooth, ext = rest
     px, py, pz = parity_of("gx"), parity_of("gy"), parity_of("gz")
-    u_at, v_at, d_at = R * Y, R * Y + 5 * Y, R * Y + 8 * Y
-
-    def got(at, count):
-        return sides(px, x_even[at : at + count, :], None if x_odd is None else x_odd[at : at + count, :])
-
-    def own(at, count):
-        return sides(px, own_even[at : at + count, :], None if own_odd is None else own_odd[at : at + count, :])
-
-    smooth[...] = partial[...]
-    lane = lax.broadcasted_iota(jnp.int32, (Y, Z), 1)
-    for odd, ref in enumerate([x_even, x_odd][: 1 + many_x]):
-        above_x = jnp.where(px == odd, 1, 0)
-        for n in range(1 + many_z):
-            above_z = jnp.where(pz == n, 1, 0)
-            value = dot(ref[d_at + n * Y : d_at + (n + 1) * Y, :], weights[2 * above_x + above_z])
-            first = (Z - R) * above_z
-            there = (lane >= first) & (lane < first + R)
-            for e in range(X):
-                at = e + X * above_x
-                moved = pltpu.roll(value, lax.rem(first + Z - R * e, Z), 1)
-                smooth[at] = smooth[at] + jnp.where(there, moved, 0.0)
-    low, high = got(0, R * Y)
-    ext[:R] = low.reshape(R, Y, Z)
-    ext[R : R + X] = factor[...]
-    ext[R + X :] = high.reshape(R, Y, Z)
-
-    def face_moment(block, names):
-        return moment_of({q: block[j * Y : (j + 1) * Y] for j, q in enumerate(names)})
-
-    def less(at, vel, moment):
-        ext[at] = ext[at] - (vel[0] * moment[0] + vel[1] * moment[1] + vel[2] * moment[2])
-
-    got_low, got_high = got(u_at, 5 * Y)
-    own_low, own_high = own(u_at, 5 * Y)
-    vel_low, vel_high = got(v_at, 3 * Y)
-    less(R - 1, [vel_low[a * Y : (a + 1) * Y] for a in range(3)], face_moment(own_low, PLUS[0]))
-    less(R, [flow_ref[a, 0] for a in range(3)], face_moment(got_low, MINUS[0]))
-    less(R + X - 1, [flow_ref[a, X - 1] for a in range(3)], face_moment(got_high, PLUS[0]))
-    less(R + X, [vel_high[a * Y : (a + 1) * Y] for a in range(3)], face_moment(own_high, MINUS[0]))
-
-    slope = -damping_max * ramp_shape * (1.0 + ramp_shape)
-    for e in range(X + 2 * R):
-        physical, steep, inverse = project(smooth[e])
-        ext[e] = (slope * steep) * (inverse * inverse) * ext[e]
-        if R <= e < R + X:
-            damp[e - R] = (2.0 * damping_max * ramp_shape) * (1.0 - physical) * inverse
-
-    for x in range(X):
-        result[x] = filter_rows(lambda k: ext[x + k])
+    damp[...] = near_damp[...]
+    for parity in range(2):
+        pl.when(px == parity)(
+            functools.partial(
+                half_source, dims, parity == 1, False, many_z, pz, weights, partial, relayed, factor, flow_ref,
+                own, got, smooth, ext, damp, near, result,
+            )
+        )
     for n, out in enumerate(outs):
 
         @pl.when(py == n)
@@ -714,12 +737,10 @@
     return vel[0] * vel[0] + vel[1] * vel[1] + vel[2] * vel[2]
 
 
-def far_x(dims, odd, weights, partial, beyond, out, smooth):
-    X, Y, Z = dims
-    smooth[...] = dot(flat(dims, beyond), weights[0])
+def far_x(dims, partial, beyond, out):
     px = parity_of("gx")
-    pl.when(px == odd)(lambda: add_side(dims, partial, smooth, 0, out, True))
-    pl.when(px != odd)(lambda: add_side(dims, partial, smooth, 0, out, False))
+    pl.when(px == 0)(lambda: add_side(dims, partial, beyond, 0, out, True))
+    pl.when(px != 0)(lambda: add_side(dims, partial, beyond, 0, out, False))
 
 
 def beside_x(dims, many_y, many_z, adj, flow_ref, mask, own, *rest):
@@ -824,7 +845,8 @@
         [f32(4, X, Y, Z)] + [f32(X, Y, Z)] * (2 + many_z),
         (to_y[0], in_hbm(forward), adjoint),
         vmem(1) + [hbm] + vmem(1),
-        [pltpu.VMEM((3, X + 2, Y, Z), jnp.float32)] * 2 + [pltpu.VMEM((Q, X, Y, Z), jnp.float32), dma((4,))],
+        [pltpu.VMEM((3, X + 2, Y, Z), jnp.float32)] * 2
+        + [pltpu.VMEM((2, X, Y, Z), jnp.float32), pltpu.VMEM((Q, X, Y, Z), jnp.float32), dma((4,))],
         limit=16,
         flops=200 * cells,
         moved=44 * 4 * cells,
@@ -842,15 +864,15 @@
     )
     got_z = some(exchange("gz", nz, *pair(to_z)))
 
-    smooth, factor, beyond = call(
+    smooth, factor = call(
         functools.partial(factor_y, dims, many_y),
-        [f32(X * Y, Z), f32(X, Y, Z), f32(X, Y, Z)],
+        [f32(X * Y, Z), f32(X, Y, Z)],
         (weights, filtered_y, flow_values, factor, *got_y),
         limit=8,
         flops=200 * cells,
         name="factor_y",
     )
-    beyond = swap(beyond, "gx", nx, 0)
+    beyond = swap(smooth, "gx", nx, 0)
 
     x_rows = R * Y + 8 * Y
     even, smooth, factor = call(
@@ -880,25 +902,36 @@
         moved=1000,
         name="beside_x",
     )
-    for odd, layers in enumerate([beyond] + ([relay(beyond, "gx", nx)] if many_x else [])):
-        (partial,) = call(
-            functools.partial(far_x, dims, odd),
-            [f32(X + 2 * R, Y, Z)],
-            (weights, partial, layers),
-            None,
-            [pltpu.VMEM((X * Y, Z), jnp.float32)],
-            limit=8,
-            flops=1000,
-            moved=1000,
-            name="far_odd" if odd else "far_even",
-        )
-
+    (partial,) = call(
+        functools.partial(far_x, dims),
+        [f32(X + 2 * R, Y, Z)],
+        (partial, beyond),
+        limit=8,
+        flops=1000,
+        moved=1000,
+        name="far_x",
+    )
+    relayed = [relay(beyond, "gx", nx)] if many_x else []
+
+    packed = jnp.asarray(packed_band(dims))
+    extended = pltpu.VMEM((X + 2 * R, Y, Z), jnp.float32)
+    near, near_damp = call(
+        functools.partial(near_x, dims, many_z),
+        [f32(X, Y, Z), f32(X, Y, Z)],
+        (packed, partial, factor, flow_values, to_x[0], got_x[0]),
+        None,
+        [extended] * 2,
+        limit=8,
+        flops=1000,
+        moved=1000,
+        name="near_x",
+    )
     result, damp, *to_y = call(
         functools.partial(source, dims, many_x, many_y, many_z),
         [f32(X, Y, Z), f32(X, Y, Z)] + [f32(X, R, Z)] * (1 + many_y),
-        (jnp.asarray(packed_band(dims)), partial, factor, flow_values, *to_x, *got_x),
+        (packed, partial, factor, flow_values, near, near_damp, *to_x[1:], *got_x[1:], *relayed),
         None,
-        [pltpu.VMEM((X + 2 * R, Y, Z), jnp.float32)] * 2,
+        [extended] * 2,
         limit=8,
         name="source",
     )

time: 29.4 us -> 28.8 us (0.980)
  Pallas kernels: 12.9 us -> 11.1 us
  starting transfers between devices: 11.3 us -> 11.9 us
  waiting for transfers between devices: 4.19 us -> 4.73 us
    pallas_call x14, Pallas kernels: 12.9 us -> 11.1 us  [call(): pl.pallas_call(body, out_shape=outs, in_specs=specs or vmem(len(args)), o...]
    ppermute x7, waiting for transfers between devices: 4.18 us -> 4.73 us  [swap(): return lax.ppermute(array, axis, pairs + [(b, a) for a, b in pairs])]
    ppermute x7, starting transfers between devices: 7.82 us -> 8.25 us  [swap(): return lax.ppermute(array, axis, pairs + [(b, a) for a, b in pairs])]
  transfers between devices with their start and end apart: 8 -> 8, of which waited for: 3 -> 4; matrix products, arithmetic and copies ran while one was open for 0% -> 0% of each run, Pallas kernels for 33% -> 28%
where the time goes in v4:
time: 28.8 us; the launch traced here: 28.6 us
  starting transfers between devices  11.9 us (41%)
  Pallas kernels  11.1 us (39%)
  waiting for transfers between devices  4.73 us (16%)
  between operations  0.82 us (3%)
    pallas_call x14, Pallas kernels, call(): pl.pallas_call(body, out_shape=outs, in_specs=specs or vmem(len(args)), o...  11.1 us
    ppermute x7, starting transfers between devices, swap(): return lax.ppermute(array, axis, pairs + [(b, a) for a, b in pairs])  8.25 us
    ppermute x7, waiting for transfers between devices, swap(): return lax.ppermute(array, axis, pairs + [(b, a) for a, b in pairs])  4.73 us
    ppermute x1, starting transfers between devices, relay(): return lax.ppermute(array, axis, pairs)  3.7 us
  transfers between devices with their start and end apart: 8, of which 4 were waited for; matrix products, arithmetic and copies ran while one was open for 0% of the time, Pallas kernels for 28%

profile of v4, /device:TPU:0, one launch (start us, length us, event | category | flops | bytes accessed | tf_op | source)
XLA Modules:
  0.0 28.6 jit_solution(7225317259652714676)
XLA Ops:
  0.6 1.3 %pack_y.1 = (f32[208,128]{1,0:T(8,128)S(1)}, f32[16,16,128]{2,1,0:T(8,128)S(1)}) custom-call(f32[19,16,16,128]{3,2,1,0:T(8,128)} %adj.11, f32[16,16,128]{2,1,0:T(8,128)} %design.1), custom_call_target="tpu_custom_call" | custom-call | flops 1000000 | bytes 1000000 | tf_op jit(solution)/shard_map/pack_y/pallas_call | solution.py:130
  1.9 0.0 copy-start.1
  1.9 3.0 %collective-permute-start = (f32[208,128]{1,0:T(8,128)S(1)}, f32[208,128]{1,0:T(8,128)S(1)}, u32[]{:S(2)}, u32[]{:S(2)}) collective-permute-start(f32[208,128]{1,0:T(8,128)S(1)} %get-tuple-element.21.ahead), channel_id=1, source_target_pairs={{0,2},{2,0},{1,3},{3,1},{4,6},{6,4},{5,7},{7,5},{8,10},{10,8},{9,1... | collective-permute-start | bytes 319496 | tf_op jit(solution)/shard_map/ppermute | solution.py:105
  5.0 2.0 %prepare.1 = (f32[4,16,16,128]{3,2,1,0:T(8,128)S(1)}, f32[16,16,128]{2,1,0:T(8,128)S(1)}, f32[16,16,128]{2,1,0:T(8,128)S(1)}) custom-call(f32[208,128]{1,0:T(8,128)S(1)} %get-tuple-element.21.ahead, f32[19,16,16,128]{3,2,1,0:T(8,128)} %forward.1, f32[19,16,16,128]{3,2,1,0:T(8,128)S(1)} %copy-done), custom_call_target="tpu_custom_call" | custom-call | flops 6553600 | bytes 5767168 | tf_op jit(solution)/shard_map/prepare/pallas_call | solution.py:130
  7.0 1.0 %collective-permute-done.rest_1_.rest_0_ = f32[208,128]{1,0:T(8,128)S(1)} collective-permute-done((f32[208,128]{1,0:T(8,128)S(1)}, f32[208,128]{1,0:T(8,128)S(1)}, u32[]{:S(2)}, u32[]{:S(2)}) %collective-permute-start) | collective-permute-done | bytes 106528 | tf_op jit(solution)/shard_map/ppermute | solution.py:105
  7.9 0.2 design_y.1
  8.2 0.1 collective-permute-start.1
  8.2 0.3 factor_y.1
  8.5 1.8 %collective-permute-start.2 = (f32[256,128]{1,0:T(8,128)S(1)}, f32[256,128]{1,0:T(8,128)S(1)}, u32[]{:S(2)}, u32[]{:S(2)}) collective-permute-start(f32[256,128]{1,0:T(8,128)S(1)} %get-tuple-element.27.smooth), channel_id=1, source_target_pairs={{0,4},{8,12},{16,20},{24,28},{4,0},{12,8},{20,16},{28,24},{1,5},{9... | collective-permute-start | bytes 393224 | tf_op jit(solution)/shard_map/ppermute | solution.py:105
  10.3 0.0 collective-permute-done.1.rest_1_
  10.3 0.5 %pack_x.1 = (f32[272,128]{1,0:T(8,128)S(1)}, f32[256,128]{1,0:T(8,128)S(1)}, f32[16,16,128]{2,1,0:T(8,128)S(1)}) custom-call(f32[19,16,16,128]{3,2,1,0:T(8,128)S(1)} %copy-done, f32[3,128,128]{2,1,0:T(8,128)S(1)} %copy-done.1, f32[256,128]{1,0:T(8,128)S(1)} %get-tuple-element.27.smooth, f32[16,16,128]{2,1,0:T(8,128)S(1)} %get-tuple-element.28.factor_in, ...), custom_call_target="tpu_custom_call" | custom-call | flops 1000000 | bytes 1000000 | tf_op jit(solution)/shard_map/pack_x/pallas_call | solution.py:130
  10.8 1.0 %collective-permute-start.3 = (f32[272,128]{1,0:T(8,128)S(1)}, f32[272,128]{1,0:T(8,128)S(1)}, u32[]{:S(2)}, u32[]{:S(2)}) collective-permute-start(f32[272,128]{1,0:T(8,128)S(1)} %get-tuple-element.34.own.ahead), channel_id=1, source_target_pairs={{0,4},{8,12},{16,20},{24,28},{4,0},{12,8},{20,16},{28,24},{1,5},{9... | collective-permute-start | bytes 417800 | tf_op jit(solution)/shard_map/ppermute | solution.py:105
  11.9 0.1 pack_odd.1.rest_0_
  12.0 0.7 %collective-permute-start.4 = (f32[272,128]{1,0:T(8,128)S(1)}, f32[272,128]{1,0:T(8,128)S(1)}, u32[]{:S(2)}, u32[]{:S(2)}) collective-permute-start(f32[272,128]{1,0:T(8,128)S(1)} %pack_odd.1.rest_0_), channel_id=1, source_target_pairs={{4,8},{12,16},{20,24},{8,4},{16,12},{24,20},{5,9},{13,17},{21,25},... | collective-permute-start | bytes 417800 | tf_op jit(solution)/shard_map/ppermute | solution.py:105
  12.6 2.2 %collective-permute-done.2.beyond = f32[256,128]{1,0:T(8,128)S(1)} collective-permute-done((f32[256,128]{1,0:T(8,128)S(1)}, f32[256,128]{1,0:T(8,128)S(1)}, u32[]{:S(2)}, u32[]{:S(2)}) %collective-permute-start.2) | collective-permute-done | bytes 131104 | tf_op jit(solution)/shard_map/ppermute | solution.py:105
  14.9 3.7 %collective-permute-start.5 = (f32[256,128]{1,0:T(8,128)S(1)}, f32[256,128]{1,0:T(8,128)S(1)}, u32[]{:S(2)}, u32[]{:S(2)}) collective-permute-start(f32[256,128]{1,0:T(8,128)S(1)} %collective-permute-done.2.beyond), channel_id=1, source_target_pairs={{12,4},{20,12},{28,20},{0,8},{8,16},{16,24},{13,5},{21,13},{29,21}... | collective-permute-start | bytes 393224 | tf_op jit(solution)/shard_map/ppermute | solution.py:110
  18.6 0.0 copy-start.2
  18.6 2.2 %beside_x.1 = (f32[32,16,128]{2,1,0:T(8,128)S(1)}, f32[19,16,16,128]{3,2,1,0:T(8,128)S(1)}) custom-call(f32[19,16,16,128]{3,2,1,0:T(8,128)S(1)} %copy-done, f32[4,16,16,128]{3,2,1,0:T(8,128)S(1)} %get-tuple-element.22.flow_ref, s32[16,16,128]{2,1,0:T(8,128)S(1)} %copy-done.3, f32[256,128]{1,0:T(8,128)S(1)} %get-tuple-element.30.own, ...), custom_call_target="tpu_custom_call" | custom-call | flops 3276800000 | bytes 1000 | tf_op jit(solution)/shard_map/beside_x/pallas_call | solution.py:130
  20.8 0.1 far_x.1.partial
  20.9 0.0 collective-permute-done.3.got.rest_2_
  20.9 0.4 %near_x.1 = (f32[16,16,128]{2,1,0:T(8,128)S(1)}, f32[16,16,128]{2,1,0:T(8,128)S(1)}) custom-call(f32[4,128,128]{2,1,0:T(8,128)S(1)} %copy-done.2, f32[32,16,128]{2,1,0:T(8,128)S(1)} %far_x.1.partial, f32[16,16,128]{2,1,0:T(8,128)S(1)} %get-tuple-element.33.factor, f32[4,16,16,128]{3,2,1,0:T(8,128)S(1)} %get-tuple-element.22.flow_ref, ...), custom_call_target="tpu_custom_call" | custom-call | flops 1000 | bytes 1000 | tf_op jit(solution)/shard_map/near_x/pallas_call | solution.py:130
  21.3 0.0 collective-permute-done.5.rest_2_
  21.4 0.0 collective-permute-done.4.rest_1_.rest_3_
  21.4 0.4 %source.1 = (f32[16,16,128]{2,1,0:T(8,128)S(1)}, f32[16,16,128]{2,1,0:T(8,128)S(1)}, f32[16,8,128]{2,1,0:T(8,128)S(1)}) custom-call(f32[4,128,128]{2,1,0:T(8,128)S(1)} %copy-done.2, f32[32,16,128]{2,1,0:T(8,128)S(1)} %far_x.1.partial, f32[16,16,128]{2,1,0:T(8,128)S(1)} %get-tuple-element.33.factor, f32[4,16,16,128]{3,2,1,0:T(8,128)S(1)} %get-tuple-element.22.flow_ref, ...), custom_call_target="tpu_custom_call" | custom-call | flops 1000000 | bytes 1000000 | tf_op jit(solution)/shard_map/source/pallas_call | solution.py:130
  21.8 1.6 %collective-permute-start.6 = (f32[16,8,128]{2,1,0:T(8,128)S(1)}, f32[16,8,128]{2,1,0:T(8,128)S(1)}, u32[]{:S(2)}, u32[]{:S(2)}) collective-permute-start(f32[16,8,128]{2,1,0:T(8,128)S(1)} %get-tuple-element.39), channel_id=1, source_target_pairs={{0,2},{2,0},{1,3},{3,1},{4,6},{6,4},{5,7},{7,5},{8,10},{10,8},{9,1... | collective-permute-start | bytes 196616 | tf_op jit(solution)/shard_map/ppermute | solution.py:105
  23.4 2.3 %collide.1.ahead = f32[19,16,16,128]{3,2,1,0:T(8,128)} custom-call(f32[19,16,16,128]{3,2,1,0:T(8,128)S(1)} %copy-done, f32[19,16,16,128]{3,2,1,0:T(8,128)S(1)} %get-tuple-element.31.base, f32[4,16,16,128]{3,2,1,0:T(8,128)S(1)} %get-tuple-element.22.flow_ref, f32[16,16,128]{2,1,0:T(8,128)S(1)} %get-tuple-element.37.damp, s32[16,16,128]{2,1,0:T(8,128)S(1)} %copy-done.3, ...), custom_call_target="tpu_custom_call" | custom-call | flops 9830400 | bytes 5767168 | tf_op jit(solution)/shard_map/collide/pallas_call | solution.py:130
  25.7 0.4 %collective-permute-done.6.rest_0_ = f32[16,8,128]{2,1,0:T(8,128)S(1)} collective-permute-done((f32[16,8,128]{2,1,0:T(8,128)S(1)}, f32[16,8,128]{2,1,0:T(8,128)S(1)}, u32[]{:S(2)}, u32[]{:S(2)}) %collective-permute-start.6) | collective-permute-done | bytes 65568 | tf_op jit(solution)/shard_map/ppermute | solution.py:105
  26.1 0.1 smooth_y.1.field
  26.3 0.1 collective-permute-start.7
  26.4 0.3 own_z.1.own
  26.6 1.1 %collective-permute-done.7.rest_0_ = f32[16,16,128]{2,1,0:T(8,128)S(1)} collective-permute-done((f32[16,16,128]{2,1,0:T(8,128)S(1)}, f32[16,16,128]{2,1,0:T(8,128)S(1)}, u32[]{:S(2)}, u32[]{:S(2)}) %collective-permute-start.7) | collective-permute-done | bytes 131104 | tf_op jit(solution)/shard_map/ppermute | solution.py:105
  27.7 0.9 %smooth_z.1 = f32[16,16,128]{2,1,0:T(8,128)} custom-call(f32[3,128,128]{2,1,0:T(8,128)S(1)} %copy-done.1, f32[256,128]{1,0:T(8,128)S(1)} %own_z.1.own, f32[16,16,128]{2,1,0:T(8,128)S(1)} %collective-permute-done.7.rest_0_), custom_call_target="tpu_custom_call" | custom-call | flops 1000000 | bytes 1000000 | tf_op jit(solution)/shard_map/smooth_z/pallas_call | solution.py:130
  (6 shorter events, 0.0 us)
Async XLA Ops:
  0.6 4.3 %copy-start = (f32[19,16,16,128]{3,2,1,0:T(8,128)S(1)}, f32[19,16,16,128]{3,2,1,0:T(8,128)}, u32[]{:S(2)}) copy-start(f32[19,16,16,128]{3,2,1,0:T(8,128)} %adj.11) | copy-start | bytes 7471108
  1.9 6.3 %copy-start.1 = (f32[3,128,128]{2,1,0:T(8,128)S(1)}, f32[3,128,128]{2,1,0:T(8,128)}, u32[]{:S(2)}) copy-start(f32[3,128,128]{2,1,0:T(8,128)} %constant.4.clone.weights) | copy-start | bytes 589828
  1.9 6.0 %collective-permute-start = (f32[208,128]{1,0:T(8,128)S(1)}, f32[208,128]{1,0:T(8,128)S(1)}, u32[]{:S(2)}, u32[]{:S(2)}) collective-permute-start(f32[208,128]{1,0:T(8,128)S(1)} %get-tuple-element.21.ahead), channel_id=1, source_target_pairs={{0,2},{2,0},{1,3},{3,1},{4,6},{6,4},{5,7},{7,5},{8,10},{10,8},{9,1... | collective-permute-start | bytes 319496 | tf_op jit(solution)/shard_map/ppermute | solution.py:105
  8.2 2.1 %collective-permute-start.1 = (f32[16,16,128]{2,1,0:T(8,128)S(1)}, f32[16,16,128]{2,1,0:T(8,128)S(1)}, u32[]{:S(2)}, u32[]{:S(2)}) collective-permute-start(f32[16,16,128]{2,1,0:T(8,128)S(1)} %get-tuple-element.29), channel_id=1, source_target_pairs={{0,1},{1,0},{2,3},{3,2},{4,5},{5,4},{6,7},{7,6},{8,9},{9,8},{10,11... | collective-permute-start | bytes 393224 | tf_op jit(solution)/shard_map/ppermute | solution.py:105
  8.5 6.4 %collective-permute-start.2 = (f32[256,128]{1,0:T(8,128)S(1)}, f32[256,128]{1,0:T(8,128)S(1)}, u32[]{:S(2)}, u32[]{:S(2)}) collective-permute-start(f32[256,128]{1,0:T(8,128)S(1)} %get-tuple-element.27.smooth), channel_id=1, source_target_pairs={{0,4},{8,12},{16,20},{24,28},{4,0},{12,8},{20,16},{28,24},{1,5},{9... | collective-permute-start | bytes 393224 | tf_op jit(solution)/shard_map/ppermute | solution.py:105
  10.8 7.7 %copy-start.3 = (s32[16,16,128]{2,1,0:T(8,128)S(1)}, s32[16,16,128]{2,1,0:T(8,128)}, u32[]{:S(2)}) copy-start(s32[16,16,128]{2,1,0:T(8,128)} %mask.3) | copy-start | bytes 393220
  10.8 10.1 %collective-permute-start.3 = (f32[272,128]{1,0:T(8,128)S(1)}, f32[272,128]{1,0:T(8,128)S(1)}, u32[]{:S(2)}, u32[]{:S(2)}) collective-permute-start(f32[272,128]{1,0:T(8,128)S(1)} %get-tuple-element.34.own.ahead), channel_id=1, source_target_pairs={{0,4},{8,12},{16,20},{24,28},{4,0},{12,8},{20,16},{28,24},{1,5},{9... | collective-permute-start | bytes 417800 | tf_op jit(solution)/shard_map/ppermute | solution.py:105
  12.0 9.4 %collective-permute-start.4 = (f32[272,128]{1,0:T(8,128)S(1)}, f32[272,128]{1,0:T(8,128)S(1)}, u32[]{:S(2)}, u32[]{:S(2)}) collective-permute-start(f32[272,128]{1,0:T(8,128)S(1)} %pack_odd.1.rest_0_), channel_id=1, source_target_pairs={{4,8},{12,16},{20,24},{8,4},{16,12},{24,20},{5,9},{13,17},{21,25},... | collective-permute-start | bytes 417800 | tf_op jit(solution)/shard_map/ppermute | solution.py:105
  14.9 6.5 %collective-permute-start.5 = (f32[256,128]{1,0:T(8,128)S(1)}, f32[256,128]{1,0:T(8,128)S(1)}, u32[]{:S(2)}, u32[]{:S(2)}) collective-permute-start(f32[256,128]{1,0:T(8,128)S(1)} %collective-permute-done.2.beyond), channel_id=1, source_target_pairs={{12,4},{20,12},{28,20},{0,8},{8,16},{16,24},{13,5},{21,13},{29,21}... | collective-permute-start | bytes 393224 | tf_op jit(solution)/shard_map/ppermute | solution.py:110
  18.6 2.3 %copy-start.2 = (f32[4,128,128]{2,1,0:T(8,128)S(1)}, f32[4,128,128]{2,1,0:T(8,128)}, u32[]{:S(2)}) copy-start(f32[4,128,128]{2,1,0:T(8,128)} %constant.5.clone.weights) | copy-start | bytes 786436
  21.8 4.3 %collective-permute-start.6 = (f32[16,8,128]{2,1,0:T(8,128)S(1)}, f32[16,8,128]{2,1,0:T(8,128)S(1)}, u32[]{:S(2)}, u32[]{:S(2)}) collective-permute-start(f32[16,8,128]{2,1,0:T(8,128)S(1)} %get-tuple-element.39), channel_id=1, source_target_pairs={{0,2},{2,0},{1,3},{3,1},{4,6},{6,4},{5,7},{7,5},{8,10},{10,8},{9,1... | collective-permute-start | bytes 196616 | tf_op jit(solution)/shard_map/ppermute | solution.py:105
  26.3 1.4 %collective-permute-start.7 = (f32[16,16,128]{2,1,0:T(8,128)S(1)}, f32[16,16,128]{2,1,0:T(8,128)S(1)}, u32[]{:S(2)}, u32[]{:S(2)}) collective-permute-start(f32[16,16,128]{2,1,0:T(8,128)S(1)} %smooth_y.1.field), channel_id=1, source_target_pairs={{0,1},{1,0},{2,3},{3,2},{4,5},{5,4},{6,7},{7,6},{8,9},{9,8},{10,11... | collective-permute-start | bytes 393224 | tf_op jit(solution)/shard_map/ppermute | solution.py:105

commit v5 on v4

--- a/solution.py
+++ b/solution.py
@@ -89,6 +89,19 @@
     return out.reshape(4, Z, Z)
 
 
+def packed_band_z(dims):
+    X, Y, Z = dims
+    out = np.zeros((2, Z, Z), np.float32)
+    for above in range(2):
+        for i in range(X):
+            for z in range(R):
+                for j in range(R):
+                    k = j - z + 2 * R * above
+                    if 0 <= k <= 2 * R:
+                        out[above, i * R + j, i * R + z] = TAPS[k]
+    return out
+
+
 def sides(parity, even, odd):
     zero = jnp.zeros_like(even)
     if odd is None:
@@ -108,6 +121,16 @@
 def relay(array, axis, count):
     pairs = [(i + 2, i) for i in range(1, count - 2, 2)] + [(i - 2, i) for i in range(2, count, 2)]
     return lax.ppermute(array, axis, pairs)
+
+
+def swap_corner(array, counts, first_y, first_z):
+    ny, nz = counts
+    pairs = []
+    for a in range(first_y, ny - 1, 2):
+        for c in range(first_z, nz - 1, 2):
+            for d, e in ((c, c + 1), (c + 1, c)):
+                pairs += [(a * nz + d, (a + 1) * nz + e), ((a + 1) * nz + e, a * nz + d)]
+    return lax.ppermute(array, ("gy", "gz"), pairs)
 
 
 def exchange(axis, count, even, odd):
@@ -598,7 +621,7 @@
         lane = lax.broadcasted_iota(jnp.int32, (Y, Z), 1)
         for n in range(1 + many_z):
             above_z = jnp.where(pz == n, 1, 0)
-            value = dot(got[d_at + n * Y : d_at + (n + 1) * Y, :], weights[2 * int(above) + above_z])
+            value = dot(got[d_at + n * Y : d_at + (n + 1) * Y, :], weights[3 + 2 * int(above) + above_z])
             first = (Z - R) * above_z
             there = (lane >= first) & (lane < first + R)
             for i in range(X):
@@ -667,11 +690,31 @@
             out[...] = result[:, :R, :]
 
 
-def smooth_y(dims, many_y, ahead, own, *rest):
+def pack_corner(dims, many_y, many_z, own, *outs):
+    X, Y, Z = dims
+    outs = iter(outs)
+    to_z = [next(outs) for _ in range(1 + many_z)]
+    py, pz = parity_of("gy"), parity_of("gz")
+    lane = lax.broadcasted_iota(jnp.int32, (Y, Z), 1)
+    for n, out in enumerate(to_z):
+        value = jnp.zeros((Y, Z), jnp.float32)
+        for x in range(X):
+            shift = jnp.where(pz == n, (R * x + R) % Z, (R * x) % Z)
+            there = (lane >= R * x) & (lane < R * (x + 1))
+            value = jnp.where(there, pltpu.roll(own[x], shift, 1), value)
+        out[...] = value
+    for m in range(1 + many_y):
+        for ref in to_z:
+            next(outs)[...] = jnp.where(py == m, ref[Y - R :, :], ref[:R, :])
+
+
+def smooth_yz(dims, many_y, ahead, weights, own, *rest):
+    X, Y, Z = dims
     rest = iter(rest)
-    y_even, y_odd = refs_of(rest, many_y)
+    rows = [next(rest) for _ in range(1 + many_y)]
     result, pad = rest
-    extend_y(dims, pad, own[...], parity_of("gy"), y_even[...], None if y_odd is None else y_odd[...])
+    rows = [dot(ref[...].reshape(X * R, Z), weights[0]).reshape(X, R, Z) for ref in rows]
+    extend_y(dims, pad, own[...].reshape(X, Y, Z), parity_of("gy"), rows[0], rows[1] if many_y else None)
 
     def store(x, value):
         result[x : x + value.shape[0]] = value
@@ -679,12 +722,37 @@
     filter_y(dims, pad, store)
 
 
-def smooth_z(dims, many_z, weights, own, *rest):
+def add_halo(dims, many_y, many_z, weights, own, *rest):
+    X, Y, Z = dims
     rest = iter(rest)
-    z_even, z_odd = refs_of(rest, many_z)
-    (result,) = rest
-    value = own[...] + halo_z(weights, parity_of("gz"), flat(dims, z_even), flat(dims, z_odd))
-    result[...] = value.reshape(dims)
+    sides_z = [next(rest) for _ in range(1 + many_z)]
+    corners = [[next(rest) for _ in range(1 + many_z)] for _ in range(1 + many_y)]
+    out, pad, result, sems = rest
+    py, pz = parity_of("gy"), parity_of("gz")
+    lane = lax.broadcasted_iota(jnp.int32, (Y, Z), 1)
+    moved = []
+    for n in range(1 + many_z):
+        below, above = sides(py, corners[0][n][...], corners[1][n][...] if many_y else None)
+        pad[:R, :] = below
+        pad[R : R + Y, :] = sides_z[n][...]
+        pad[R + Y :, :] = above
+        side = jnp.where(pz == n, 1, 0)
+        first = (Z - R) * side
+        extra = dot(filter_rows(lambda k: pad[k : k + Y, :]), weights[7 + side])
+        moved.append((extra, first, (lane >= first) & (lane < first + R)))
+    part = X // 4
+    copies = []
+    for i in range(4):
+        for x in range(i * part, (i + 1) * part):
+            value = own[x]
+            for extra, first, there in moved:
+                value = value + jnp.where(there, pltpu.roll(extra, lax.rem(first + Z - R * x, Z), 1), 0.0)
+            result[x] = value
+        here = pl.ds(i * part, part)
+        copies.append(pltpu.make_async_copy(result.at[here], out.at[here], sems.at[i]))
+        copies[-1].start()
+    for c in copies:
+        c.wait()
 
 
 def relax(pulled, vel, speed_sq, label, drag, store):
@@ -774,26 +842,23 @@
     y_even, y_odd = refs_of(rest, many_y)
     z_even, z_odd = refs_of(rest, many_z)
     x_even, x_odd = refs_of(rest, many_x)
-    (out,) = rest
+    target, out, sems = rest
     px, py, pz = parity_of("gx"), parity_of("gy"), parity_of("gz")
     pull = Pull(adj, dims, py, y_even, y_odd, pz, z_even, z_odd)
-    begin = pl.program_id(0) * step
     u_at = R * Y
 
-    def layer(i, _):
-        x = begin + i
+    def layer(x):
         vel = [flow_ref[a, x] for a in range(3)]
         drag = jnp.where(mask[x] == 0, damp[x] * flow_ref[3, x], 0.0)
         level = drag * square(vel)
         tilt = [drag * v for v in vel]
-        out[0, i] = base[0, x] - level
+        out[0, x] = base[0, x] - level
         for q in range(1, Q, 2):
             lean = lean_of(q, tilt)
-            out[q, i] = base[q, x] + (lean - level)
-            out[q + 1, i] = base[q + 1, x] - (lean + level)
-        return 0
-
-    def edge(x, i, toward):
+            out[q, x] = base[q, x] + (lean - level)
+            out[q + 1, x] = base[q + 1, x] - (lean + level)
+
+    def edge(x, toward):
         around = {c: pull.faces(x + c) for c in (0, -toward)}
         pulled = []
         for q in range(Q):
@@ -807,13 +872,25 @@
         vel = [flow_ref[a, x] for a in range(3)]
 
         def store(q, value):
-            out[q, i] = value
+            out[q, x] = value
 
         relax(pulled, vel, square(vel), mask[x], damp[x] * flow_ref[3, x], store)
 
-    lax.fori_loop(0, step, layer, 0, unroll=2)
-    pl.when(pl.program_id(0) == 0)(lambda: edge(0, 0, -1))
-    pl.when(pl.program_id(0) == X // step - 1)(lambda: edge(X - 1, step - 1, 1))
+    last = X // step - 1
+    copies = []
+    for part in [1, 0, 2, last, *range(3, last)]:
+        for x in range(part * step, (part + 1) * step):
+            if x == 0:
+                edge(x, -1)
+            elif x == X - 1:
+                edge(x, 1)
+            else:
+                layer(x)
+        here = pl.ds(part * step, step)
+        copies.append(pltpu.make_async_copy(out.at[:, here], target.at[:, here], sems.at[part]))
+        copies[-1].start()
+    for c in copies:
+        c.wait()
 
 
 def local(counts, forward, adjoint, design, mask):
@@ -821,7 +898,7 @@
     nx, ny, nz = counts
     dims = design.shape
     X, Y, Z = dims
-    weights = jnp.asarray(band(Z))
+    weights = jnp.asarray(np.concatenate([band(Z), packed_band(dims), packed_band_z(dims)]))
     hbm = pl.BlockSpec(memory_space=pltpu.HBM)
     cells = X * Y * Z
     some = lambda pair: [v for v in pair if v is not None]
@@ -913,12 +990,11 @@
     )
     relayed = [relay(beyond, "gx", nx)] if many_x else []
 
-    packed = jnp.asarray(packed_band(dims))
     extended = pltpu.VMEM((X + 2 * R, Y, Z), jnp.float32)
     near, near_damp = call(
         functools.partial(near_x, dims, many_z),
         [f32(X, Y, Z), f32(X, Y, Z)],
-        (packed, partial, factor, flow_values, to_x[0], got_x[0]),
+        (weights, partial, factor, flow_values, to_x[0], got_x[0]),
         None,
         [extended] * 2,
         limit=8,
@@ -929,7 +1005,7 @@
     result, damp, *to_y = call(
         functools.partial(source, dims, many_x, many_y, many_z),
         [f32(X, Y, Z), f32(X, Y, Z)] + [f32(X, R, Z)] * (1 + many_y),
-        (packed, partial, factor, flow_values, near, near_damp, *to_x[1:], *got_x[1:], *relayed),
+        (weights, partial, factor, flow_values, near, near_damp, *to_x[1:], *got_x[1:], *relayed),
         None,
         [extended] * 2,
         limit=8,
@@ -937,45 +1013,62 @@
     )
     got_y2 = some(exchange("gy", ny, *pair(to_y)))
 
-    step = 4
-    whole = pl.BlockSpec(memory_space=pltpu.VMEM)
-    adjoint_next = call(
+    step = 2
+    (adjoint_next,) = call(
         functools.partial(collide, dims, many_x, many_y, many_z, step),
-        f32(Q, X, Y, Z),
+        [f32(Q, X, Y, Z)],
         (adjoint, base, flow_values, damp, mask, *got_y, *got_z, *got_x),
-        [whole] * (5 + len(got_y) + len(got_z) + len(got_x)),
-        out_specs=pl.BlockSpec((Q, step, Y, Z), lambda i: (0, i, 0, 0)),
-        grid=(X // step,),
-        limit=16,
+        None,
+        [pltpu.VMEM((Q, X, Y, Z), jnp.float32), dma((X // step,))],
+        out_specs=(hbm,),
+        limit=8,
         flops=300 * cells,
         moved=44 * 4 * cells,
         name="collide",
     )
 
-    (filtered_xy,) = call(
-        functools.partial(smooth_y, dims, many_y),
-        [f32(X, Y, Z)],
-        (in_hbm(adjoint_next), result, *got_y2),
-        [hbm] + vmem(1 + len(got_y2)),
-        [pltpu.VMEM((X, Y + 2 * R, Z), jnp.float32)],
+    packs = call(
+        functools.partial(pack_corner, dims, many_y, many_z),
+        [f32(Y, Z)] * (1 + many_z) + [f32(R, Z)] * ((1 + many_y) * (1 + many_z)),
+        (result,),
         limit=4,
-        name="smooth_y",
-    )
-    got_z2 = some(exchange("gz", nz, filtered_xy, filtered_xy if many_z else None))
+        flops=1000,
+        moved=1000,
+        name="pack_corner",
+    )
+    got_z2 = some(exchange("gz", nz, *pair(packs[: 1 + many_z])))
+    corners = [
+        swap_corner(packs[(1 + m) * (1 + many_z) + n], (ny, nz), m, n)
+        for m in range(1 + many_y)
+        for n in range(1 + many_z)
+    ]
     (own,) = call(
         functools.partial(own_z, dims),
         [f32(X * Y, Z)],
-        (weights, filtered_xy),
+        (weights, result),
         limit=4,
-        flops=200 * cells,
+        flops=1000,
+        moved=1000,
         name="own_z",
     )
+    (smooth,) = call(
+        functools.partial(smooth_yz, dims, many_y),
+        [f32(X, Y, Z)],
+        (in_hbm(adjoint_next), weights, own, *got_y2),
+        [hbm] + vmem(2 + len(got_y2)),
+        [pltpu.VMEM((X, Y + 2 * R, Z), jnp.float32)],
+        limit=4,
+        name="smooth_yz",
+    )
     (sensitivity,) = call(
-        functools.partial(smooth_z, dims, many_z),
+        functools.partial(add_halo, dims, many_y, many_z),
         [f32(X, Y, Z)],
-        (weights, own, *got_z2),
+        (weights, smooth, *got_z2, *corners),
+        None,
+        [pltpu.VMEM((Y + 2 * R, Z), jnp.float32), pltpu.VMEM((X, Y, Z), jnp.float32), dma((4,))],
+        out_specs=(hbm,),
         limit=4,
-        name="smooth_z",
+        name="add_halo",
     )
     return adjoint_next, sensitivity
 

time: 28.8 us -> 28 us (0.972)
  waiting for transfers between devices: 4.73 us -> 3.38 us
  starting transfers between devices: 11.9 us -> 12.6 us
  Pallas kernels: 11.1 us -> 10.8 us
    ppermute x7, waiting for transfers between devices: 4.73 us -> 3.21 us  [swap(): return lax.ppermute(array, axis, pairs + [(b, a) for a, b in pairs])]
    ppermute x0 -> x1, starting transfers between devices: none -> 0.61 us  [swap_corner(): return lax.ppermute(array, ('gy', 'gz'), pairs)]
    pallas_call x14 -> x15, Pallas kernels: 11.1 us -> 10.8 us  [call(): pl.pallas_call(body, out_shape=outs, in_specs=specs or vmem(len(args)), o...]
  transfers between devices with their start and end apart: 8 -> 9, of which waited for: 4 -> 3; matrix products, arithmetic and copies ran while one was open for 0% -> 0% of each run, Pallas kernels for 28% -> 29%
where the time goes in v5:
time: 28 us; the launch traced here: 27.6 us
  starting transfers between devices  12.6 us (45%)
  Pallas kernels  10.8 us (39%)
  waiting for transfers between devices  3.38 us (12%)
  between operations  0.82 us (3%)
    pallas_call x15, Pallas kernels, call(): pl.pallas_call(body, out_shape=outs, in_specs=specs or vmem(len(args)), o...  10.8 us
    ppermute x7, starting transfers between devices, swap(): return lax.ppermute(array, axis, pairs + [(b, a) for a, b in pairs])  8.26 us
    ppermute x1, starting transfers between devices, relay(): return lax.ppermute(array, axis, pairs)  3.69 us
    ppermute x7, waiting for transfers between devices, swap(): return lax.ppermute(array, axis, pairs + [(b, a) for a, b in pairs])  3.21 us
    ppermute x1, starting transfers between devices, swap_corner(): return lax.ppermute(array, ('gy', 'gz'), pairs)  0.61 us
  transfers between devices with their start and end apart: 9, of which 3 were waited for; matrix products, arithmetic and copies ran while one was open for 0% of the time, Pallas kernels for 29%

profile of v5, /device:TPU:0, one launch (start us, length us, event | category | flops | bytes accessed | tf_op | source)
XLA Modules:
  0.0 27.6 jit_solution(14907499046814559151)
XLA Ops:
  0.6 1.3 %pack_y.1 = (f32[208,128]{1,0:T(8,128)S(1)}, f32[16,16,128]{2,1,0:T(8,128)S(1)}) custom-call(f32[19,16,16,128]{3,2,1,0:T(8,128)} %adj.11, f32[16,16,128]{2,1,0:T(8,128)} %design.1), custom_call_target="tpu_custom_call" | custom-call | flops 1000000 | bytes 1000000 | tf_op jit(solution)/shard_map/pack_y/pallas_call | solution.py:153
  1.9 0.0 copy-start.1
  1.9 3.0 %collective-permute-start = (f32[208,128]{1,0:T(8,128)S(1)}, f32[208,128]{1,0:T(8,128)S(1)}, u32[]{:S(2)}, u32[]{:S(2)}) collective-permute-start(f32[208,128]{1,0:T(8,128)S(1)} %get-tuple-element.23.ahead), channel_id=1, source_target_pairs={{0,2},{2,0},{1,3},{3,1},{4,6},{6,4},{5,7},{7,5},{8,10},{10,8},{9,1... | collective-permute-start | bytes 319496 | tf_op jit(solution)/shard_map/ppermute | solution.py:118
  5.0 2.0 %prepare.1 = (f32[4,16,16,128]{3,2,1,0:T(8,128)S(1)}, f32[16,16,128]{2,1,0:T(8,128)S(1)}, f32[16,16,128]{2,1,0:T(8,128)S(1)}) custom-call(f32[208,128]{1,0:T(8,128)S(1)} %get-tuple-element.23.ahead, f32[19,16,16,128]{3,2,1,0:T(8,128)} %forward.1, f32[19,16,16,128]{3,2,1,0:T(8,128)S(1)} %copy-done), custom_call_target="tpu_custom_call" | custom-call | flops 6553600 | bytes 5767168 | tf_op jit(solution)/shard_map/prepare/pallas_call | solution.py:153
  7.0 1.0 %collective-permute-done.rest_1_.rest_0_ = f32[208,128]{1,0:T(8,128)S(1)} collective-permute-done((f32[208,128]{1,0:T(8,128)S(1)}, f32[208,128]{1,0:T(8,128)S(1)}, u32[]{:S(2)}, u32[]{:S(2)}) %collective-permute-start) | collective-permute-done | bytes 106528 | tf_op jit(solution)/shard_map/ppermute | solution.py:118
  7.9 0.2 design_y.1
  8.2 0.1 collective-permute-start.1
  8.2 0.3 factor_y.1
  8.5 1.8 %collective-permute-start.2 = (f32[256,128]{1,0:T(8,128)S(1)}, f32[256,128]{1,0:T(8,128)S(1)}, u32[]{:S(2)}, u32[]{:S(2)}) collective-permute-start(f32[256,128]{1,0:T(8,128)S(1)} %get-tuple-element.29.smooth), channel_id=1, source_target_pairs={{0,4},{8,12},{16,20},{24,28},{4,0},{12,8},{20,16},{28,24},{1,5},{9... | collective-permute-start | bytes 393224 | tf_op jit(solution)/shard_map/ppermute | solution.py:118
  10.3 0.0 collective-permute-done.1.rest_1_
  10.3 0.5 %pack_x.1 = (f32[272,128]{1,0:T(8,128)S(1)}, f32[256,128]{1,0:T(8,128)S(1)}, f32[16,16,128]{2,1,0:T(8,128)S(1)}) custom-call(f32[19,16,16,128]{3,2,1,0:T(8,128)S(1)} %copy-done, f32[9,128,128]{2,1,0:T(8,128)S(1)} %copy-done.1, f32[256,128]{1,0:T(8,128)S(1)} %get-tuple-element.29.smooth, f32[16,16,128]{2,1,0:T(8,128)S(1)} %get-tuple-element.30.factor_in, ...), custom_call_target="tpu_custom_call" | custom-call | flops 1000000 | bytes 1000000 | tf_op jit(solution)/shard_map/pack_x/pallas_call | solution.py:153
  10.8 1.0 %collective-permute-start.3 = (f32[272,128]{1,0:T(8,128)S(1)}, f32[272,128]{1,0:T(8,128)S(1)}, u32[]{:S(2)}, u32[]{:S(2)}) collective-permute-start(f32[272,128]{1,0:T(8,128)S(1)} %get-tuple-element.36.own.ahead), channel_id=1, source_target_pairs={{0,4},{8,12},{16,20},{24,28},{4,0},{12,8},{20,16},{28,24},{1,5},{9... | collective-permute-start | bytes 417800 | tf_op jit(solution)/shard_map/ppermute | solution.py:118
  11.9 0.1 pack_odd.1.rest_0_
  12.0 0.7 %collective-permute-start.4 = (f32[272,128]{1,0:T(8,128)S(1)}, f32[272,128]{1,0:T(8,128)S(1)}, u32[]{:S(2)}, u32[]{:S(2)}) collective-permute-start(f32[272,128]{1,0:T(8,128)S(1)} %pack_odd.1.rest_0_), channel_id=1, source_target_pairs={{4,8},{12,16},{20,24},{8,4},{16,12},{24,20},{5,9},{13,17},{21,25},... | collective-permute-start | bytes 417800 | tf_op jit(solution)/shard_map/ppermute | solution.py:118
  12.6 2.2 %collective-permute-done.2.beyond = f32[256,128]{1,0:T(8,128)S(1)} collective-permute-done((f32[256,128]{1,0:T(8,128)S(1)}, f32[256,128]{1,0:T(8,128)S(1)}, u32[]{:S(2)}, u32[]{:S(2)}) %collective-permute-start.2) | collective-permute-done | bytes 131104 | tf_op jit(solution)/shard_map/ppermute | solution.py:118
  14.9 3.7 %collective-permute-start.5 = (f32[256,128]{1,0:T(8,128)S(1)}, f32[256,128]{1,0:T(8,128)S(1)}, u32[]{:S(2)}, u32[]{:S(2)}) collective-permute-start(f32[256,128]{1,0:T(8,128)S(1)} %collective-permute-done.2.beyond), channel_id=1, source_target_pairs={{12,4},{20,12},{28,20},{0,8},{8,16},{16,24},{13,5},{21,13},{29,21}... | collective-permute-start | bytes 393224 | tf_op jit(solution)/shard_map/ppermute | solution.py:123
  18.6 2.2 %beside_x.1 = (f32[32,16,128]{2,1,0:T(8,128)S(1)}, f32[19,16,16,128]{3,2,1,0:T(8,128)S(1)}) custom-call(f32[19,16,16,128]{3,2,1,0:T(8,128)S(1)} %copy-done, f32[4,16,16,128]{3,2,1,0:T(8,128)S(1)} %get-tuple-element.24.flow_ref, s32[16,16,128]{2,1,0:T(8,128)S(1)} %copy-done.2, f32[256,128]{1,0:T(8,128)S(1)} %get-tuple-element.32.own, ...), custom_call_target="tpu_custom_call" | custom-call | flops 3276800000 | bytes 1000 | tf_op jit(solution)/shard_map/beside_x/pallas_call | solution.py:153
  20.8 0.1 far_x.1.partial
  20.9 0.0 collective-permute-done.3.got.rest_2_
  20.9 0.4 %near_x.1 = (f32[16,16,128]{2,1,0:T(8,128)S(1)}, f32[16,16,128]{2,1,0:T(8,128)S(1)}) custom-call(f32[9,128,128]{2,1,0:T(8,128)S(1)} %copy-done.1, f32[32,16,128]{2,1,0:T(8,128)S(1)} %far_x.1.partial, f32[16,16,128]{2,1,0:T(8,128)S(1)} %get-tuple-element.35.factor, f32[4,16,16,128]{3,2,1,0:T(8,128)S(1)} %get-tuple-element.24.flow_ref, ...), custom_call_target="tpu_custom_call" | custom-call | flops 1000 | bytes 1000 | tf_op jit(solution)/shard_map/near_x/pallas_call | solution.py:153
  21.3 0.0 collective-permute-done.5.rest_2_
  21.3 0.4 %source.1 = (f32[16,16,128]{2,1,0:T(8,128)S(1)}, f32[16,16,128]{2,1,0:T(8,128)S(1)}, f32[16,8,128]{2,1,0:T(8,128)S(1)}) custom-call(f32[9,128,128]{2,1,0:T(8,128)S(1)} %copy-done.1, f32[32,16,128]{2,1,0:T(8,128)S(1)} %far_x.1.partial, f32[16,16,128]{2,1,0:T(8,128)S(1)} %get-tuple-element.35.factor, f32[4,16,16,128]{3,2,1,0:T(8,128)S(1)} %get-tuple-element.24.flow_ref, ...), custom_call_target="tpu_custom_call" | custom-call | flops 1000000 | bytes 1000000 | tf_op jit(solution)/shard_map/source/pallas_call | solution.py:153
  21.8 1.6 %collective-permute-start.6 = (f32[16,8,128]{2,1,0:T(8,128)S(1)}, f32[16,8,128]{2,1,0:T(8,128)S(1)}, u32[]{:S(2)}, u32[]{:S(2)}) collective-permute-start(f32[16,8,128]{2,1,0:T(8,128)S(1)} %get-tuple-element.41), channel_id=1, source_target_pairs={{0,2},{2,0},{1,3},{3,1},{4,6},{6,4},{5,7},{7,5},{8,10},{10,8},{9,1... | collective-permute-start | bytes 196616 | tf_op jit(solution)/shard_map/ppermute | solution.py:118
  23.4 0.1 pack_corner.1
  23.5 0.1 collective-permute-start.7
  23.6 0.6 %collective-permute-start.8 = (f32[8,128]{1,0:T(8,128)S(1)}, f32[8,128]{1,0:T(8,128)S(1)}, u32[]{:S(2)}, u32[]{:S(2)}) collective-permute-start(f32[8,128]{1,0:T(8,128)S(1)} %get-tuple-element.43), channel_id=1, source_target_pairs={{0,3},{3,0},{1,2},{2,1},{4,7},{7,4},{5,6},{6,5},{8,11},{11,8},{9,1... | collective-permute-start | bytes 12296 | tf_op jit(solution)/shard_map/ppermute | solution.py:133
  24.2 0.3 own_z.1.own
  24.4 1.7 %collide.1.ahead = f32[19,16,16,128]{3,2,1,0:T(8,128)} custom-call(f32[19,16,16,128]{3,2,1,0:T(8,128)S(1)} %copy-done, f32[19,16,16,128]{3,2,1,0:T(8,128)S(1)} %get-tuple-element.33.base, f32[4,16,16,128]{3,2,1,0:T(8,128)S(1)} %get-tuple-element.24.flow_ref, f32[16,16,128]{2,1,0:T(8,128)S(1)} %get-tuple-element.39.damp, s32[16,16,128]{2,1,0:T(8,128)S(1)} %copy-done.2, ...), custom_call_target="tpu_custom_call" | custom-call | flops 9830400 | bytes 5767168 | tf_op jit(solution)/shard_map/collide/pallas_call | solution.py:153
  26.2 0.0 collective-permute-done.6.rest_0_
  26.2 0.3 %smooth_yz.1.own = f32[16,16,128]{2,1,0:T(8,128)S(1)} custom-call(f32[19,16,16,128]{3,2,1,0:T(8,128)} %collide.1.ahead, f32[9,128,128]{2,1,0:T(8,128)S(1)} %copy-done.1, f32[256,128]{1,0:T(8,128)S(1)} %own_z.1.own, f32[16,8,128]{2,1,0:T(8,128)S(1)} %collective-permute-done.6.rest_0_), custom_call_target="tpu_custom_call" | custom-call | flops 1000000 | bytes 1000000 | tf_op jit(solution)/shard_map/smooth_yz/pallas_call | solution.py:153
  26.5 0.2 collective-permute-done.8.rest_1_
  26.7 1.0 %add_halo.1 = f32[16,16,128]{2,1,0:T(8,128)} custom-call(f32[9,128,128]{2,1,0:T(8,128)S(1)} %copy-done.1, f32[16,16,128]{2,1,0:T(8,128)S(1)} %smooth_yz.1.own, f32[16,128]{1,0:T(8,128)S(1)} %collective-permute-done.7.rest_0_, f32[8,128]{1,0:T(8,128)S(1)} %collective-permute-done.8.rest_1_), custom_call_target="tpu_custom_call" | custom-call | flops 1000000 | bytes 1000000 | tf_op jit(solution)/shard_map/add_halo/pallas_call | solution.py:153
  (7 shorter events, 0.0 us)
Async XLA Ops:
  0.6 4.3 %copy-start = (f32[19,16,16,128]{3,2,1,0:T(8,128)S(1)}, f32[19,16,16,128]{3,2,1,0:T(8,128)}, u32[]{:S(2)}) copy-start(f32[19,16,16,128]{3,2,1,0:T(8,128)} %adj.11) | copy-start | bytes 7471108
  1.9 6.3 %copy-start.1 = (f32[9,128,128]{2,1,0:T(8,128)S(1)}, f32[9,128,128]{2,1,0:T(8,128)}, u32[]{:S(2)}) copy-start(f32[9,128,128]{2,1,0:T(8,128)} %constant.2.clone.weights) | copy-start | bytes 1769476
  1.9 6.0 %collective-permute-start = (f32[208,128]{1,0:T(8,128)S(1)}, f32[208,128]{1,0:T(8,128)S(1)}, u32[]{:S(2)}, u32[]{:S(2)}) collective-permute-start(f32[208,128]{1,0:T(8,128)S(1)} %get-tuple-element.23.ahead), channel_id=1, source_target_pairs={{0,2},{2,0},{1,3},{3,1},{4,6},{6,4},{5,7},{7,5},{8,10},{10,8},{9,1... | collective-permute-start | bytes 319496 | tf_op jit(solution)/shard_map/ppermute | solution.py:118
  8.2 2.1 %collective-permute-start.1 = (f32[16,16,128]{2,1,0:T(8,128)S(1)}, f32[16,16,128]{2,1,0:T(8,128)S(1)}, u32[]{:S(2)}, u32[]{:S(2)}) collective-permute-start(f32[16,16,128]{2,1,0:T(8,128)S(1)} %get-tuple-element.31), channel_id=1, source_target_pairs={{0,1},{1,0},{2,3},{3,2},{4,5},{5,4},{6,7},{7,6},{8,9},{9,8},{10,11... | collective-permute-start | bytes 393224 | tf_op jit(solution)/shard_map/ppermute | solution.py:118
  8.5 6.4 %collective-permute-start.2 = (f32[256,128]{1,0:T(8,128)S(1)}, f32[256,128]{1,0:T(8,128)S(1)}, u32[]{:S(2)}, u32[]{:S(2)}) collective-permute-start(f32[256,128]{1,0:T(8,128)S(1)} %get-tuple-element.29.smooth), channel_id=1, source_target_pairs={{0,4},{8,12},{16,20},{24,28},{4,0},{12,8},{20,16},{28,24},{1,5},{9... | collective-permute-start | bytes 393224 | tf_op jit(solution)/shard_map/ppermute | solution.py:118
  10.8 7.7 %copy-start.2 = (s32[16,16,128]{2,1,0:T(8,128)S(1)}, s32[16,16,128]{2,1,0:T(8,128)}, u32[]{:S(2)}) copy-start(s32[16,16,128]{2,1,0:T(8,128)} %mask.3) | copy-start | bytes 393220
  10.8 10.1 %collective-permute-start.3 = (f32[272,128]{1,0:T(8,128)S(1)}, f32[272,128]{1,0:T(8,128)S(1)}, u32[]{:S(2)}, u32[]{:S(2)}) collective-permute-start(f32[272,128]{1,0:T(8,128)S(1)} %get-tuple-element.36.own.ahead), channel_id=1, source_target_pairs={{0,4},{8,12},{16,20},{24,28},{4,0},{12,8},{20,16},{28,24},{1,5},{9... | collective-permute-start | bytes 417800 | tf_op jit(solution)/shard_map/ppermute | solution.py:118
  12.0 9.4 %collective-permute-start.4 = (f32[272,128]{1,0:T(8,128)S(1)}, f32[272,128]{1,0:T(8,128)S(1)}, u32[]{:S(2)}, u32[]{:S(2)}) collective-permute-start(f32[272,128]{1,0:T(8,128)S(1)} %pack_odd.1.rest_0_), channel_id=1, source_target_pairs={{4,8},{12,16},{20,24},{8,4},{16,12},{24,20},{5,9},{13,17},{21,25},... | collective-permute-start | bytes 417800 | tf_op jit(solution)/shard_map/ppermute | solution.py:118
  14.9 6.4 %collective-permute-start.5 = (f32[256,128]{1,0:T(8,128)S(1)}, f32[256,128]{1,0:T(8,128)S(1)}, u32[]{:S(2)}, u32[]{:S(2)}) collective-permute-start(f32[256,128]{1,0:T(8,128)S(1)} %collective-permute-done.2.beyond), channel_id=1, source_target_pairs={{12,4},{20,12},{28,20},{0,8},{8,16},{16,24},{13,5},{21,13},{29,21}... | collective-permute-start | bytes 393224 | tf_op jit(solution)/shard_map/ppermute | solution.py:123
  21.8 4.4 %collective-permute-start.6 = (f32[16,8,128]{2,1,0:T(8,128)S(1)}, f32[16,8,128]{2,1,0:T(8,128)S(1)}, u32[]{:S(2)}, u32[]{:S(2)}) collective-permute-start(f32[16,8,128]{2,1,0:T(8,128)S(1)} %get-tuple-element.41), channel_id=1, source_target_pairs={{0,2},{2,0},{1,3},{3,1},{4,6},{6,4},{5,7},{7,5},{8,10},{10,8},{9,1... | collective-permute-start | bytes 196616 | tf_op jit(solution)/shard_map/ppermute | solution.py:118
  23.5 3.2 %collective-permute-start.7 = (f32[16,128]{1,0:T(8,128)S(1)}, f32[16,128]{1,0:T(8,128)S(1)}, u32[]{:S(2)}, u32[]{:S(2)}) collective-permute-start(f32[16,128]{1,0:T(8,128)S(1)} %get-tuple-element.42), channel_id=1, source_target_pairs={{0,1},{1,0},{2,3},{3,2},{4,5},{5,4},{6,7},{7,6},{8,9},{9,8},{10,11... | collective-permute-start | bytes 24584 | tf_op jit(solution)/shard_map/ppermute | solution.py:118
  23.6 3.1 %collective-permute-start.8 = (f32[8,128]{1,0:T(8,128)S(1)}, f32[8,128]{1,0:T(8,128)S(1)}, u32[]{:S(2)}, u32[]{:S(2)}) collective-permute-start(f32[8,128]{1,0:T(8,128)S(1)} %get-tuple-element.43), channel_id=1, source_target_pairs={{0,3},{3,0},{1,2},{2,1},{4,7},{7,4},{5,6},{6,5},{8,11},{11,8},{9,1... | collective-permute-start | bytes 12296 | tf_op jit(solution)/shard_map/ppermute | solution.py:133

commit v6 on v5

--- a/solution.py
+++ b/solution.py
@@ -523,15 +523,13 @@
     pl.when(px != 1)(lambda: faces_x(dims, out, False, factor, flow_ref, pull))
 
 
-def pack_x(dims, many_y, many_z, adj, weights, smooth, factor_in, flow_ref, *rest):
+def pack_x(dims, many_y, many_z, adj, factor_in, flow_ref, *rest):
     X, Y, Z = dims
     rest = iter(rest)
     y_even, y_odd = refs_of(rest, many_y)
     z_even, z_odd = refs_of(rest, many_z)
-    out, whole, factor = rest
+    out, factor = rest
     px, py, pz = parity_of("gx"), parity_of("gy"), parity_of("gz")
-    value = smooth[...] + halo_z(weights, pz, flat(dims, z_even), flat(dims, z_odd))
-    whole[...] = value
     pack_halo(dims, pz, [z_even, z_odd][: 1 + many_z], out)
     lane = lax.broadcasted_iota(jnp.int32, (Y, Z), 1)
     factor[...] = factor_in[...]
@@ -597,19 +595,18 @@
     return jnp.where(pz == n, (R * x) % Z, (R * x + R) % Z)
 
 
-def half_source(dims, above, near, many_z, pz, weights, partial, relayed, factor, flow_ref, own, got, smooth, ext, damp, base, result):
-    X, Y, Z = dims
+def layers_toward(dims, above, near):
+    X = dims[0]
     if near:
-        layers = range(2 * R, X + 2 * R) if above else range(X)
-    else:
-        layers = range(X, X + 2 * R) if above else range(2 * R)
+        return range(2 * R, X + 2 * R) if above else range(X)
+    return range(X, X + 2 * R) if above else range(2 * R)
+
+
+def complete(dims, above, layers, many_z, pz, weights, partial, factor, flow_ref, own, got, smooth, ext):
+    X, Y, Z = dims
     u_at, v_at, d_at = R * Y, R * Y + 5 * Y, R * Y + 8 * Y
     for e in layers:
-        total = partial[e]
-        if relayed is not None:
-            for tap, i in taps_of(X, above, e):
-                total = total + tap * relayed[i * Y : (i + 1) * Y, :]
-        smooth[e] = total
+        smooth[e] = partial[e]
         if R <= e < R + X:
             ext[e] = factor[e - R]
         elif got is None:
@@ -617,36 +614,45 @@
         else:
             at = (e - R - X if above else e) * Y
             ext[e] = got[at : at + Y, :]
-    if got is not None:
-        lane = lax.broadcasted_iota(jnp.int32, (Y, Z), 1)
-        for n in range(1 + many_z):
-            above_z = jnp.where(pz == n, 1, 0)
-            value = dot(got[d_at + n * Y : d_at + (n + 1) * Y, :], weights[3 + 2 * int(above) + above_z])
-            first = (Z - R) * above_z
-            there = (lane >= first) & (lane < first + R)
-            for i in range(X):
-                e = i + X * int(above)
-                moved = pltpu.roll(value, lax.rem(first + Z - R * i, Z), 1)
-                smooth[e] = smooth[e] + jnp.where(there, moved, 0.0)
-
-        def moment(ref, names):
-            return moment_of({q: ref[u_at + j * Y : u_at + (j + 1) * Y, :] for j, q in enumerate(names)})
-
-        def less(e, vel, m):
-            ext[e] = ext[e] - (vel[0] * m[0] + vel[1] * m[1] + vel[2] * m[2])
-
-        inner, outer = (R + X - 1, R + X) if above else (R, R - 1)
-        there, here = (PLUS[0], MINUS[0]) if above else (MINUS[0], PLUS[0])
-        less(inner, [flow_ref[a, inner - R] for a in range(3)], moment(got, there))
-        less(outer, [got[v_at + a * Y : v_at + (a + 1) * Y, :] for a in range(3)], moment(own, here))
+    if got is None:
+        return
+    lane = lax.broadcasted_iota(jnp.int32, (Y, Z), 1)
+    for n in range(1 + many_z):
+        above_z = jnp.where(pz == n, 1, 0)
+        value = dot(got[d_at + n * Y : d_at + (n + 1) * Y, :], weights[3 + 2 * int(above) + above_z])
+        first = (Z - R) * above_z
+        there = (lane >= first) & (lane < first + R)
+        for i in range(X):
+            e = i + X * int(above)
+            moved = pltpu.roll(value, lax.rem(first + Z - R * i, Z), 1)
+            smooth[e] = smooth[e] + jnp.where(there, moved, 0.0)
+
+    def moment(ref, names):
+        return moment_of({q: ref[u_at + j * Y : u_at + (j + 1) * Y, :] for j, q in enumerate(names)})
+
+    def less(e, vel, m):
+        ext[e] = ext[e] - (vel[0] * m[0] + vel[1] * m[1] + vel[2] * m[2])
+
+    inner, outer = (R + X - 1, R + X) if above else (R, R - 1)
+    there, here = (PLUS[0], MINUS[0]) if above else (MINUS[0], PLUS[0])
+    less(inner, [flow_ref[a, inner - R] for a in range(3)], moment(got, there))
+    less(outer, [got[v_at + a * Y : v_at + (a + 1) * Y, :] for a in range(3)], moment(own, here))
+
+
+def half_source(dims, above, layers, smooth, relayed, ext, new, damp, base, result):
+    X, Y, Z = dims
     slope = -damping_max * ramp_shape * (1.0 + ramp_shape)
     for e in layers:
-        physical, steep, inverse = project(smooth[e])
-        ext[e] = (slope * steep) * (inverse * inverse) * ext[e]
+        total = smooth[e]
+        if relayed is not None:
+            for tap, i in taps_of(X, above, e):
+                total = total + tap * relayed[i * Y : (i + 1) * Y, :]
+        physical, steep, inverse = project(total)
+        new[e] = (slope * steep) * (inverse * inverse) * ext[e]
         if R <= e < R + X:
             damp[e - R] = (2.0 * damping_max * ramp_shape) * (1.0 - physical) * inverse
     for x in range(X):
-        terms = [TAPS[e - x] * ext[e] for e in layers if 0 <= e - x <= 2 * R]
+        terms = [TAPS[e - x] * new[e] for e in layers if 0 <= e - x <= 2 * R]
         if base is not None:
             terms = [base[x]] + terms
         result[x] = sum(terms[1:], terms[0]) if terms else jnp.zeros((Y, Z), jnp.float32)
@@ -654,32 +660,48 @@
 
 def near_x(dims, many_z, weights, partial, factor, flow_ref, own, got, result, damp, smooth, ext):
     px, pz = parity_of("gx"), parity_of("gz")
-    for parity in range(2):
-        pl.when(px == parity)(
-            functools.partial(
-                half_source, dims, parity == 0, True, many_z, pz, weights, partial, None, factor, flow_ref,
-                own, got, smooth, ext, damp, None, result,
-            )
-        )
-
-
-def source(dims, many_x, many_y, many_z, weights, partial, factor, flow_ref, near, near_damp, *rest):
+
+    def act(above):
+        layers = layers_toward(dims, above, True)
+        complete(dims, above, layers, many_z, pz, weights, partial, factor, flow_ref, own, got, smooth, ext)
+        half_source(dims, above, layers, smooth, None, ext, ext, damp, None, result)
+
+    pl.when(px == 0)(lambda: act(True))
+    pl.when(px != 0)(lambda: act(False))
+
+
+def far_ready(dims, many_x, many_z, ahead, weights, partial, factor, flow_ref, *rest):
+    own, got = rest[:2] if many_x else (None, None)
+    smooth, ext = rest[-2:]
+    px, pz = parity_of("gx"), parity_of("gz")
+
+    def act(above):
+        layers = layers_toward(dims, above, False)
+        complete(dims, above, layers, many_z, pz, weights, partial, factor, flow_ref, own, got, smooth, ext)
+
+    pl.when(px == 1)(lambda: act(True))
+    pl.when(px != 1)(lambda: act(False))
+
+
+def source(dims, many_x, many_y, many_z, smooth, ext, near, near_damp, *rest):
     X, Y, Z = dims
     rest = iter(rest)
-    own, got, relayed = (next(rest), next(rest), next(rest)) if many_x else (None, None, None)
+    relayed = next(rest) if many_x else None
     result, damp = next(rest), next(rest)
-    outs = [next(rest) for _ in range(1 + many_y)]
-    smooth, ext = rest
+    rows = [next(rest) for _ in range(1 + many_y)]
+    to_z = [next(rest) for _ in range(1 + many_z)]
+    corners = [[next(rest) for _ in range(1 + many_z)] for _ in range(1 + many_y)]
+    (new,) = rest
     px, py, pz = parity_of("gx"), parity_of("gy"), parity_of("gz")
     damp[...] = near_damp[...]
-    for parity in range(2):
-        pl.when(px == parity)(
-            functools.partial(
-                half_source, dims, parity == 1, False, many_z, pz, weights, partial, relayed, factor, flow_ref,
-                own, got, smooth, ext, damp, near, result,
-            )
-        )
-    for n, out in enumerate(outs):
+
+    def act(above):
+        layers = layers_toward(dims, above, False)
+        half_source(dims, above, layers, smooth, relayed, ext, new, damp, near, result)
+
+    pl.when(px == 1)(lambda: act(True))
+    pl.when(px != 1)(lambda: act(False))
+    for n, out in enumerate(rows):
 
         @pl.when(py == n)
         def _(out=out):
@@ -689,12 +711,11 @@
         def _(out=out):
             out[...] = result[:, :R, :]
 
-
-def pack_corner(dims, many_y, many_z, own, *outs):
-    X, Y, Z = dims
-    outs = iter(outs)
-    to_z = [next(outs) for _ in range(1 + many_z)]
-    py, pz = parity_of("gy"), parity_of("gz")
+    pack_corner(dims, py, pz, result, to_z, corners)
+
+
+def pack_corner(dims, py, pz, own, to_z, corners):
+    X, Y, Z = dims
     lane = lax.broadcasted_iota(jnp.int32, (Y, Z), 1)
     for n, out in enumerate(to_z):
         value = jnp.zeros((Y, Z), jnp.float32)
@@ -703,9 +724,8 @@
             there = (lane >= R * x) & (lane < R * (x + 1))
             value = jnp.where(there, pltpu.roll(own[x], shift, 1), value)
         out[...] = value
-    for m in range(1 + many_y):
-        for ref in to_z:
-            next(outs)[...] = jnp.where(py == m, ref[Y - R :, :], ref[:R, :])
+        for m, row in enumerate(corners):
+            row[n][...] = jnp.where(py == m, value[Y - R :], value[:R])
 
 
 def smooth_yz(dims, many_y, ahead, weights, own, *rest):
@@ -811,12 +831,13 @@
     pl.when(px != 0)(lambda: add_side(dims, partial, beyond, 0, out, False))
 
 
-def beside_x(dims, many_y, many_z, adj, flow_ref, mask, own, *rest):
+def beside_x(dims, many_y, many_z, ahead, weights, adj, flow_ref, mask, smooth, *rest):
     X, Y, Z = dims
     rest = iter(rest)
     y_even, y_odd = refs_of(rest, many_y)
     z_even, z_odd = refs_of(rest, many_z)
-    partial, base = rest
+    partial, base, own = rest
+    own[...] = smooth[...] + halo_z(weights, parity_of("gz"), flat(dims, z_even), flat(dims, z_odd))
     for e in range(X + 2 * R):
         terms = [(i - e + 2 * R, i * Y) for i in range(X) if 0 <= i - e + 2 * R <= 2 * R]
         partial[e] = sum(TAPS[k] * own[at : at + Y, :] for k, at in terms)
@@ -833,7 +854,7 @@
         relax(pulled, vel, square(vel), mask[x], None, store)
         return 0
 
-    lax.fori_loop(1, X - 1, layer, 0)
+    lax.fori_loop(1, X - 1, layer, 0, unroll=7)
 
 
 def collide(dims, many_x, many_y, many_z, step, adj, base, flow_ref, damp, mask, *rest):
@@ -952,10 +973,10 @@
     beyond = swap(smooth, "gx", nx, 0)
 
     x_rows = R * Y + 8 * Y
-    even, smooth, factor = call(
+    even, factor = call(
         functools.partial(pack_x, dims, many_y, many_z),
-        [f32(x_rows + (1 + many_z) * Y, Z), f32(X * Y, Z), f32(X, Y, Z)],
-        (adjoint, weights, smooth, factor, flow_values, *got_y, *got_z),
+        [f32(x_rows + (1 + many_z) * Y, Z), f32(X, Y, Z)],
+        (adjoint, factor, flow_values, *got_y, *got_z),
         limit=16,
         name="pack_x",
     )
@@ -973,7 +994,9 @@
     partial, base = call(
         functools.partial(beside_x, dims, many_y, many_z),
         [f32(X + 2 * R, Y, Z), f32(Q, X, Y, Z)],
-        (adjoint, flow_values, mask, smooth, *got_y, *got_z),
+        (to_x[-1], weights, adjoint, flow_values, mask, smooth, *got_y, *got_z),
+        None,
+        [pltpu.VMEM((X * Y, Z), jnp.float32)],
         limit=16,
         flops=100000 * cells,
         moved=1000,
@@ -1002,15 +1025,29 @@
         moved=1000,
         name="near_x",
     )
-    result, damp, *to_y = call(
+    smooth, ext = call(
+        functools.partial(far_ready, dims, many_x, many_z),
+        [f32(X + 2 * R, Y, Z)] * 2,
+        (near, weights, partial, factor, flow_values, *to_x[1:], *got_x[1:]),
+        limit=8,
+        flops=1000,
+        moved=1000,
+        name="far_ready",
+    )
+    n_corners = (1 + many_y) * (1 + many_z)
+    result, damp, *packs = call(
         functools.partial(source, dims, many_x, many_y, many_z),
-        [f32(X, Y, Z), f32(X, Y, Z)] + [f32(X, R, Z)] * (1 + many_y),
-        (weights, partial, factor, flow_values, near, near_damp, *to_x[1:], *got_x[1:], *relayed),
+        [f32(X, Y, Z), f32(X, Y, Z)]
+        + [f32(X, R, Z)] * (1 + many_y)
+        + [f32(Y, Z)] * (1 + many_z)
+        + [f32(R, Z)] * n_corners,
+        (smooth, ext, near, near_damp, *relayed),
         None,
-        [extended] * 2,
+        [extended],
         limit=8,
         name="source",
     )
+    to_y, to_z, to_corner = packs[: 1 + many_y], packs[1 + many_y : -n_corners], packs[-n_corners:]
     got_y2 = some(exchange("gy", ny, *pair(to_y)))
 
     step = 2
@@ -1027,21 +1064,12 @@
         name="collide",
     )
 
-    packs = call(
-        functools.partial(pack_corner, dims, many_y, many_z),
-        [f32(Y, Z)] * (1 + many_z) + [f32(R, Z)] * ((1 + many_y) * (1 + many_z)),
-        (result,),
-        limit=4,
-        flops=1000,
-        moved=1000,
-        name="pack_corner",
-    )
-    got_z2 = some(exchange("gz", nz, *pair(packs[: 1 + many_z])))
     corners = [
-        swap_corner(packs[(1 + m) * (1 + many_z) + n], (ny, nz), m, n)
+        swap_corner(to_corner[m * (1 + many_z) + n], (ny, nz), m, n)
         for m in range(1 + many_y)
         for n in range(1 + many_z)
     ]
+    got_z2 = some(exchange("gz", nz, *pair(to_z)))
     (own,) = call(
         functools.partial(own_z, dims),
         [f32(X * Y, Z)],

time: 28 us -> 27.5 us (0.982)
  Pallas kernels: 10.8 us -> 10.2 us
    pallas_call x15, Pallas kernels: 10.8 us -> 10.2 us  [call(): pl.pallas_call(body, out_shape=outs, in_specs=specs or vmem(len(args)), o...]
    ppermute x7, waiting for transfers between devices: 3.21 us -> 3.51 us  [swap(): return lax.ppermute(array, axis, pairs + [(b, a) for a, b in pairs])]
  transfers between devices with their start and end apart: 9 -> 9, of which waited for: 3 -> 3; matrix products, arithmetic and copies ran while one was open for 0% -> 0% of each run, Pallas kernels for 29% -> 27%
where the time goes in v6:
time: 27.5 us; the launch traced here: 27.1 us
  starting transfers between devices  12.5 us (45%)
  Pallas kernels  10.2 us (37%)
  waiting for transfers between devices  3.51 us (13%)
  between operations  0.82 us (3%)
    pallas_call x15, Pallas kernels, call(): pl.pallas_call(body, out_shape=outs, in_specs=specs or vmem(len(args)), o...  10.2 us
    ppermute x7, starting transfers between devices, swap(): return lax.ppermute(array, axis, pairs + [(b, a) for a, b in pairs])  8.18 us
    ppermute x1, starting transfers between devices, relay(): return lax.ppermute(array, axis, pairs)  3.69 us
    ppermute x7, waiting for transfers between devices, swap(): return lax.ppermute(array, axis, pairs + [(b, a) for a, b in pairs])  3.51 us
    ppermute x1, starting transfers between devices, swap_corner(): return lax.ppermute(array, ('gy', 'gz'), pairs)  0.61 us
  transfers between devices with their start and end apart: 9, of which 3 were waited for; matrix products, arithmetic and copies ran while one was open for 0% of the time, Pallas kernels for 27%

profile of v6, /device:TPU:0, one launch (start us, length us, event | category | flops | bytes accessed | tf_op | source)
XLA Modules:
  0.0 27.1 jit_solution(11355643166836618566)
XLA Ops:
  0.6 1.3 %pack_y.1 = (f32[208,128]{1,0:T(8,128)S(1)}, f32[16,16,128]{2,1,0:T(8,128)S(1)}) custom-call(f32[19,16,16,128]{3,2,1,0:T(8,128)} %adj.11, f32[16,16,128]{2,1,0:T(8,128)} %design.1), custom_call_target="tpu_custom_call" | custom-call | flops 1000000 | bytes 1000000 | tf_op jit(solution)/shard_map/pack_y/pallas_call | solution.py:153
  1.9 0.0 copy-start.1
  1.9 3.0 %collective-permute-start = (f32[208,128]{1,0:T(8,128)S(1)}, f32[208,128]{1,0:T(8,128)S(1)}, u32[]{:S(2)}, u32[]{:S(2)}) collective-permute-start(f32[208,128]{1,0:T(8,128)S(1)} %get-tuple-element.25.ahead), channel_id=1, source_target_pairs={{0,2},{2,0},{1,3},{3,1},{4,6},{6,4},{5,7},{7,5},{8,10},{10,8},{9,1... | collective-permute-start | bytes 319496 | tf_op jit(solution)/shard_map/ppermute | solution.py:118
  5.0 2.0 %prepare.1 = (f32[4,16,16,128]{3,2,1,0:T(8,128)S(1)}, f32[16,16,128]{2,1,0:T(8,128)S(1)}, f32[16,16,128]{2,1,0:T(8,128)S(1)}) custom-call(f32[208,128]{1,0:T(8,128)S(1)} %get-tuple-element.25.ahead, f32[19,16,16,128]{3,2,1,0:T(8,128)} %forward.1, f32[19,16,16,128]{3,2,1,0:T(8,128)S(1)} %copy-done), custom_call_target="tpu_custom_call" | custom-call | flops 6553600 | bytes 5767168 | tf_op jit(solution)/shard_map/prepare/pallas_call | solution.py:153
  7.0 1.0 %collective-permute-done.rest_1_.rest_0_ = f32[208,128]{1,0:T(8,128)S(1)} collective-permute-done((f32[208,128]{1,0:T(8,128)S(1)}, f32[208,128]{1,0:T(8,128)S(1)}, u32[]{:S(2)}, u32[]{:S(2)}) %collective-permute-start) | collective-permute-done | bytes 106528 | tf_op jit(solution)/shard_map/ppermute | solution.py:118
  7.9 0.2 design_y.1
  8.2 0.1 collective-permute-start.1
  8.2 0.3 factor_y.1
  8.5 1.8 %collective-permute-start.2 = (f32[256,128]{1,0:T(8,128)S(1)}, f32[256,128]{1,0:T(8,128)S(1)}, u32[]{:S(2)}, u32[]{:S(2)}) collective-permute-start(f32[256,128]{1,0:T(8,128)S(1)} %get-tuple-element.34.smooth), channel_id=1, source_target_pairs={{0,4},{8,12},{16,20},{24,28},{4,0},{12,8},{20,16},{28,24},{1,5},{9... | collective-permute-start | bytes 393224 | tf_op jit(solution)/shard_map/ppermute | solution.py:118
  10.3 0.4 %pack_x.1 = (f32[272,128]{1,0:T(8,128)S(1)}, f32[16,16,128]{2,1,0:T(8,128)S(1)}) custom-call(f32[19,16,16,128]{3,2,1,0:T(8,128)S(1)} %copy-done, f32[16,16,128]{2,1,0:T(8,128)S(1)} %get-tuple-element.30.factor_in, f32[4,16,16,128]{3,2,1,0:T(8,128)S(1)} %get-tuple-element.28.flow_ref, f32[208,128]{1,0:T(8,128)S(1)} %collective-permute-done.rest_1_.rest_0_, ...), custom_call_target="tpu_custom_call" | custom-call | flops 1000000 | bytes 1000000 | tf_op jit(solution)/shard_map/pack_x/pallas_call | solution.py:153
  10.7 1.0 %collective-permute-start.3 = (f32[272,128]{1,0:T(8,128)S(1)}, f32[272,128]{1,0:T(8,128)S(1)}, u32[]{:S(2)}, u32[]{:S(2)}) collective-permute-start(f32[272,128]{1,0:T(8,128)S(1)} %get-tuple-element.32.ahead.own), channel_id=1, source_target_pairs={{0,4},{8,12},{16,20},{24,28},{4,0},{12,8},{20,16},{28,24},{1,5},{9... | collective-permute-start | bytes 417800 | tf_op jit(solution)/shard_map/ppermute | solution.py:118
  11.7 0.1 pack_odd.1.ahead.rest_0_
  11.8 0.7 %collective-permute-start.4 = (f32[272,128]{1,0:T(8,128)S(1)}, f32[272,128]{1,0:T(8,128)S(1)}, u32[]{:S(2)}, u32[]{:S(2)}) collective-permute-start(f32[272,128]{1,0:T(8,128)S(1)} %pack_odd.1.ahead.rest_0_), channel_id=1, source_target_pairs={{4,8},{12,16},{20,24},{8,4},{16,12},{24,20},{5,9},{13,17},{21,25},... | collective-permute-start | bytes 417800 | tf_op jit(solution)/shard_map/ppermute | solution.py:118
  12.5 2.4 %collective-permute-done.2.beyond = f32[256,128]{1,0:T(8,128)S(1)} collective-permute-done((f32[256,128]{1,0:T(8,128)S(1)}, f32[256,128]{1,0:T(8,128)S(1)}, u32[]{:S(2)}, u32[]{:S(2)}) %collective-permute-start.2) | collective-permute-done | bytes 131104 | tf_op jit(solution)/shard_map/ppermute | solution.py:118
  14.9 3.7 %collective-permute-start.5 = (f32[256,128]{1,0:T(8,128)S(1)}, f32[256,128]{1,0:T(8,128)S(1)}, u32[]{:S(2)}, u32[]{:S(2)}) collective-permute-start(f32[256,128]{1,0:T(8,128)S(1)} %collective-permute-done.2.beyond), channel_id=1, source_target_pairs={{12,4},{20,12},{28,20},{0,8},{8,16},{16,24},{13,5},{21,13},{29,21}... | collective-permute-start | bytes 393224 | tf_op jit(solution)/shard_map/ppermute | solution.py:123
  18.6 1.6 %beside_x.1 = (f32[32,16,128]{2,1,0:T(8,128)S(1)}, f32[19,16,16,128]{3,2,1,0:T(8,128)S(1)}) custom-call(f32[272,128]{1,0:T(8,128)S(1)} %pack_odd.1.ahead.rest_0_, f32[9,128,128]{2,1,0:T(8,128)S(1)} %copy-done.1, f32[19,16,16,128]{3,2,1,0:T(8,128)S(1)} %copy-done, f32[4,16,16,128]{3,2,1,0:T(8,128)S(1)} %get-tuple-element.28.flow_ref, ...), custom_call_target="tpu_custom_call" | custom-call | flops 3276800000 | bytes 1000 | tf_op jit(solution)/shard_map/beside_x/pallas_call | solution.py:153
  20.2 0.1 far_x.1.partial
  20.3 0.0 collective-permute-done.3.got.rest_2_
  20.4 0.4 %near_x.1 = (f32[16,16,128]{2,1,0:T(8,128)S(1)}, f32[16,16,128]{2,1,0:T(8,128)S(1)}) custom-call(f32[9,128,128]{2,1,0:T(8,128)S(1)} %copy-done.1, f32[32,16,128]{2,1,0:T(8,128)S(1)} %far_x.1.partial, f32[16,16,128]{2,1,0:T(8,128)S(1)} %get-tuple-element.33.factor, f32[4,16,16,128]{3,2,1,0:T(8,128)S(1)} %get-tuple-element.28.flow_ref, ...), custom_call_target="tpu_custom_call" | custom-call | flops 1000 | bytes 1000 | tf_op jit(solution)/shard_map/near_x/pallas_call | solution.py:153
  20.8 0.0 collective-permute-done.4.rest_1_.rest_3_
  20.8 0.3 %far_ready.1 = (f32[32,16,128]{2,1,0:T(8,128)S(1)}, f32[32,16,128]{2,1,0:T(8,128)S(1)}) custom-call(f32[16,16,128]{2,1,0:T(8,128)S(1)} %get-tuple-element.37.ahead.near, f32[9,128,128]{2,1,0:T(8,128)S(1)} %copy-done.1, f32[32,16,128]{2,1,0:T(8,128)S(1)} %far_x.1.partial, f32[16,16,128]{2,1,0:T(8,128)S(1)} %get-tuple-element.33.factor, ...), custom_call_target="tpu_custom_call" | custom-call | flops 1000 | bytes 1000 | tf_op jit(solution)/shard_map/far_ready/pallas_call | solution.py:153
  21.1 0.0 collective-permute-done.5.rest_0_
  21.1 0.3 %source.1 = (f32[16,16,128]{2,1,0:T(8,128)S(1)}, f32[16,16,128]{2,1,0:T(8,128)S(1)}, f32[16,8,128]{2,1,0:T(8,128)S(1)}, f32[16,128]{1,0:T(8,128)S(1)}, f32[8,128]{1,0:T(8,128)S(1)}) custom-call(f32[32,16,128]{2,1,0:T(8,128)S(1)} %get-tuple-element.38.smooth, f32[32,16,128]{2,1,0:T(8,128)S(1)} %get-tuple-element.39.ext, ...), custom_call_target="tpu_custom_call" | custom-call | flops 1000000 | bytes 1000000 | tf_op jit(solution)/shard_map/source/pallas_call | solution.py:153
  21.4 1.6 %collective-permute-start.6 = (f32[16,8,128]{2,1,0:T(8,128)S(1)}, f32[16,8,128]{2,1,0:T(8,128)S(1)}, u32[]{:S(2)}, u32[]{:S(2)}) collective-permute-start(f32[16,8,128]{2,1,0:T(8,128)S(1)} %get-tuple-element.43), channel_id=1, source_target_pairs={{0,2},{2,0},{1,3},{3,1},{4,6},{6,4},{5,7},{7,5},{8,10},{10,8},{9,1... | collective-permute-start | bytes 196616 | tf_op jit(solution)/shard_map/ppermute | solution.py:118
  23.0 0.0 collective-permute-start.7
  23.0 0.6 %collective-permute-start.8 = (f32[8,128]{1,0:T(8,128)S(1)}, f32[8,128]{1,0:T(8,128)S(1)}, u32[]{:S(2)}, u32[]{:S(2)}) collective-permute-start(f32[8,128]{1,0:T(8,128)S(1)} %get-tuple-element.45), channel_id=1, source_target_pairs={{0,3},{3,0},{1,2},{2,1},{4,7},{7,4},{5,6},{6,5},{8,11},{11,8},{9,1... | collective-permute-start | bytes 12296 | tf_op jit(solution)/shard_map/ppermute | solution.py:133
  23.7 0.3 own_z.1.own
  23.9 1.7 %collide.1.ahead = f32[19,16,16,128]{3,2,1,0:T(8,128)} custom-call(f32[19,16,16,128]{3,2,1,0:T(8,128)S(1)} %copy-done, f32[19,16,16,128]{3,2,1,0:T(8,128)S(1)} %get-tuple-element.35.base, f32[4,16,16,128]{3,2,1,0:T(8,128)S(1)} %get-tuple-element.28.flow_ref, f32[16,16,128]{2,1,0:T(8,128)S(1)} %get-tuple-element.41.damp, s32[16,16,128]{2,1,0:T(8,128)S(1)} %copy-done.2, ...), custom_call_target="tpu_custom_call" | custom-call | flops 9830400 | bytes 5767168 | tf_op jit(solution)/shard_map/collide/pallas_call | solution.py:153
  25.6 0.1 collective-permute-done.6.rest_0_
  25.8 0.3 %smooth_yz.1.own = f32[16,16,128]{2,1,0:T(8,128)S(1)} custom-call(f32[19,16,16,128]{3,2,1,0:T(8,128)} %collide.1.ahead, f32[9,128,128]{2,1,0:T(8,128)S(1)} %copy-done.1, f32[256,128]{1,0:T(8,128)S(1)} %own_z.1.own, f32[16,8,128]{2,1,0:T(8,128)S(1)} %collective-permute-done.6.rest_0_), custom_call_target="tpu_custom_call" | custom-call | flops 1000000 | bytes 1000000 | tf_op jit(solution)/shard_map/smooth_yz/pallas_call | solution.py:153
  26.1 0.0 collective-permute-done.8.rest_1_
  26.1 1.0 %add_halo.1 = f32[16,16,128]{2,1,0:T(8,128)} custom-call(f32[9,128,128]{2,1,0:T(8,128)S(1)} %copy-done.1, f32[16,16,128]{2,1,0:T(8,128)S(1)} %smooth_yz.1.own, f32[16,128]{1,0:T(8,128)S(1)} %collective-permute-done.7.rest_0_, f32[8,128]{1,0:T(8,128)S(1)} %collective-permute-done.8.rest_1_), custom_call_target="tpu_custom_call" | custom-call | flops 1000000 | bytes 1000000 | tf_op jit(solution)/shard_map/add_halo/pallas_call | solution.py:153
  (7 shorter events, 0.0 us)
Async XLA Ops:
  0.6 4.3 %copy-start = (f32[19,16,16,128]{3,2,1,0:T(8,128)S(1)}, f32[19,16,16,128]{3,2,1,0:T(8,128)}, u32[]{:S(2)}) copy-start(f32[19,16,16,128]{3,2,1,0:T(8,128)} %adj.11) | copy-start | bytes 7471108
  1.9 6.3 %copy-start.1 = (f32[9,128,128]{2,1,0:T(8,128)S(1)}, f32[9,128,128]{2,1,0:T(8,128)}, u32[]{:S(2)}) copy-start(f32[9,128,128]{2,1,0:T(8,128)} %constant.2.clone.weights) | copy-start | bytes 1769476
  1.9 6.0 %collective-permute-start = (f32[208,128]{1,0:T(8,128)S(1)}, f32[208,128]{1,0:T(8,128)S(1)}, u32[]{:S(2)}, u32[]{:S(2)}) collective-permute-start(f32[208,128]{1,0:T(8,128)S(1)} %get-tuple-element.25.ahead), channel_id=1, source_target_pairs={{0,2},{2,0},{1,3},{3,1},{4,6},{6,4},{5,7},{7,5},{8,10},{10,8},{9,1... | collective-permute-start | bytes 319496 | tf_op jit(solution)/shard_map/ppermute | solution.py:118
  8.2 2.1 %collective-permute-start.1 = (f32[16,16,128]{2,1,0:T(8,128)S(1)}, f32[16,16,128]{2,1,0:T(8,128)S(1)}, u32[]{:S(2)}, u32[]{:S(2)}) collective-permute-start(f32[16,16,128]{2,1,0:T(8,128)S(1)} %get-tuple-element.31), channel_id=1, source_target_pairs={{0,1},{1,0},{2,3},{3,2},{4,5},{5,4},{6,7},{7,6},{8,9},{9,8},{10,11... | collective-permute-start | bytes 393224 | tf_op jit(solution)/shard_map/ppermute | solution.py:118
  8.5 6.4 %collective-permute-start.2 = (f32[256,128]{1,0:T(8,128)S(1)}, f32[256,128]{1,0:T(8,128)S(1)}, u32[]{:S(2)}, u32[]{:S(2)}) collective-permute-start(f32[256,128]{1,0:T(8,128)S(1)} %get-tuple-element.34.smooth), channel_id=1, source_target_pairs={{0,4},{8,12},{16,20},{24,28},{4,0},{12,8},{20,16},{28,24},{1,5},{9... | collective-permute-start | bytes 393224 | tf_op jit(solution)/shard_map/ppermute | solution.py:118
  10.7 7.9 %copy-start.2 = (s32[16,16,128]{2,1,0:T(8,128)S(1)}, s32[16,16,128]{2,1,0:T(8,128)}, u32[]{:S(2)}) copy-start(s32[16,16,128]{2,1,0:T(8,128)} %mask.3) | copy-start | bytes 393220
  10.7 9.7 %collective-permute-start.3 = (f32[272,128]{1,0:T(8,128)S(1)}, f32[272,128]{1,0:T(8,128)S(1)}, u32[]{:S(2)}, u32[]{:S(2)}) collective-permute-start(f32[272,128]{1,0:T(8,128)S(1)} %get-tuple-element.32.ahead.own), channel_id=1, source_target_pairs={{0,4},{8,12},{16,20},{24,28},{4,0},{12,8},{20,16},{28,24},{1,5},{9... | collective-permute-start | bytes 417800 | tf_op jit(solution)/shard_map/ppermute | solution.py:118
  11.8 9.0 %collective-permute-start.4 = (f32[272,128]{1,0:T(8,128)S(1)}, f32[272,128]{1,0:T(8,128)S(1)}, u32[]{:S(2)}, u32[]{:S(2)}) collective-permute-start(f32[272,128]{1,0:T(8,128)S(1)} %pack_odd.1.ahead.rest_0_), channel_id=1, source_target_pairs={{4,8},{12,16},{20,24},{8,4},{16,12},{24,20},{5,9},{13,17},{21,25},... | collective-permute-start | bytes 417800 | tf_op jit(solution)/shard_map/ppermute | solution.py:118
  14.9 6.2 %collective-permute-start.5 = (f32[256,128]{1,0:T(8,128)S(1)}, f32[256,128]{1,0:T(8,128)S(1)}, u32[]{:S(2)}, u32[]{:S(2)}) collective-permute-start(f32[256,128]{1,0:T(8,128)S(1)} %collective-permute-done.2.beyond), channel_id=1, source_target_pairs={{12,4},{20,12},{28,20},{0,8},{8,16},{16,24},{13,5},{21,13},{29,21}... | collective-permute-start | bytes 393224 | tf_op jit(solution)/shard_map/ppermute | solution.py:123
  21.4 4.3 %collective-permute-start.6 = (f32[16,8,128]{2,1,0:T(8,128)S(1)}, f32[16,8,128]{2,1,0:T(8,128)S(1)}, u32[]{:S(2)}, u32[]{:S(2)}) collective-permute-start(f32[16,8,128]{2,1,0:T(8,128)S(1)} %get-tuple-element.43), channel_id=1, source_target_pairs={{0,2},{2,0},{1,3},{3,1},{4,6},{6,4},{5,7},{7,5},{8,10},{10,8},{9,1... | collective-permute-start | bytes 196616 | tf_op jit(solution)/shard_map/ppermute | solution.py:118
  23.0 3.1 %collective-permute-start.7 = (f32[16,128]{1,0:T(8,128)S(1)}, f32[16,128]{1,0:T(8,128)S(1)}, u32[]{:S(2)}, u32[]{:S(2)}) collective-permute-start(f32[16,128]{1,0:T(8,128)S(1)} %get-tuple-element.44), channel_id=1, source_target_pairs={{0,1},{1,0},{2,3},{3,2},{4,5},{5,4},{6,7},{7,6},{8,9},{9,8},{10,11... | collective-permute-start | bytes 24584 | tf_op jit(solution)/shard_map/ppermute | solution.py:118
  23.0 3.1 %collective-permute-start.8 = (f32[8,128]{1,0:T(8,128)S(1)}, f32[8,128]{1,0:T(8,128)S(1)}, u32[]{:S(2)}, u32[]{:S(2)}) collective-permute-start(f32[8,128]{1,0:T(8,128)S(1)} %get-tuple-element.45), channel_id=1, source_target_pairs={{0,3},{3,0},{1,2},{2,1},{4,7},{7,4},{5,6},{6,5},{8,11},{11,8},{9,1... | collective-permute-start | bytes 12296 | tf_op jit(solution)/shard_map/ppermute | solution.py:133

commit v7 on v6

--- a/solution.py
+++ b/solution.py
@@ -725,7 +725,8 @@
             value = jnp.where(there, pltpu.roll(own[x], shift, 1), value)
         out[...] = value
         for m, row in enumerate(corners):
-            row[n][...] = jnp.where(py == m, value[Y - R :], value[:R])
+            row[n][:R, :] = jnp.where(py == m, value[Y - R :], value[:R])
+            row[n][R:, :] = jnp.zeros((3 * R, Z), jnp.float32)
 
 
 def smooth_yz(dims, many_y, ahead, weights, own, *rest):
@@ -752,7 +753,7 @@
     lane = lax.broadcasted_iota(jnp.int32, (Y, Z), 1)
     moved = []
     for n in range(1 + many_z):
-        below, above = sides(py, corners[0][n][...], corners[1][n][...] if many_y else None)
+        below, above = sides(py, corners[0][n][:R, :], corners[1][n][:R, :] if many_y else None)
         pad[:R, :] = below
         pad[R : R + Y, :] = sides_z[n][...]
         pad[R + Y :, :] = above
@@ -1040,7 +1041,7 @@
         [f32(X, Y, Z), f32(X, Y, Z)]
         + [f32(X, R, Z)] * (1 + many_y)
         + [f32(Y, Z)] * (1 + many_z)
-        + [f32(R, Z)] * n_corners,
+        + [f32(4 * R, Z)] * n_corners,
         (smooth, ext, near, near_damp, *relayed),
         None,
         [extended],

time: 27.5 us -> 27.3 us (level); the launches traced: 27.1 us -> 27.2 us
    ppermute x7, starting transfers between devices: 8.18 us -> 8.79 us  [swap(): return lax.ppermute(array, axis, pairs + [(b, a) for a, b in pairs])]
    ppermute x1, starting transfers between devices: 0.61 us -> 0.01 us  [swap_corner(): return lax.ppermute(array, ('gy', 'gz'), pairs)]
  transfers between devices with their start and end apart: 9 -> 9, of which waited for: 3 -> 4; matrix products, arithmetic and copies ran while one was open for 0% -> 0% of each run, Pallas kernels for 27% -> 27%
where the time goes in v7:
time: 27.3 us; the launch traced here: 27.2 us
  starting transfers between devices  12.5 us (46%)
  Pallas kernels  10.2 us (37%)
  waiting for transfers between devices  3.61 us (13%)
  between operations  0.81 us (3%)
    pallas_call x15, Pallas kernels, call(): pl.pallas_call(body, out_shape=outs, in_specs=specs or vmem(len(args)), o...  10.2 us
    ppermute x7, starting transfers between devices, swap(): return lax.ppermute(array, axis, pairs + [(b, a) for a, b in pairs])  8.79 us
    ppermute x1, starting transfers between devices, relay(): return lax.ppermute(array, axis, pairs)  3.69 us
    ppermute x7, waiting for transfers between devices, swap(): return lax.ppermute(array, axis, pairs + [(b, a) for a, b in pairs])  3.51 us
  transfers between devices with their start and end apart: 9, of which 4 were waited for; matrix products, arithmetic and copies ran while one was open for 0% of the time, Pallas kernels for 27%

profile of v7, /device:TPU:0, one launch (start us, length us, event | category | flops | bytes accessed | tf_op | source)
XLA Modules:
  0.0 27.2 jit_solution(18238846773890269619)
XLA Ops:
  0.6 1.3 %pack_y.1 = (f32[208,128]{1,0:T(8,128)S(1)}, f32[16,16,128]{2,1,0:T(8,128)S(1)}) custom-call(f32[19,16,16,128]{3,2,1,0:T(8,128)} %adj.11, f32[16,16,128]{2,1,0:T(8,128)} %design.1), custom_call_target="tpu_custom_call" | custom-call | flops 1000000 | bytes 1000000 | tf_op jit(solution)/shard_map/pack_y/pallas_call | solution.py:153
  1.9 0.0 copy-start.1
  1.9 3.0 %collective-permute-start = (f32[208,128]{1,0:T(8,128)S(1)}, f32[208,128]{1,0:T(8,128)S(1)}, u32[]{:S(2)}, u32[]{:S(2)}) collective-permute-start(f32[208,128]{1,0:T(8,128)S(1)} %get-tuple-element.25.ahead), channel_id=1, source_target_pairs={{0,2},{2,0},{1,3},{3,1},{4,6},{6,4},{5,7},{7,5},{8,10},{10,8},{9,1... | collective-permute-start | bytes 319496 | tf_op jit(solution)/shard_map/ppermute | solution.py:118
  5.0 2.0 %prepare.1 = (f32[4,16,16,128]{3,2,1,0:T(8,128)S(1)}, f32[16,16,128]{2,1,0:T(8,128)S(1)}, f32[16,16,128]{2,1,0:T(8,128)S(1)}) custom-call(f32[208,128]{1,0:T(8,128)S(1)} %get-tuple-element.25.ahead, f32[19,16,16,128]{3,2,1,0:T(8,128)} %forward.1, f32[19,16,16,128]{3,2,1,0:T(8,128)S(1)} %copy-done), custom_call_target="tpu_custom_call" | custom-call | flops 6553600 | bytes 5767168 | tf_op jit(solution)/shard_map/prepare/pallas_call | solution.py:153
  7.0 1.0 %collective-permute-done.rest_1_.rest_0_ = f32[208,128]{1,0:T(8,128)S(1)} collective-permute-done((f32[208,128]{1,0:T(8,128)S(1)}, f32[208,128]{1,0:T(8,128)S(1)}, u32[]{:S(2)}, u32[]{:S(2)}) %collective-permute-start) | collective-permute-done | bytes 106528 | tf_op jit(solution)/shard_map/ppermute | solution.py:118
  7.9 0.2 design_y.1
  8.2 0.1 collective-permute-start.1
  8.2 0.3 factor_y.1
  8.5 1.8 %collective-permute-start.2 = (f32[256,128]{1,0:T(8,128)S(1)}, f32[256,128]{1,0:T(8,128)S(1)}, u32[]{:S(2)}, u32[]{:S(2)}) collective-permute-start(f32[256,128]{1,0:T(8,128)S(1)} %get-tuple-element.34.smooth), channel_id=1, source_target_pairs={{0,4},{8,12},{16,20},{24,28},{4,0},{12,8},{20,16},{28,24},{1,5},{9... | collective-permute-start | bytes 393224 | tf_op jit(solution)/shard_map/ppermute | solution.py:118
  10.3 0.4 %pack_x.1 = (f32[272,128]{1,0:T(8,128)S(1)}, f32[16,16,128]{2,1,0:T(8,128)S(1)}) custom-call(f32[19,16,16,128]{3,2,1,0:T(8,128)S(1)} %copy-done, f32[16,16,128]{2,1,0:T(8,128)S(1)} %get-tuple-element.30.factor_in, f32[4,16,16,128]{3,2,1,0:T(8,128)S(1)} %get-tuple-element.28.flow_ref, f32[208,128]{1,0:T(8,128)S(1)} %collective-permute-done.rest_1_.rest_0_, ...), custom_call_target="tpu_custom_call" | custom-call | flops 1000000 | bytes 1000000 | tf_op jit(solution)/shard_map/pack_x/pallas_call | solution.py:153
  10.7 1.0 %collective-permute-start.3 = (f32[272,128]{1,0:T(8,128)S(1)}, f32[272,128]{1,0:T(8,128)S(1)}, u32[]{:S(2)}, u32[]{:S(2)}) collective-permute-start(f32[272,128]{1,0:T(8,128)S(1)} %get-tuple-element.32.ahead.own), channel_id=1, source_target_pairs={{0,4},{8,12},{16,20},{24,28},{4,0},{12,8},{20,16},{28,24},{1,5},{9... | collective-permute-start | bytes 417800 | tf_op jit(solution)/shard_map/ppermute | solution.py:118
  11.7 0.1 pack_odd.1.ahead.rest_0_
  11.8 0.7 %collective-permute-start.4 = (f32[272,128]{1,0:T(8,128)S(1)}, f32[272,128]{1,0:T(8,128)S(1)}, u32[]{:S(2)}, u32[]{:S(2)}) collective-permute-start(f32[272,128]{1,0:T(8,128)S(1)} %pack_odd.1.ahead.rest_0_), channel_id=1, source_target_pairs={{4,8},{12,16},{20,24},{8,4},{16,12},{24,20},{5,9},{13,17},{21,25},... | collective-permute-start | bytes 417800 | tf_op jit(solution)/shard_map/ppermute | solution.py:118
  12.5 2.4 %collective-permute-done.2.beyond = f32[256,128]{1,0:T(8,128)S(1)} collective-permute-done((f32[256,128]{1,0:T(8,128)S(1)}, f32[256,128]{1,0:T(8,128)S(1)}, u32[]{:S(2)}, u32[]{:S(2)}) %collective-permute-start.2) | collective-permute-done | bytes 131104 | tf_op jit(solution)/shard_map/ppermute | solution.py:118
  14.9 3.7 %collective-permute-start.5 = (f32[256,128]{1,0:T(8,128)S(1)}, f32[256,128]{1,0:T(8,128)S(1)}, u32[]{:S(2)}, u32[]{:S(2)}) collective-permute-start(f32[256,128]{1,0:T(8,128)S(1)} %collective-permute-done.2.beyond), channel_id=1, source_target_pairs={{12,4},{20,12},{28,20},{0,8},{8,16},{16,24},{13,5},{21,13},{29,21}... | collective-permute-start | bytes 393224 | tf_op jit(solution)/shard_map/ppermute | solution.py:123
  18.6 1.6 %beside_x.1 = (f32[32,16,128]{2,1,0:T(8,128)S(1)}, f32[19,16,16,128]{3,2,1,0:T(8,128)S(1)}) custom-call(f32[272,128]{1,0:T(8,128)S(1)} %pack_odd.1.ahead.rest_0_, f32[9,128,128]{2,1,0:T(8,128)S(1)} %copy-done.1, f32[19,16,16,128]{3,2,1,0:T(8,128)S(1)} %copy-done, f32[4,16,16,128]{3,2,1,0:T(8,128)S(1)} %get-tuple-element.28.flow_ref, ...), custom_call_target="tpu_custom_call" | custom-call | flops 3276800000 | bytes 1000 | tf_op jit(solution)/shard_map/beside_x/pallas_call | solution.py:153
  20.2 0.1 far_x.1.partial
  20.3 0.0 collective-permute-done.3.got.rest_2_
  20.4 0.4 %near_x.1 = (f32[16,16,128]{2,1,0:T(8,128)S(1)}, f32[16,16,128]{2,1,0:T(8,128)S(1)}) custom-call(f32[9,128,128]{2,1,0:T(8,128)S(1)} %copy-done.1, f32[32,16,128]{2,1,0:T(8,128)S(1)} %far_x.1.partial, f32[16,16,128]{2,1,0:T(8,128)S(1)} %get-tuple-element.33.factor, f32[4,16,16,128]{3,2,1,0:T(8,128)S(1)} %get-tuple-element.28.flow_ref, ...), custom_call_target="tpu_custom_call" | custom-call | flops 1000 | bytes 1000 | tf_op jit(solution)/shard_map/near_x/pallas_call | solution.py:153
  20.8 0.0 collective-permute-done.4.rest_1_.rest_3_
  20.8 0.3 %far_ready.1 = (f32[32,16,128]{2,1,0:T(8,128)S(1)}, f32[32,16,128]{2,1,0:T(8,128)S(1)}) custom-call(f32[16,16,128]{2,1,0:T(8,128)S(1)} %get-tuple-element.37.ahead.near, f32[9,128,128]{2,1,0:T(8,128)S(1)} %copy-done.1, f32[32,16,128]{2,1,0:T(8,128)S(1)} %far_x.1.partial, f32[16,16,128]{2,1,0:T(8,128)S(1)} %get-tuple-element.33.factor, ...), custom_call_target="tpu_custom_call" | custom-call | flops 1000 | bytes 1000 | tf_op jit(solution)/shard_map/far_ready/pallas_call | solution.py:153
  21.1 0.0 collective-permute-done.5.rest_0_
  21.1 0.3 %source.1 = (f32[16,16,128]{2,1,0:T(8,128)S(1)}, f32[16,16,128]{2,1,0:T(8,128)S(1)}, f32[16,8,128]{2,1,0:T(8,128)S(1)}, f32[16,128]{1,0:T(8,128)S(1)}, f32[32,128]{1,0:T(8,128)S(1)}) custom-call(f32[32,16,128]{2,1,0:T(8,128)S(1)} %get-tuple-element.38.smooth, f32[32,16,128]{2,1,0:T(8,128)S(1)} %get-tuple-element.39.ext, ...), custom_call_target="tpu_custom_call" | custom-call | flops 1000000 | bytes 1000000 | tf_op jit(solution)/shard_map/source/pallas_call | solution.py:153
  21.4 1.6 %collective-permute-start.6 = (f32[16,8,128]{2,1,0:T(8,128)S(1)}, f32[16,8,128]{2,1,0:T(8,128)S(1)}, u32[]{:S(2)}, u32[]{:S(2)}) collective-permute-start(f32[16,8,128]{2,1,0:T(8,128)S(1)} %get-tuple-element.43), channel_id=1, source_target_pairs={{0,2},{2,0},{1,3},{3,1},{4,6},{6,4},{5,7},{7,5},{8,10},{10,8},{9,1... | collective-permute-start | bytes 196616 | tf_op jit(solution)/shard_map/ppermute | solution.py:118
  23.0 0.6 %collective-permute-start.7 = (f32[16,128]{1,0:T(8,128)S(1)}, f32[16,128]{1,0:T(8,128)S(1)}, u32[]{:S(2)}, u32[]{:S(2)}) collective-permute-start(f32[16,128]{1,0:T(8,128)S(1)} %get-tuple-element.44), channel_id=1, source_target_pairs={{0,1},{1,0},{2,3},{3,2},{4,5},{5,4},{6,7},{7,6},{8,9},{9,8},{10,11... | collective-permute-start | bytes 24584 | tf_op jit(solution)/shard_map/ppermute | solution.py:118
  23.7 0.3 own_z.1.own
  23.9 1.7 %collide.1.ahead = f32[19,16,16,128]{3,2,1,0:T(8,128)} custom-call(f32[19,16,16,128]{3,2,1,0:T(8,128)S(1)} %copy-done, f32[19,16,16,128]{3,2,1,0:T(8,128)S(1)} %get-tuple-element.35.base, f32[4,16,16,128]{3,2,1,0:T(8,128)S(1)} %get-tuple-element.28.flow_ref, f32[16,16,128]{2,1,0:T(8,128)S(1)} %get-tuple-element.41.damp, s32[16,16,128]{2,1,0:T(8,128)S(1)} %copy-done.2, ...), custom_call_target="tpu_custom_call" | custom-call | flops 9830400 | bytes 5767168 | tf_op jit(solution)/shard_map/collide/pallas_call | solution.py:153
  25.6 0.1 collective-permute-done.6.rest_0_
  25.8 0.3 %smooth_yz.1.own = f32[16,16,128]{2,1,0:T(8,128)S(1)} custom-call(f32[19,16,16,128]{3,2,1,0:T(8,128)} %collide.1.ahead, f32[9,128,128]{2,1,0:T(8,128)S(1)} %copy-done.1, f32[256,128]{1,0:T(8,128)S(1)} %own_z.1.own, f32[16,8,128]{2,1,0:T(8,128)S(1)} %collective-permute-done.6.rest_0_), custom_call_target="tpu_custom_call" | custom-call | flops 1000000 | bytes 1000000 | tf_op jit(solution)/shard_map/smooth_yz/pallas_call | solution.py:153
  26.1 0.0 collective-permute-done.7.rest_0_
  26.1 0.1 collective-permute-done.8.rest_1_
  26.2 1.0 %add_halo.1 = f32[16,16,128]{2,1,0:T(8,128)} custom-call(f32[9,128,128]{2,1,0:T(8,128)S(1)} %copy-done.1, f32[16,16,128]{2,1,0:T(8,128)S(1)} %smooth_yz.1.own, f32[16,128]{1,0:T(8,128)S(1)} %collective-permute-done.7.rest_0_, f32[32,128]{1,0:T(8,128)S(1)} %collective-permute-done.8.rest_1_), custom_call_target="tpu_custom_call" | custom-call | flops 1000000 | bytes 1000000 | tf_op jit(solution)/shard_map/add_halo/pallas_call | solution.py:153
  (7 shorter events, 0.0 us)
Async XLA Ops:
  0.6 4.3 %copy-start = (f32[19,16,16,128]{3,2,1,0:T(8,128)S(1)}, f32[19,16,16,128]{3,2,1,0:T(8,128)}, u32[]{:S(2)}) copy-start(f32[19,16,16,128]{3,2,1,0:T(8,128)} %adj.11) | copy-start | bytes 7471108
  1.9 6.3 %copy-start.1 = (f32[9,128,128]{2,1,0:T(8,128)S(1)}, f32[9,128,128]{2,1,0:T(8,128)}, u32[]{:S(2)}) copy-start(f32[9,128,128]{2,1,0:T(8,128)} %constant.2.clone.weights) | copy-start | bytes 1769476
  1.9 6.0 %collective-permute-start = (f32[208,128]{1,0:T(8,128)S(1)}, f32[208,128]{1,0:T(8,128)S(1)}, u32[]{:S(2)}, u32[]{:S(2)}) collective-permute-start(f32[208,128]{1,0:T(8,128)S(1)} %get-tuple-element.25.ahead), channel_id=1, source_target_pairs={{0,2},{2,0},{1,3},{3,1},{4,6},{6,4},{5,7},{7,5},{8,10},{10,8},{9,1... | collective-permute-start | bytes 319496 | tf_op jit(solution)/shard_map/ppermute | solution.py:118
  8.2 2.1 %collective-permute-start.1 = (f32[16,16,128]{2,1,0:T(8,128)S(1)}, f32[16,16,128]{2,1,0:T(8,128)S(1)}, u32[]{:S(2)}, u32[]{:S(2)}) collective-permute-start(f32[16,16,128]{2,1,0:T(8,128)S(1)} %get-tuple-element.31), channel_id=1, source_target_pairs={{0,1},{1,0},{2,3},{3,2},{4,5},{5,4},{6,7},{7,6},{8,9},{9,8},{10,11... | collective-permute-start | bytes 393224 | tf_op jit(solution)/shard_map/ppermute | solution.py:118
  8.5 6.4 %collective-permute-start.2 = (f32[256,128]{1,0:T(8,128)S(1)}, f32[256,128]{1,0:T(8,128)S(1)}, u32[]{:S(2)}, u32[]{:S(2)}) collective-permute-start(f32[256,128]{1,0:T(8,128)S(1)} %get-tuple-element.34.smooth), channel_id=1, source_target_pairs={{0,4},{8,12},{16,20},{24,28},{4,0},{12,8},{20,16},{28,24},{1,5},{9... | collective-permute-start | bytes 393224 | tf_op jit(solution)/shard_map/ppermute | solution.py:118
  10.7 7.9 %copy-start.2 = (s32[16,16,128]{2,1,0:T(8,128)S(1)}, s32[16,16,128]{2,1,0:T(8,128)}, u32[]{:S(2)}) copy-start(s32[16,16,128]{2,1,0:T(8,128)} %mask.3) | copy-start | bytes 393220
  10.7 9.7 %collective-permute-start.3 = (f32[272,128]{1,0:T(8,128)S(1)}, f32[272,128]{1,0:T(8,128)S(1)}, u32[]{:S(2)}, u32[]{:S(2)}) collective-permute-start(f32[272,128]{1,0:T(8,128)S(1)} %get-tuple-element.32.ahead.own), channel_id=1, source_target_pairs={{0,4},{8,12},{16,20},{24,28},{4,0},{12,8},{20,16},{28,24},{1,5},{9... | collective-permute-start | bytes 417800 | tf_op jit(solution)/shard_map/ppermute | solution.py:118
  11.8 9.0 %collective-permute-start.4 = (f32[272,128]{1,0:T(8,128)S(1)}, f32[272,128]{1,0:T(8,128)S(1)}, u32[]{:S(2)}, u32[]{:S(2)}) collective-permute-start(f32[272,128]{1,0:T(8,128)S(1)} %pack_odd.1.ahead.rest_0_), channel_id=1, source_target_pairs={{4,8},{12,16},{20,24},{8,4},{16,12},{24,20},{5,9},{13,17},{21,25},... | collective-permute-start | bytes 417800 | tf_op jit(solution)/shard_map/ppermute | solution.py:118
  14.9 6.2 %collective-permute-start.5 = (f32[256,128]{1,0:T(8,128)S(1)}, f32[256,128]{1,0:T(8,128)S(1)}, u32[]{:S(2)}, u32[]{:S(2)}) collective-permute-start(f32[256,128]{1,0:T(8,128)S(1)} %collective-permute-done.2.beyond), channel_id=1, source_target_pairs={{12,4},{20,12},{28,20},{0,8},{8,16},{16,24},{13,5},{21,13},{29,21}... | collective-permute-start | bytes 393224 | tf_op jit(solution)/shard_map/ppermute | solution.py:123
  21.4 4.3 %collective-permute-start.6 = (f32[16,8,128]{2,1,0:T(8,128)S(1)}, f32[16,8,128]{2,1,0:T(8,128)S(1)}, u32[]{:S(2)}, u32[]{:S(2)}) collective-permute-start(f32[16,8,128]{2,1,0:T(8,128)S(1)} %get-tuple-element.43), channel_id=1, source_target_pairs={{0,2},{2,0},{1,3},{3,1},{4,6},{6,4},{5,7},{7,5},{8,10},{10,8},{9,1... | collective-permute-start | bytes 196616 | tf_op jit(solution)/shard_map/ppermute | solution.py:118
  23.0 3.2 %collective-permute-start.8 = (f32[32,128]{1,0:T(8,128)S(1)}, f32[32,128]{1,0:T(8,128)S(1)}, u32[]{:S(2)}, u32[]{:S(2)}) collective-permute-start(f32[32,128]{1,0:T(8,128)S(1)} %get-tuple-element.45), channel_id=1, source_target_pairs={{0,3},{3,0},{1,2},{2,1},{4,7},{7,4},{5,6},{6,5},{8,11},{11,8},{9,1... | collective-permute-start | bytes 49160 | tf_op jit(solution)/shard_map/ppermute | solution.py:133
  23.0 3.1 %collective-permute-start.7 = (f32[16,128]{1,0:T(8,128)S(1)}, f32[16,128]{1,0:T(8,128)S(1)}, u32[]{:S(2)}, u32[]{:S(2)}) collective-permute-start(f32[16,128]{1,0:T(8,128)S(1)} %get-tuple-element.44), channel_id=1, source_target_pairs={{0,1},{1,0},{2,3},{3,2},{4,5},{5,4},{6,7},{7,6},{8,9},{9,8},{10,11... | collective-permute-start | bytes 24584 | tf_op jit(solution)/shard_map/ppermute | solution.py:118

commit v8 on v7

--- a/solution.py
+++ b/solution.py
@@ -683,7 +683,7 @@
     pl.when(px != 1)(lambda: act(False))
 
 
-def source(dims, many_x, many_y, many_z, smooth, ext, near, near_damp, *rest):
+def source(dims, many_x, many_y, many_z, ahead, smooth, ext, near, near_damp, *rest):
     X, Y, Z = dims
     rest = iter(rest)
     relayed = next(rest) if many_x else None
@@ -855,30 +855,19 @@
         relax(pulled, vel, square(vel), mask[x], None, store)
         return 0
 
-    lax.fori_loop(1, X - 1, layer, 0, unroll=7)
-
-
-def collide(dims, many_x, many_y, many_z, step, adj, base, flow_ref, damp, mask, *rest):
+    lax.fori_loop(1, X - 1, layer, 0, unroll=True)
+
+
+def edges_x(dims, many_x, many_y, many_z, ahead, adj, flow_ref, mask, *rest):
     X, Y, Z = dims
     rest = iter(rest)
     y_even, y_odd = refs_of(rest, many_y)
     z_even, z_odd = refs_of(rest, many_z)
     x_even, x_odd = refs_of(rest, many_x)
-    target, out, sems = rest
+    (out,) = rest
     px, py, pz = parity_of("gx"), parity_of("gy"), parity_of("gz")
     pull = Pull(adj, dims, py, y_even, y_odd, pz, z_even, z_odd)
     u_at = R * Y
-
-    def layer(x):
-        vel = [flow_ref[a, x] for a in range(3)]
-        drag = jnp.where(mask[x] == 0, damp[x] * flow_ref[3, x], 0.0)
-        level = drag * square(vel)
-        tilt = [drag * v for v in vel]
-        out[0, x] = base[0, x] - level
-        for q in range(1, Q, 2):
-            lean = lean_of(q, tilt)
-            out[q, x] = base[q, x] + (lean - level)
-            out[q + 1, x] = base[q + 1, x] - (lean + level)
 
     def edge(x, toward):
         around = {c: pull.faces(x + c) for c in (0, -toward)}
@@ -894,20 +883,34 @@
         vel = [flow_ref[a, x] for a in range(3)]
 
         def store(q, value):
-            out[q, x] = value
-
-        relax(pulled, vel, square(vel), mask[x], damp[x] * flow_ref[3, x], store)
+            out[int(x > 0), q] = value
+
+        relax(pulled, vel, square(vel), mask[x], None, store)
+
+    edge(0, -1)
+    edge(X - 1, 1)
+
+
+def collide(dims, step, edges, base, flow_ref, damp, mask, target, out, sems):
+    X, Y, Z = dims
+
+    def layer(x):
+        vel = [flow_ref[a, x] for a in range(3)]
+        drag = jnp.where(mask[x] == 0, damp[x] * flow_ref[3, x], 0.0)
+        level = drag * square(vel)
+        tilt = [drag * v for v in vel]
+        here = {0: edges.at[0], X - 1: edges.at[1]}.get(x, base.at[:, x])
+        out[0, x] = here[0] - level
+        for q in range(1, Q, 2):
+            lean = lean_of(q, tilt)
+            out[q, x] = here[q] + (lean - level)
+            out[q + 1, x] = here[q + 1] - (lean + level)
 
     last = X // step - 1
     copies = []
     for part in [1, 0, 2, last, *range(3, last)]:
         for x in range(part * step, (part + 1) * step):
-            if x == 0:
-                edge(x, -1)
-            elif x == X - 1:
-                edge(x, 1)
-            else:
-                layer(x)
+            layer(x)
         here = pl.ds(part * step, step)
         copies.append(pltpu.make_async_copy(out.at[:, here], target.at[:, here], sems.at[part]))
         copies[-1].start()
@@ -1035,6 +1038,15 @@
         moved=1000,
         name="far_ready",
     )
+    (edges,) = call(
+        functools.partial(edges_x, dims, many_x, many_y, many_z),
+        [f32(2, Q, Y, Z)],
+        (smooth, adjoint, flow_values, mask, *got_y, *got_z, *got_x),
+        limit=8,
+        flops=1000,
+        moved=1000,
+        name="edges_x",
+    )
     n_corners = (1 + many_y) * (1 + many_z)
     result, damp, *packs = call(
         functools.partial(source, dims, many_x, many_y, many_z),
@@ -1042,7 +1054,7 @@
         + [f32(X, R, Z)] * (1 + many_y)
         + [f32(Y, Z)] * (1 + many_z)
         + [f32(4 * R, Z)] * n_corners,
-        (smooth, ext, near, near_damp, *relayed),
+        (edges, smooth, ext, near, near_damp, *relayed),
         None,
         [extended],
         limit=8,
@@ -1053,9 +1065,9 @@
 
     step = 2
     (adjoint_next,) = call(
-        functools.partial(collide, dims, many_x, many_y, many_z, step),
+        functools.partial(collide, dims, step),
         [f32(Q, X, Y, Z)],
-        (adjoint, base, flow_values, damp, mask, *got_y, *got_z, *got_x),
+        (edges, base, flow_values, damp, mask),
         None,
         [pltpu.VMEM((Q, X, Y, Z), jnp.float32), dma((X // step,))],
         out_specs=(hbm,),

time: 27.3 us -> 27.3 us (level)
    pallas_call x15 -> x16, Pallas kernels: 10.2 us -> 10.1 us  [call(): pl.pallas_call(body, out_shape=outs, in_specs=specs or vmem(len(args)), o...]
where the time goes in v8:
time: 27.3 us; the launch traced here: 27.2 us
  starting transfers between devices  12.5 us (46%)
  Pallas kernels  10.1 us (37%)
  waiting for transfers between devices  3.78 us (14%)
  between operations  0.82 us (3%)
    pallas_call x16, Pallas kernels, call(): pl.pallas_call(body, out_shape=outs, in_specs=specs or vmem(len(args)), o...  10.1 us
    ppermute x7, starting transfers between devices, swap(): return lax.ppermute(array, axis, pairs + [(b, a) for a, b in pairs])  8.79 us
    ppermute x1, starting transfers between devices, relay(): return lax.ppermute(array, axis, pairs)  3.69 us
    ppermute x7, waiting for transfers between devices, swap(): return lax.ppermute(array, axis, pairs + [(b, a) for a, b in pairs])  3.68 us
  transfers between devices with their start and end apart: 9, of which 4 were waited for; matrix products, arithmetic and copies ran while one was open for 0% of the time, Pallas kernels for 27%

profile of v8, /device:TPU:0, one launch (start us, length us, event | category | flops | bytes accessed | tf_op | source)
XLA Modules:
  0.0 27.2 jit_solution(2910933024449104622)
XLA Ops:
  0.6 1.3 %pack_y.1 = (f32[208,128]{1,0:T(8,128)S(1)}, f32[16,16,128]{2,1,0:T(8,128)S(1)}) custom-call(f32[19,16,16,128]{3,2,1,0:T(8,128)} %adj.11, f32[16,16,128]{2,1,0:T(8,128)} %design.1), custom_call_target="tpu_custom_call" | custom-call | flops 1000000 | bytes 1000000 | tf_op jit(solution)/shard_map/pack_y/pallas_call | solution.py:153
  1.9 0.0 copy-start.1
  1.9 3.0 %collective-permute-start = (f32[208,128]{1,0:T(8,128)S(1)}, f32[208,128]{1,0:T(8,128)S(1)}, u32[]{:S(2)}, u32[]{:S(2)}) collective-permute-start(f32[208,128]{1,0:T(8,128)S(1)} %get-tuple-element.25.ahead), channel_id=1, source_target_pairs={{0,2},{2,0},{1,3},{3,1},{4,6},{6,4},{5,7},{7,5},{8,10},{10,8},{9,1... | collective-permute-start | bytes 319496 | tf_op jit(solution)/shard_map/ppermute | solution.py:118
  5.0 2.0 %prepare.1 = (f32[4,16,16,128]{3,2,1,0:T(8,128)S(1)}, f32[16,16,128]{2,1,0:T(8,128)S(1)}, f32[16,16,128]{2,1,0:T(8,128)S(1)}) custom-call(f32[208,128]{1,0:T(8,128)S(1)} %get-tuple-element.25.ahead, f32[19,16,16,128]{3,2,1,0:T(8,128)} %forward.1, f32[19,16,16,128]{3,2,1,0:T(8,128)S(1)} %copy-done), custom_call_target="tpu_custom_call" | custom-call | flops 6553600 | bytes 5767168 | tf_op jit(solution)/shard_map/prepare/pallas_call | solution.py:153
  7.0 1.0 %collective-permute-done.rest_1_.rest_0_ = f32[208,128]{1,0:T(8,128)S(1)} collective-permute-done((f32[208,128]{1,0:T(8,128)S(1)}, f32[208,128]{1,0:T(8,128)S(1)}, u32[]{:S(2)}, u32[]{:S(2)}) %collective-permute-start) | collective-permute-done | bytes 106528 | tf_op jit(solution)/shard_map/ppermute | solution.py:118
  7.9 0.2 design_y.1
  8.2 0.1 collective-permute-start.1
  8.2 0.3 factor_y.1
  8.5 1.8 %collective-permute-start.2 = (f32[256,128]{1,0:T(8,128)S(1)}, f32[256,128]{1,0:T(8,128)S(1)}, u32[]{:S(2)}, u32[]{:S(2)}) collective-permute-start(f32[256,128]{1,0:T(8,128)S(1)} %get-tuple-element.34.smooth), channel_id=1, source_target_pairs={{0,4},{8,12},{16,20},{24,28},{4,0},{12,8},{20,16},{28,24},{1,5},{9... | collective-permute-start | bytes 393224 | tf_op jit(solution)/shard_map/ppermute | solution.py:118
  10.3 0.4 %pack_x.1 = (f32[272,128]{1,0:T(8,128)S(1)}, f32[16,16,128]{2,1,0:T(8,128)S(1)}) custom-call(f32[19,16,16,128]{3,2,1,0:T(8,128)S(1)} %copy-done, f32[16,16,128]{2,1,0:T(8,128)S(1)} %get-tuple-element.30.factor_in, f32[4,16,16,128]{3,2,1,0:T(8,128)S(1)} %get-tuple-element.28.flow_ref, f32[208,128]{1,0:T(8,128)S(1)} %collective-permute-done.rest_1_.rest_0_, ...), custom_call_target="tpu_custom_call" | custom-call | flops 1000000 | bytes 1000000 | tf_op jit(solution)/shard_map/pack_x/pallas_call | solution.py:153
  10.7 1.0 %collective-permute-start.3 = (f32[272,128]{1,0:T(8,128)S(1)}, f32[272,128]{1,0:T(8,128)S(1)}, u32[]{:S(2)}, u32[]{:S(2)}) collective-permute-start(f32[272,128]{1,0:T(8,128)S(1)} %get-tuple-element.32.ahead.own), channel_id=1, source_target_pairs={{0,4},{8,12},{16,20},{24,28},{4,0},{12,8},{20,16},{28,24},{1,5},{9... | collective-permute-start | bytes 417800 | tf_op jit(solution)/shard_map/ppermute | solution.py:118
  11.7 0.1 pack_odd.1.ahead.rest_0_
  11.8 0.7 %collective-permute-start.4 = (f32[272,128]{1,0:T(8,128)S(1)}, f32[272,128]{1,0:T(8,128)S(1)}, u32[]{:S(2)}, u32[]{:S(2)}) collective-permute-start(f32[272,128]{1,0:T(8,128)S(1)} %pack_odd.1.ahead.rest_0_), channel_id=1, source_target_pairs={{4,8},{12,16},{20,24},{8,4},{16,12},{24,20},{5,9},{13,17},{21,25},... | collective-permute-start | bytes 417800 | tf_op jit(solution)/shard_map/ppermute | solution.py:118
  12.5 2.4 %collective-permute-done.2.beyond = f32[256,128]{1,0:T(8,128)S(1)} collective-permute-done((f32[256,128]{1,0:T(8,128)S(1)}, f32[256,128]{1,0:T(8,128)S(1)}, u32[]{:S(2)}, u32[]{:S(2)}) %collective-permute-start.2) | collective-permute-done | bytes 131104 | tf_op jit(solution)/shard_map/ppermute | solution.py:118
  14.9 3.7 %collective-permute-start.5 = (f32[256,128]{1,0:T(8,128)S(1)}, f32[256,128]{1,0:T(8,128)S(1)}, u32[]{:S(2)}, u32[]{:S(2)}) collective-permute-start(f32[256,128]{1,0:T(8,128)S(1)} %collective-permute-done.2.beyond), channel_id=1, source_target_pairs={{12,4},{20,12},{28,20},{0,8},{8,16},{16,24},{13,5},{21,13},{29,21}... | collective-permute-start | bytes 393224 | tf_op jit(solution)/shard_map/ppermute | solution.py:123
  18.6 1.4 %beside_x.1 = (f32[32,16,128]{2,1,0:T(8,128)S(1)}, f32[19,16,16,128]{3,2,1,0:T(8,128)S(1)}) custom-call(f32[272,128]{1,0:T(8,128)S(1)} %pack_odd.1.ahead.rest_0_, f32[9,128,128]{2,1,0:T(8,128)S(1)} %copy-done.1, f32[19,16,16,128]{3,2,1,0:T(8,128)S(1)} %copy-done, f32[4,16,16,128]{3,2,1,0:T(8,128)S(1)} %get-tuple-element.28.flow_ref, ...), custom_call_target="tpu_custom_call" | custom-call | flops 3276800000 | bytes 1000 | tf_op jit(solution)/shard_map/beside_x/pallas_call | solution.py:153
  20.0 0.1 far_x.1.partial
  20.2 0.0 collective-permute-done.3.got.rest_2_
  20.2 0.4 %near_x.1 = (f32[16,16,128]{2,1,0:T(8,128)S(1)}, f32[16,16,128]{2,1,0:T(8,128)S(1)}) custom-call(f32[9,128,128]{2,1,0:T(8,128)S(1)} %copy-done.1, f32[32,16,128]{2,1,0:T(8,128)S(1)} %far_x.1.partial, f32[16,16,128]{2,1,0:T(8,128)S(1)} %get-tuple-element.33.factor, f32[4,16,16,128]{3,2,1,0:T(8,128)S(1)} %get-tuple-element.28.flow_ref, ...), custom_call_target="tpu_custom_call" | custom-call | flops 1000 | bytes 1000 | tf_op jit(solution)/shard_map/near_x/pallas_call | solution.py:153
  20.6 0.0 collective-permute-done.4.rest_1_.rest_3_
  20.6 0.3 %far_ready.1 = (f32[32,16,128]{2,1,0:T(8,128)S(1)}, f32[32,16,128]{2,1,0:T(8,128)S(1)}) custom-call(f32[16,16,128]{2,1,0:T(8,128)S(1)} %get-tuple-element.36.ahead.near, f32[9,128,128]{2,1,0:T(8,128)S(1)} %copy-done.1, f32[32,16,128]{2,1,0:T(8,128)S(1)} %far_x.1.partial, f32[16,16,128]{2,1,0:T(8,128)S(1)} %get-tuple-element.33.factor, ...), custom_call_target="tpu_custom_call" | custom-call | flops 1000 | bytes 1000 | tf_op jit(solution)/shard_map/far_ready/pallas_call | solution.py:153
  20.9 0.2 edges_x.1.ahead.edges
  21.1 0.0 collective-permute-done.5.rest_0_
  21.1 0.3 %source.1 = (f32[16,16,128]{2,1,0:T(8,128)S(1)}, f32[16,16,128]{2,1,0:T(8,128)S(1)}, f32[16,8,128]{2,1,0:T(8,128)S(1)}, f32[16,128]{1,0:T(8,128)S(1)}, f32[32,128]{1,0:T(8,128)S(1)}) custom-call(f32[2,19,16,128]{3,2,1,0:T(8,128)S(1)} %edges_x.1.ahead.edges, f32[32,16,128]{2,1,0:T(8,128)S(1)} %get-tuple-element.37.ahead.smooth, ...), custom_call_target="tpu_custom_call" | custom-call | flops 1000000 | bytes 1000000 | tf_op jit(solution)/shard_map/source/pallas_call | solution.py:153
  21.5 1.6 %collective-permute-start.6 = (f32[16,8,128]{2,1,0:T(8,128)S(1)}, f32[16,8,128]{2,1,0:T(8,128)S(1)}, u32[]{:S(2)}, u32[]{:S(2)}) collective-permute-start(f32[16,8,128]{2,1,0:T(8,128)S(1)} %get-tuple-element.43), channel_id=1, source_target_pairs={{0,2},{2,0},{1,3},{3,1},{4,6},{6,4},{5,7},{7,5},{8,10},{10,8},{9,1... | collective-permute-start | bytes 196616 | tf_op jit(solution)/shard_map/ppermute | solution.py:118
  23.1 0.6 %collective-permute-start.7 = (f32[16,128]{1,0:T(8,128)S(1)}, f32[16,128]{1,0:T(8,128)S(1)}, u32[]{:S(2)}, u32[]{:S(2)}) collective-permute-start(f32[16,128]{1,0:T(8,128)S(1)} %get-tuple-element.44), channel_id=1, source_target_pairs={{0,1},{1,0},{2,3},{3,2},{4,5},{5,4},{6,7},{7,6},{8,9},{9,8},{10,11... | collective-permute-start | bytes 24584 | tf_op jit(solution)/shard_map/ppermute | solution.py:118
  23.7 0.3 own_z.1.own
  23.9 1.5 %collide.1.ahead = f32[19,16,16,128]{3,2,1,0:T(8,128)} custom-call(f32[2,19,16,128]{3,2,1,0:T(8,128)S(1)} %edges_x.1.ahead.edges, f32[19,16,16,128]{3,2,1,0:T(8,128)S(1)} %get-tuple-element.38.base, f32[4,16,16,128]{3,2,1,0:T(8,128)S(1)} %get-tuple-element.28.flow_ref, f32[16,16,128]{2,1,0:T(8,128)S(1)} %get-tuple-element.41.damp, s32[16,16,128]{2,1,0:T(8,128)S(1)} %copy-done.2), custom_call_target="tpu_custom_call" | custom-call | flops 9830400 | bytes 5767168 | tf_op jit(solution)/shard_map/collide/pallas_call | solution.py:153
  25.5 0.3 %collective-permute-done.6.rest_0_ = f32[16,8,128]{2,1,0:T(8,128)S(1)} collective-permute-done((f32[16,8,128]{2,1,0:T(8,128)S(1)}, f32[16,8,128]{2,1,0:T(8,128)S(1)}, u32[]{:S(2)}, u32[]{:S(2)}) %collective-permute-start.6) | collective-permute-done | bytes 65568 | tf_op jit(solution)/shard_map/ppermute | solution.py:118
  25.8 0.3 %smooth_yz.1.own = f32[16,16,128]{2,1,0:T(8,128)S(1)} custom-call(f32[19,16,16,128]{3,2,1,0:T(8,128)} %collide.1.ahead, f32[9,128,128]{2,1,0:T(8,128)S(1)} %copy-done.1, f32[256,128]{1,0:T(8,128)S(1)} %own_z.1.own, f32[16,8,128]{2,1,0:T(8,128)S(1)} %collective-permute-done.6.rest_0_), custom_call_target="tpu_custom_call" | custom-call | flops 1000000 | bytes 1000000 | tf_op jit(solution)/shard_map/smooth_yz/pallas_call | solution.py:153
  26.1 0.1 collective-permute-done.8.rest_1_
  26.2 1.0 %add_halo.1 = f32[16,16,128]{2,1,0:T(8,128)} custom-call(f32[9,128,128]{2,1,0:T(8,128)S(1)} %copy-done.1, f32[16,16,128]{2,1,0:T(8,128)S(1)} %smooth_yz.1.own, f32[16,128]{1,0:T(8,128)S(1)} %collective-permute-done.7.rest_0_, f32[32,128]{1,0:T(8,128)S(1)} %collective-permute-done.8.rest_1_), custom_call_target="tpu_custom_call" | custom-call | flops 1000000 | bytes 1000000 | tf_op jit(solution)/shard_map/add_halo/pallas_call | solution.py:153
  (8 shorter events, 0.0 us)
Async XLA Ops:
  0.6 4.3 %copy-start = (f32[19,16,16,128]{3,2,1,0:T(8,128)S(1)}, f32[19,16,16,128]{3,2,1,0:T(8,128)}, u32[]{:S(2)}) copy-start(f32[19,16,16,128]{3,2,1,0:T(8,128)} %adj.11) | copy-start | bytes 7471108
  1.9 6.3 %copy-start.1 = (f32[9,128,128]{2,1,0:T(8,128)S(1)}, f32[9,128,128]{2,1,0:T(8,128)}, u32[]{:S(2)}) copy-start(f32[9,128,128]{2,1,0:T(8,128)} %constant.2.clone.weights) | copy-start | bytes 1769476
  1.9 6.0 %collective-permute-start = (f32[208,128]{1,0:T(8,128)S(1)}, f32[208,128]{1,0:T(8,128)S(1)}, u32[]{:S(2)}, u32[]{:S(2)}) collective-permute-start(f32[208,128]{1,0:T(8,128)S(1)} %get-tuple-element.25.ahead), channel_id=1, source_target_pairs={{0,2},{2,0},{1,3},{3,1},{4,6},{6,4},{5,7},{7,5},{8,10},{10,8},{9,1... | collective-permute-start | bytes 319496 | tf_op jit(solution)/shard_map/ppermute | solution.py:118
  8.2 2.1 %collective-permute-start.1 = (f32[16,16,128]{2,1,0:T(8,128)S(1)}, f32[16,16,128]{2,1,0:T(8,128)S(1)}, u32[]{:S(2)}, u32[]{:S(2)}) collective-permute-start(f32[16,16,128]{2,1,0:T(8,128)S(1)} %get-tuple-element.31), channel_id=1, source_target_pairs={{0,1},{1,0},{2,3},{3,2},{4,5},{5,4},{6,7},{7,6},{8,9},{9,8},{10,11... | collective-permute-start | bytes 393224 | tf_op jit(solution)/shard_map/ppermute | solution.py:118
  8.5 6.4 %collective-permute-start.2 = (f32[256,128]{1,0:T(8,128)S(1)}, f32[256,128]{1,0:T(8,128)S(1)}, u32[]{:S(2)}, u32[]{:S(2)}) collective-permute-start(f32[256,128]{1,0:T(8,128)S(1)} %get-tuple-element.34.smooth), channel_id=1, source_target_pairs={{0,4},{8,12},{16,20},{24,28},{4,0},{12,8},{20,16},{28,24},{1,5},{9... | collective-permute-start | bytes 393224 | tf_op jit(solution)/shard_map/ppermute | solution.py:118
  10.7 7.9 %copy-start.2 = (s32[16,16,128]{2,1,0:T(8,128)S(1)}, s32[16,16,128]{2,1,0:T(8,128)}, u32[]{:S(2)}) copy-start(s32[16,16,128]{2,1,0:T(8,128)} %mask.5) | copy-start | bytes 393220
  10.7 9.5 %collective-permute-start.3 = (f32[272,128]{1,0:T(8,128)S(1)}, f32[272,128]{1,0:T(8,128)S(1)}, u32[]{:S(2)}, u32[]{:S(2)}) collective-permute-start(f32[272,128]{1,0:T(8,128)S(1)} %get-tuple-element.32.ahead.own), channel_id=1, source_target_pairs={{0,4},{8,12},{16,20},{24,28},{4,0},{12,8},{20,16},{28,24},{1,5},{9... | collective-permute-start | bytes 417800 | tf_op jit(solution)/shard_map/ppermute | solution.py:118
  11.8 8.8 %collective-permute-start.4 = (f32[272,128]{1,0:T(8,128)S(1)}, f32[272,128]{1,0:T(8,128)S(1)}, u32[]{:S(2)}, u32[]{:S(2)}) collective-permute-start(f32[272,128]{1,0:T(8,128)S(1)} %pack_odd.1.ahead.rest_0_), channel_id=1, source_target_pairs={{4,8},{12,16},{20,24},{8,4},{16,12},{24,20},{5,9},{13,17},{21,25},... | collective-permute-start | bytes 417800 | tf_op jit(solution)/shard_map/ppermute | solution.py:118
  14.9 6.2 %collective-permute-start.5 = (f32[256,128]{1,0:T(8,128)S(1)}, f32[256,128]{1,0:T(8,128)S(1)}, u32[]{:S(2)}, u32[]{:S(2)}) collective-permute-start(f32[256,128]{1,0:T(8,128)S(1)} %collective-permute-done.2.beyond), channel_id=1, source_target_pairs={{12,4},{20,12},{28,20},{0,8},{8,16},{16,24},{13,5},{21,13},{29,21}... | collective-permute-start | bytes 393224 | tf_op jit(solution)/shard_map/ppermute | solution.py:123
  21.5 4.3 %collective-permute-start.6 = (f32[16,8,128]{2,1,0:T(8,128)S(1)}, f32[16,8,128]{2,1,0:T(8,128)S(1)}, u32[]{:S(2)}, u32[]{:S(2)}) collective-permute-start(f32[16,8,128]{2,1,0:T(8,128)S(1)} %get-tuple-element.43), channel_id=1, source_target_pairs={{0,2},{2,0},{1,3},{3,1},{4,6},{6,4},{5,7},{7,5},{8,10},{10,8},{9,1... | collective-permute-start | bytes 196616 | tf_op jit(solution)/shard_map/ppermute | solution.py:118
  23.0 3.2 %collective-permute-start.8 = (f32[32,128]{1,0:T(8,128)S(1)}, f32[32,128]{1,0:T(8,128)S(1)}, u32[]{:S(2)}, u32[]{:S(2)}) collective-permute-start(f32[32,128]{1,0:T(8,128)S(1)} %get-tuple-element.45), channel_id=1, source_target_pairs={{0,3},{3,0},{1,2},{2,1},{4,7},{7,4},{5,6},{6,5},{8,11},{11,8},{9,1... | collective-permute-start | bytes 49160 | tf_op jit(solution)/shard_map/ppermute | solution.py:133
  23.1 3.1 %collective-permute-start.7 = (f32[16,128]{1,0:T(8,128)S(1)}, f32[16,128]{1,0:T(8,128)S(1)}, u32[]{:S(2)}, u32[]{:S(2)}) collective-permute-start(f32[16,128]{1,0:T(8,128)S(1)} %get-tuple-element.44), channel_id=1, source_target_pairs={{0,1},{1,0},{2,3},{3,2},{4,5},{5,4},{6,7},{7,6},{8,9},{9,8},{10,11... | collective-permute-start | bytes 24584 | tf_op jit(solution)/shard_map/ppermute | solution.py:118
